TPU v7x, 32 devices: a whole 2x2x4 slice. The times are simulated.
32 devices in a mesh: row: 4 (over y, core), col: 8 (over z, x).
Axes of the slice: x: 2, y: 2, z: 4, core: 2. Of those that a mesh axis runs over, the one named last changes fastest.
Arguments:
- raw_blocks: bfloat16 [2, 4096, 4096], P(None, 'row', 'col'), may hold values from -1.25 to 1.25
- occupancy: int32 [8, 4096], P('row', 'col'), may hold values 0 or 1
- exponent: int32 [8, 8], P('row', 'col'), may hold values from -2 to 2
Outputs:
- multiples: bfloat16 [2, 2, 4096, 512], P(None, None, ('row', 'col'))
All inputs are finite; a program needn't handle non-finite values. No bound on the sum of `occupancy` on one device may be relied on, other than what follows from the above.
Results may differ from a plain program's by a relative error of at most 0.02.
Values may be sent and summed in bfloat16 or wider, within the bound.
No kernel may reach another device: no remote copies, remote signals or barrier semaphores. Data moves between devices by JAX's collectives and lax.ppermute only.
A program may use at most 64 MiB of HBM per device.

v0:
```python
import jax
import jax.numpy as jnp
from jax import lax
from jax.sharding import PartitionSpec as P


def from_root(value, axis, source):
    kept = jnp.where(lax.axis_index(axis) == source, value, 0).astype(value.dtype)
    return lax.psum(kept, axis)


def decode_block(raw_blocks, occupancy, exponent):
    tile_rows = occupancy.shape[0]
    tile_len = raw_blocks.shape[1] // tile_rows
    panel_width = raw_blocks.shape[2]
    tile_scale = jnp.exp2(exponent.astype(jnp.float32))
    col_scale = jnp.repeat(tile_scale, panel_width // tile_scale.shape[1], axis=1)
    factor = occupancy.astype(jnp.float32) * col_scale
    shaped = (
        raw_blocks.astype(jnp.float32).reshape(2, tile_rows, tile_len, panel_width)
        * factor[None, :, None, :]
    )
    return shaped.reshape(raw_blocks.shape).astype(jnp.bfloat16)


def fetch_piece(decoded, which_panel):
    col_count = lax.axis_size("col")
    col_ratio = col_count // lax.axis_size("row")
    root_col = which_panel * (col_count // 2)
    my_col = lax.axis_index("col")
    panel_width = decoded.shape[2]
    root_block = from_root(decoded, "col", root_col)
    slab_piece = lax.dynamic_slice_in_dim(
        root_block, my_col % col_ratio * panel_width, panel_width, 1
    )
    return from_root(slab_piece, "row", my_col // col_ratio)


def complex_term(decoded, slab_piece):
    real_part = jnp.dot(decoded[0], slab_piece[0], preferred_element_type=jnp.float32) - jnp.dot(
        decoded[1], slab_piece[1], preferred_element_type=jnp.float32
    )
    imag_part = jnp.dot(decoded[0], slab_piece[1], preferred_element_type=jnp.float32) + jnp.dot(
        decoded[1], slab_piece[0], preferred_element_type=jnp.float32
    )
    return jnp.concatenate([real_part, imag_part], axis=1)


def on_device(raw_blocks, occupancy, exponent):
    decoded = decode_block(raw_blocks, occupancy, exponent)
    row_total = decoded.shape[1]
    kept_rows = row_total // lax.axis_size("col")
    panel_width = decoded.shape[2]
    results = []
    for which_panel in range(2):
        slab_piece = fetch_piece(decoded, which_panel)

        def one_term(offset, amount, slab_piece=slab_piece):
            return complex_term(decoded, slab_piece)

        results.append(
            lax.psum_scatter(
                one_term(jnp.int32(0), kept_rows * lax.axis_size("col")).astype(jnp.bfloat16),
                "col",
                scatter_dimension=0,
                tiled=True,
            ).astype(jnp.float32)
        )
    stacked = [
        jnp.transpose(result.reshape(result.shape[0], 2, panel_width), (1, 0, 2))
        for result in results
    ]
    return jnp.stack(stacked).astype(jnp.bfloat16)


def solution(mesh):
    placed = (P(None, "row", "col"), P("row", "col"), P("row", "col"))
    return jax.shard_map(
        on_device,
        mesh=mesh,
        in_specs=placed,
        out_specs=P(None, None, ("row", "col"), None),
        check_vma=False,
    )
```

profile of v0, /device:TPU:7, one launch (start us, length us, event | category | flops | bytes accessed | tf_op | source)
XLA Modules:
  0.0 379.1 jit_solution(8793437081229703739)
XLA Ops:
  6.5 0.8 exponential_bitcast_fusion
  7.3 0.8 convert_multiply_fusion
  8.4 2.1 broadcast_select_fusion.1
  10.5 1.5 broadcast_select_fusion
  12.1 157.9 %all-reduce.5.cloned.1.call-done = (bf16[2,1024,512]{2,1,0:T(8,128)(2,1)}, bf16[2,1024,512]{2,1,0:T(8,128)(2,1)}) async-done(((bf16[2,1024,512]{2,1,0:T(8,128)(2,1)}, bf16[2,1024,512]{2,1,0:T(8,128)(2,1)}), (bf16[2,1024,512]{2,1,0:T(8,128)(2,1)}, bf16[2,1024,512]{2,1,0:T(8,128)(2,1)})) %all-reduce.5.cloned.1.call-update) | async-done | bytes 4194320 | tf_op jit(solution)/shard_map/psum | solution.py:9
  169.9 3.3 dynamic-slice_select_fusion
  173.3 49.9 %all-reduce.7.cloned.1.call-done = (bf16[2,512,512]{2,1,0:T(8,128)(2,1)}, bf16[2,512,512]{2,1,0:T(8,128)(2,1)}) async-done(((bf16[2,512,512]{2,1,0:T(8,128)(2,1)}, bf16[2,512,512]{2,1,0:T(8,128)(2,1)}), (bf16[2,512,512]{2,1,0:T(8,128)(2,1)}, bf16[2,512,512]{2,1,0:T(8,128)(2,1)})) %all-reduce.7.cloned.1.call-update) | async-done | bytes 2097168 | tf_op jit(solution)/shard_map/psum | solution.py:9
  223.2 1.9 fusion
  225.1 0.8 fusion.1
  225.9 0.8 add_convert_fusion
  226.7 0.8 subtract_convert_fusion
  227.4 1.5 pad_maximum_fusion.1
  228.9 3.9 %copy.10 = bf16[1024,1024]{1,0:T(8,128)(2,1)} copy(bf16[1024,1024]{0,1:T(8,128)(2,1)} %pad_maximum_fusion.1) | data formatting | bytes 4194304
  232.9 1.1 copy-done
  234.1 0.8 fusion.2
  234.8 0.8 fusion.3
  235.6 0.8 add_convert_fusion.1
  236.4 0.8 subtract_convert_fusion.1
  237.3 2.6 copy.8
  239.9 60.1 %reduce-scatter.9.cloned.1.call-done = bf16[128,1024]{1,0:T(8,128)(2,1)} async-done(((bf16[1024,1024]{1,0:T(8,128)(2,1)}), bf16[128,1024]{1,0:T(8,128)(2,1)}) %reduce-scatter.9.cloned.1.call-update) | async-done | bytes 262160
  300.0 1.1 copy.11
  301.3 69.2 %reduce-scatter.7.cloned.1.call-done = bf16[128,1024]{1,0:T(8,128)(2,1)} async-done(((bf16[1024,1024]{1,0:T(8,128)(2,1)}), bf16[128,1024]{1,0:T(8,128)(2,1)}) %reduce-scatter.7.cloned.1.call-update) | async-done | bytes 262160
  370.4 1.1 copy.9
  371.7 0.8 pad_maximum_fusion.2
  (17 shorter events, 0.9 us)
Async XLA Ops:
  6.5 163.4 %all-reduce.5.cloned.1.call-start = ((), (), s32[]{:S(2)}) async-start(), calls=%async_computation.4 | async-start | bytes 8388608 | tf_op jit(solution)/shard_map/psum | solution.py:9
  6.5 1.8 copy-start.2
  12.0 211.3 %all-reduce.7.cloned.1.call-start = ((), (), s32[]{:S(2)}) async-start(), calls=%async_computation.5 | async-start | bytes 4194304 | tf_op jit(solution)/shard_map/psum | solution.py:9
  173.3 126.7 %reduce-scatter.9.cloned.1.call-start = ((), (), s32[]{:S(2)}) async-start(), calls=%async_computation.3 | async-start | bytes 2359296
  223.2 1.9 copy-start.1
  232.8 1.2 copy-start
  232.9 137.6 %reduce-scatter.7.cloned.1.call-start = ((), (), s32[]{:S(2)}) async-start(), calls=%async_computation.2 | async-start | bytes 2359296
Sparse Core Ops, SparseCore 0:
  12.1 157.7 all-reduce.4
  173.4 49.8 all-reduce.6
  233.0 66.9 reduce-scatter.8
  303.8 66.6 reduce-scatter.6
where the time goes:
time: 383 us; the launch traced here: 379 us
  waiting for transfers between devices  337 us (88%)
  between operations  13.3 us (3%)
  other arithmetic  11 us (3%)
  local copies, waits for them, and re-layouts  10.4 us (3%)
  matrix products  7.18 us (2%)
    psum x2, waiting for transfers between devices, from_root(): return lax.psum(kept, axis)  208 us
    unnamed x6, waiting for transfers between devices  129 us
    unnamed x10, local copies, waits for them, and re-layouts  9.87 us
  transfers between devices with their start and end apart: 4, of which 4 were waited for; matrix products, arithmetic and copies ran while one was open for 2% of the time, Pallas kernels for 0%

commit v1 on v0

v1 whole, which is shorter than its diff:
```python
import functools

import jax
import jax.numpy as jnp
from jax import lax
from jax.experimental import pallas as pl
from jax.experimental.pallas import tpu as pltpu
from jax.sharding import PartitionSpec as P

WAVES = 2
VMEM_BYTES = 48 * 1024 * 1024
VMEM = pl.BlockSpec(memory_space=pltpu.VMEM)
SMEM = pl.BlockSpec(memory_space=pltpu.SMEM)
PARAMS = pltpu.CompilerParams(vmem_limit_bytes=VMEM_BYTES)


def after(value, *done):
    return lax.optimization_barrier((value,) + done)[0]


def bits_of(count):
    return list(range(count.bit_length() - 1))


def layout_kernel(x_count, raw_ref, occupancy_ref, exponent_ref, *refs):
    piece_refs, left_ref, factor_ref = refs[:-2], refs[-2], refs[-1]
    tiles = []
    for tile in range(x_count):
        row = occupancy_ref[tile : tile + 1, :].astype(jnp.float32)
        power = jnp.exp2(jnp.full(row.shape, exponent_ref[0, tile], jnp.int32).astype(jnp.float32))
        tiles.append((row * power).astype(jnp.bfloat16))
        factor_ref[tile] = tiles[tile].astype(jnp.float32)
    _, share, width = piece_refs[0].shape
    for index, out_ref in enumerate(piece_refs):
        wave, tile = divmod(index, x_count)
        columns = slice(wave * width, (wave + 1) * width)
        for part in range(2):
            out_ref[part] = raw_ref[part, tile * share : (tile + 1) * share, columns] * tiles[tile][:, columns]
    col, col_count = lax.axis_index("col"), lax.axis_size("col")
    depth = raw_ref.shape[2]
    rows = raw_ref.shape[1] // col_count
    for distance in range(col_count):
        block = col ^ distance
        factor = factor_ref[block // (col_count // x_count)].astype(jnp.bfloat16)
        start = pl.multiple_of(block * rows, rows)
        for part in range(2):
            value = raw_ref[part, pl.ds(start, rows), :] * factor
            left_ref[distance * rows : (distance + 1) * rows, part * depth : (part + 1) * depth] = value


def lay_out(raw_blocks, occupancy, exponent, x_count):
    _, length, depth = raw_blocks.shape
    piece = jax.ShapeDtypeStruct((2, length // x_count, depth // WAVES), jnp.bfloat16)
    left = jax.ShapeDtypeStruct((length, 2 * depth), jnp.bfloat16)
    count = WAVES * x_count
    out = pl.pallas_call(
        functools.partial(layout_kernel, x_count),
        out_shape=[piece] * count + [left],
        in_specs=[VMEM, VMEM, SMEM],
        out_specs=[VMEM] * (count + 1),
        scratch_shapes=[pltpu.VMEM((x_count, 1, depth), jnp.float32)],
        compiler_params=PARAMS,
    )(raw_blocks, occupancy, exponent.T)
    return out[:count], out[count]


def halves(blocks, bit):
    keep = [block for block in blocks if not block >> bit & 1]
    return [block | 1 << bit for block in keep], keep


def product_kernel(orders, mine_ref, theirs_ref, here_ref, across_ref, *refs):
    outs, slab_ref = refs[:-1], refs[-1]
    row = lax.axis_index("row")
    holds = row // 2 == row % 2
    depth, width = here_ref.shape[1:]

    def build(piece_ref):
        real, imag = piece_ref[0], piece_ref[1]
        slab_ref[:depth, :width] = real
        slab_ref[:depth, width:] = imag
        slab_ref[depth:, :width] = -imag
        slab_ref[depth:, width:] = real

    pl.when(holds)(lambda: build(here_ref))
    pl.when(jnp.logical_not(holds))(lambda: build(across_ref))
    for chain, left_ref in enumerate((mine_ref, theirs_ref)):
        send_ref, keep_ref = outs[2 * chain : 2 * chain + 2]
        blocks, _, rows, _ = send_ref.shape
        send, keep = halves(range(2 * blocks), orders[chain][0])
        value = jnp.dot(left_ref[...], slab_ref[...], preferred_element_type=jnp.float32).astype(send_ref.dtype)
        for out_ref, kept in ((send_ref, send), (keep_ref, keep)):
            for place, block in enumerate(kept):
                for part in range(2):
                    out_ref[place, part] = value[block * rows : (block + 1) * rows, part * width : (part + 1) * width]


def products(orders, mine, theirs, here, across, col_count):
    out = jax.ShapeDtypeStruct((col_count // 2, 2, mine.shape[0] // col_count, here.shape[2]), jnp.bfloat16)
    return pl.pallas_call(
        functools.partial(product_kernel, orders),
        out_shape=[out] * 4,
        in_specs=[VMEM] * 4,
        out_specs=[VMEM] * 4,
        scratch_shapes=[pltpu.VMEM((2 * here.shape[1], 2 * here.shape[2]), jnp.bfloat16)],
        compiler_params=PARAMS,
    )(mine, theirs, here, across)


def halve_kernel(orders, step, joined, *refs):
    ins, outs = refs[:4], refs[4:]
    for chain, order in enumerate(orders):
        keep_ref, other_ref = ins[2 * chain : 2 * chain + 2]
        blocks = range(1 << len(order))
        for bit in order[:step]:
            blocks = halves(blocks, bit)[1]
        blocks = list(blocks)
        for index, kept in enumerate(halves(blocks, order[step])):
            for place, block in enumerate(kept):
                at = blocks.index(block)
                total = keep_ref[at].astype(jnp.float32) + other_ref[at].astype(jnp.float32)
                if joined:
                    outs[index][chain] = total.astype(outs[index].dtype)
                else:
                    outs[2 * chain + index][place] = total.astype(outs[2 * chain + index].dtype)


def halve(orders, step, keeps, others):
    blocks, *rest = keeps[0].shape
    joined = step == len(orders[0]) - 1
    send = jax.ShapeDtypeStruct((2 if joined else blocks // 2, *rest), jnp.bfloat16)
    keep = jax.ShapeDtypeStruct(send.shape, jnp.float32)
    outs = pl.pallas_call(
        functools.partial(halve_kernel, orders, step, joined),
        out_shape=[send, keep] if joined else [send, keep] * 2,
        in_specs=[VMEM] * 4,
        out_specs=[VMEM] * (2 if joined else 4),
        compiler_params=PARAMS,
    )(keeps[0], others[0], keeps[1], others[1])
    return outs[0::2], outs[1::2]


def add_kernel(keep_ref, other_ref, out_ref):
    out_ref[...] = (keep_ref[...] + other_ref[...].astype(jnp.float32)).astype(out_ref.dtype)


def add(keep, other):
    return pl.pallas_call(
        add_kernel,
        out_shape=jax.ShapeDtypeStruct(keep.shape, jnp.bfloat16),
        in_specs=[VMEM] * 2,
        out_specs=VMEM,
        compiler_params=PARAMS,
    )(keep, other)


def solution(mesh):
    row_count, col_count = mesh.shape["row"], mesh.shape["col"]
    x_count = col_count // row_count
    y_count = row_count // 2
    half_cols = col_count // 2
    every = range(row_count * col_count)
    x_bits = bits_of(x_count)
    z_bits = [bit for bit in bits_of(col_count) if bit not in x_bits]
    orders = (x_bits + z_bits, z_bits[:1] + x_bits + z_bits[1:])
    steps = len(orders[0])
    swap_core = [(r, r ^ 1) for r in range(row_count)]

    def exchange(value, bit):
        return lax.ppermute(value, "col", [(c, c ^ (1 << bit)) for c in range(col_count)])

    def filled(pairs):
        def apart(a, b):
            (row_a, col_a), (row_b, col_b) = divmod(a, col_count), divmod(b, col_count)
            far = abs(col_a // x_count - col_b // x_count) + abs(col_a % x_count - col_b % x_count)
            return 4 * far + 4 * abs(row_a // 2 - row_b // 2) + abs(row_a - row_b)

        free = sorted(set(every) - {s for s, _ in pairs})
        for d in sorted(set(every) - {t for _, t in pairs}, key=lambda d: (d not in free, d)):
            nearest = min(free, key=lambda s: (apart(s, d), s))
            free.remove(nearest)
            pairs = pairs + [(nearest, d)]
        return pairs

    def target(s, panel, h):
        return 3 * panel * col_count + s * x_count + h

    def straight_pairs(h):
        return filled(
            [(s * col_count + p * half_cols, target(s, p, h)) for s in range(row_count) for p in range(2)]
        )

    def hop_pairs(h):
        return [(d, d ^ h if d % col_count % half_cols in (0, h) else d) for d in every]

    def spread_pairs():
        return filled(
            [
                (s * col_count + p * half_cols + h, target(s, p, h))
                for s in range(row_count)
                for p in range(2)
                for h in range(x_count)
            ]
        )

    def across_pairs():
        pairs = []
        for r in range(row_count):
            y, core = divmod(r, 2)
            pairs.append((r, r if y > 1 else r ^ 2 if y == core else r ^ 1))
        return pairs

    def to_all_y(here):
        across = lax.ppermute(here, "row", across_pairs())
        y = lax.axis_index("row") // 2
        if y_count > 2:
            slab = jnp.where(y == lax.axis_index("row") % 2, here, across)
            for bit in range(1, y_count.bit_length() - 1):
                got = lax.ppermute(slab, "row", [(r, r ^ (2 << bit)) for r in range(row_count)])
                slab = jnp.where((y >> bit) & 1 == 1, got, slab)
            return slab, slab
        return here, across

    def on_device(raw_blocks, occupancy, exponent):
        my_col = lax.axis_index("col")
        core = lax.axis_index("row") % 2
        x = my_col % x_count
        pieces, left = lay_out(raw_blocks, occupancy, exponent, x_count)

        first = None
        for h in range(x_count):
            got = lax.ppermute(pieces[h], ("row", "col"), straight_pairs(h))
            first = got if h == 0 else jnp.where(x == h, got, first)
        second = pieces[x_count]
        for h in range(1, x_count):
            got = lax.ppermute(pieces[x_count + h], ("row", "col"), hop_pairs(h))
            second = jnp.where(my_col % half_cols == h, got, second)
        first, second = lax.optimization_barrier((first, second))
        theirs = lax.ppermute(left, "row", swap_core)

        second = lax.ppermute(second, ("row", "col"), spread_pairs())
        slabs = to_all_y(first)
        outs = products(orders, left, theirs, *slabs, col_count)
        second = after(second, outs[0])
        slabs = to_all_y(second)

        sums = [None] * WAVES
        state = [None] * WAVES

        def send_step(wave, sends, keeps, step):
            if len(sends) == 1:
                state[wave] = (keeps, [exchange(sends[0], orders[0][step])])
            else:
                state[wave] = (keeps, [exchange(send, order[step]) for send, order in zip(sends, orders)])

        def next_step(wave, step):
            keeps, others = state[wave]
            if step == steps:
                sums[wave] = add(keeps[0], others[0])
            else:
                sends, keeps = halve(orders, step, keeps, others)
                send_step(wave, sends, keeps, step)

        send_step(0, outs[0::2], outs[1::2], 0)
        outs = products(orders, left, theirs, *slabs, col_count)
        send_step(1, outs[0::2], outs[1::2], 0)
        state[0] = (state[0][0], [after(other, outs[0]) for other in state[0][1]])
        for step in range(1, steps + 1):
            next_step(0, step)
            if step > 1:
                mark = sums[0] if step == steps else state[0][0][0]
                keeps, others = state[1]
                state[1] = (keeps, [after(other, mark) for other in others])
                next_step(1, step - 1)
        next_step(1, steps)

        total = jnp.concatenate(sums, axis=-1)
        back = lax.ppermute(total[1], "row", swap_core)
        return jnp.stack([jnp.where(core == 0, total[0], back), jnp.where(core == 0, back, total[0])])

    placed = (P(None, "row", "col"), P("row", "col"), P("row", "col"))
    return jax.shard_map(
        on_device,
        mesh=mesh,
        in_specs=placed,
        out_specs=P(None, None, ("row", "col"), None),
        check_vma=False,
    )
```

time: 383 us -> 121 us (0.32)
  the two profiles are of different devices: /device:TPU:7 before, /device:TPU:0 now
where the time goes in v1:
time: 121 us; the launch traced here: 120 us
  waiting for transfers between devices  71.6 us (59%)
  starting transfers between devices  33.2 us (27%)
  Pallas kernels  11.5 us (10%)
  other arithmetic  2.11 us (2%)
  local copies, waits for them, and re-layouts  1.34 us (1%)
    ppermute x10, waiting for transfers between devices, exchange(): lax.ppermute(value, 'col', [(c, c ^ 1 << bit) for c in range(col_count)])  40.9 us
    ppermute x2, waiting for transfers between devices, to_all_y(): across = lax.ppermute(here, 'row', across_pairs())  13.3 us
    ppermute x2, starting transfers between devices, to_all_y(): across = lax.ppermute(here, 'row', across_pairs())  10.3 us
    ppermute x10, starting transfers between devices, exchange(): lax.ppermute(value, 'col', [(c, c ^ 1 << bit) for c in range(col_count)])  9.97 us
    ppermute x2, starting transfers between devices, on_device(): got = lax.ppermute(pieces[h], ('row', 'col'), straight_pairs(h))  9.75 us
    ppermute x1, waiting for transfers between devices, on_device(): got = lax.ppermute(pieces[x_count + h], ('row', 'col'), hop_pairs(h))  9.27 us
    pallas_call x2, Pallas kernels, products(): pl.pallas_call(functools.partial(product_kernel, orders), out_shape=[out]...  7.97 us
    ppermute x2, waiting for transfers between devices, on_device(): got = lax.ppermute(pieces[h], ('row', 'col'), straight_pairs(h))  6.64 us
  transfers between devices with their start and end apart: 18, of which 10 were waited for; matrix products, arithmetic and copies ran while one was open for 1% of the time, Pallas kernels for 7%

profile of v1, /device:TPU:0, one launch (start us, length us, event | category | flops | bytes accessed | tf_op | source)
XLA Modules:
  0.0 120.0 jit_solution(13097002804928625668)
XLA Ops:
  0.0 0.7 copy-done
  1.3 2.9 %shard_map.37 = (bf16[2,512,256]{2,1,0:T(8,128)(2,1)}, bf16[2,512,256]{2,1,0:T(8,128)(2,1)}, bf16[2,512,256]{2,1,0:T(8,128)(2,1)S(1)}, bf16[2,512,256]{2,1,0:T(8,128)(2,1)S(1)}, bf16[1024,1024]{1,0:T(8,128)(2,1)S(1)}) custom-call(bf16[2,1024,512]{2,1,0:T(8,128)(2,1)} %raw_ref.1, s32[2,512]{1,0:T(2,128)S(1)} %copy-done, s32[1,2]{1,0:T(1,128)S(1)} %bitcast.13), custom_call_target="tpu_custom_call" | custom-call | tf_op jit(solution)/shard_map/pallas_call | solution.py:56
  4.7 4.4 %collective-permute-start.1 = (bf16[2,512,256]{2,1,0:T(8,128)(2,1)}, bf16[2,512,256]{2,1,0:T(8,128)(2,1)}, u32[]{:S(2)}, u32[]{:S(2)}) collective-permute-start(bf16[2,512,256]{2,1,0:T(8,128)(2,1)} %get-tuple-element.40), channel_id=1, source_target_pairs={{0,1},{4,25},{8,3},{12,27},{16,5},{20,29},{24,7},{28,31},{2,2},{6,... | collective-permute-start | bytes 1572872 | tf_op jit(solution)/shard_map/ppermute | solution.py:232
  9.1 5.4 %collective-permute-start.2 = (bf16[2,512,256]{2,1,0:T(8,128)(2,1)}, bf16[2,512,256]{2,1,0:T(8,128)(2,1)}, u32[]{:S(2)}, u32[]{:S(2)}) collective-permute-start(bf16[2,512,256]{2,1,0:T(8,128)(2,1)} %get-tuple-element.41), channel_id=1, source_target_pairs={{0,0},{4,24},{8,2},{12,26},{16,4},{20,28},{24,6},{28,30},{1,1},{3,... | collective-permute-start | bytes 1572872 | tf_op jit(solution)/shard_map/ppermute | solution.py:232
  14.4 1.9 %collective-permute-start.3 = (bf16[2,512,256]{2,1,0:T(8,128)(2,1)S(1)}, bf16[2,512,256]{2,1,0:T(8,128)(2,1)}, u32[]{:S(2)}, u32[]{:S(2)}) collective-permute-start(bf16[2,512,256]{2,1,0:T(8,128)(2,1)S(1)} %get-tuple-element.42), channel_id=1, source_target_pairs={{0,1},{1,0},{2,2},{3,3},{4,5},{5,4},{6,6},{7,7},{8,9},{9,8},{10,10... | collective-permute-start | bytes 1572872 | tf_op jit(solution)/shard_map/ppermute | solution.py:236
  16.4 6.6 %collective-permute-done.1 = bf16[2,512,256]{2,1,0:T(8,128)(2,1)} collective-permute-done((bf16[2,512,256]{2,1,0:T(8,128)(2,1)}, bf16[2,512,256]{2,1,0:T(8,128)(2,1)}, u32[]{:S(2)}, u32[]{:S(2)}) %collective-permute-start.1) | collective-permute-done | bytes 524320 | tf_op jit(solution)/shard_map/ppermute | solution.py:232
  23.0 1.1 broadcast_select_fusion.1.here_ref
  24.1 9.3 %collective-permute-done.3 = bf16[2,512,256]{2,1,0:T(8,128)(2,1)} collective-permute-done((bf16[2,512,256]{2,1,0:T(8,128)(2,1)S(1)}, bf16[2,512,256]{2,1,0:T(8,128)(2,1)}, u32[]{:S(2)}, u32[]{:S(2)}) %collective-permute-start.3) | collective-permute-done | bytes 524320 | tf_op jit(solution)/shard_map/ppermute | solution.py:236
  33.4 3.8 %collective-permute-start.4 = (bf16[2,512,256]{2,1,0:T(8,128)(2,1)S(1)}, bf16[2,512,256]{2,1,0:T(8,128)(2,1)S(1)}, u32[]{:S(2)}, u32[]{:S(2)}) collective-permute-start(bf16[2,512,256]{2,1,0:T(8,128)(2,1)S(1)} %broadcast_select_fusion.1.here_ref), channel_id=1, source_target_pairs={{0,16},{8,0},{16,24},{24,8},{1,17},{9,1},{17,25},{25,9},{2,18},{10... | collective-permute-start | bytes 1572872 | tf_op jit(solution)/shard_map/ppermute | solution.py:214
  37.2 0.7 collective-permute-start.6
  37.9 6.6 %collective-permute-done.4.across_ref = bf16[2,512,256]{2,1,0:T(8,128)(2,1)S(1)} collective-permute-done((bf16[2,512,256]{2,1,0:T(8,128)(2,1)S(1)}, bf16[2,512,256]{2,1,0:T(8,128)(2,1)S(1)}, u32[]{:S(2)}, u32[]{:S(2)}) %collective-permute-start.4) | collective-permute-done | bytes 524320 | tf_op jit(solution)/shard_map/ppermute | solution.py:214
  44.5 4.0 %shard_map.38 = (bf16[4,2,128,256]{3,2,1,0:T(8,128)(2,1)S(1)}, bf16[4,2,128,256]{3,2,1,0:T(8,128)(2,1)S(1)}, bf16[4,2,128,256]{3,2,1,0:T(8,128)(2,1)S(1)}, bf16[4,2,128,256]{3,2,1,0:T(8,128)(2,1)S(1)}) custom-call(bf16[1024,1024]{1,0:T(8,128)(2,1)S(1)} %get-tuple-element.39.mine_ref, bf16[1024,1024]{1,0:T(8,128)(2,1)} %collective-permute-done.theirs_ref, ...), custom_call_target="tpu_custom_call" | custom-call | tf_op jit(solution)/shard_map/pallas_call | solution.py:100
  48.5 6.5 %collective-permute-start.7 = (bf16[2,512,256]{2,1,0:T(8,128)(2,1)S(1)}, bf16[2,512,256]{2,1,0:T(8,128)(2,1)S(1)}, u32[]{:S(2)}, u32[]{:S(2)}) collective-permute-start(bf16[2,512,256]{2,1,0:T(8,128)(2,1)S(1)} %collective-permute-done.6.here_ref), channel_id=1, source_target_pairs={{0,16},{8,0},{16,24},{24,8},{1,17},{9,1},{17,25},{25,9},{2,18},{10... | collective-permute-start | bytes 1572872 | tf_op jit(solution)/shard_map/ppermute | solution.py:214
  55.1 6.7 %collective-permute-done.7.across_ref = bf16[2,512,256]{2,1,0:T(8,128)(2,1)S(1)} collective-permute-done((bf16[2,512,256]{2,1,0:T(8,128)(2,1)S(1)}, bf16[2,512,256]{2,1,0:T(8,128)(2,1)S(1)}, u32[]{:S(2)}, u32[]{:S(2)}) %collective-permute-start.7) | collective-permute-done | bytes 524320 | tf_op jit(solution)/shard_map/ppermute | solution.py:214
  61.8 4.0 %shard_map.39 = (bf16[4,2,128,256]{3,2,1,0:T(8,128)(2,1)S(1)}, bf16[4,2,128,256]{3,2,1,0:T(8,128)(2,1)S(1)}, bf16[4,2,128,256]{3,2,1,0:T(8,128)(2,1)S(1)}, bf16[4,2,128,256]{3,2,1,0:T(8,128)(2,1)S(1)}) custom-call(bf16[1024,1024]{1,0:T(8,128)(2,1)S(1)} %get-tuple-element.39.mine_ref, bf16[1024,1024]{1,0:T(8,128)(2,1)} %collective-permute-done.theirs_ref, ...), custom_call_target="tpu_custom_call" | custom-call | tf_op jit(solution)/shard_map/pallas_call | solution.py:100
  66.2 2.0 %collective-permute-start.9 = (bf16[2,2,128,256]{3,2,1,0:T(8,128)(2,1)S(1)}, bf16[2,2,128,256]{3,2,1,0:T(8,128)(2,1)S(1)}, u32[]{:S(2)}, u32[]{:S(2)}) collective-permute-start(bf16[2,2,128,256]{3,2,1,0:T(8,128)(2,1)S(1)} %get-tuple-element.55), channel_id=1, source_target_pairs={{0,2},{1,3},{2,0},{3,1},{4,6},{5,7},{6,4},{7,5},{8,10},{9,11},{10,... | collective-permute-start | bytes 786440 | tf_op jit(solution)/shard_map/ppermute | solution.py:170
  68.2 2.0 %collective-permute-start.10 = (bf16[2,2,128,256]{3,2,1,0:T(8,128)(2,1)S(1)}, bf16[2,2,128,256]{3,2,1,0:T(8,128)(2,1)S(1)}, u32[]{:S(2)}, u32[]{:S(2)}) collective-permute-start(bf16[2,2,128,256]{3,2,1,0:T(8,128)(2,1)S(1)} %get-tuple-element.57), channel_id=1, source_target_pairs={{0,1},{1,0},{2,3},{3,2},{4,5},{5,4},{6,7},{7,6},{8,9},{9,8},{10,11... | collective-permute-start | bytes 786440 | tf_op jit(solution)/shard_map/ppermute | solution.py:170
  70.2 15.8 %collective-permute-done.9.refs_1_ = bf16[2,2,128,256]{3,2,1,0:T(8,128)(2,1)S(1)} collective-permute-done((bf16[2,2,128,256]{3,2,1,0:T(8,128)(2,1)S(1)}, bf16[2,2,128,256]{3,2,1,0:T(8,128)(2,1)S(1)}, u32[]{:S(2)}, u32[]{:S(2)}) %collective-permute-start.9) | collective-permute-done | bytes 262176 | tf_op jit(solution)/shard_map/ppermute | solution.py:170
  86.1 5.1 %collective-permute-start.11 = (bf16[2,2,128,256]{3,2,1,0:T(8,128)(2,1)S(1)}, bf16[2,2,128,256]{3,2,1,0:T(8,128)(2,1)S(1)}, u32[]{:S(2)}, u32[]{:S(2)}) collective-permute-start(bf16[2,2,128,256]{3,2,1,0:T(8,128)(2,1)S(1)} %get-tuple-element.59), channel_id=1, source_target_pairs={{0,4},{1,5},{2,6},{3,7},{4,0},{5,1},{6,2},{7,3},{8,12},{9,13},{10,... | collective-permute-start | bytes 786440 | tf_op jit(solution)/shard_map/ppermute | solution.py:170
  92.1 10.7 %collective-permute-done.11.other_ref = bf16[2,2,128,256]{3,2,1,0:T(8,128)(2,1)S(1)} collective-permute-done((bf16[2,2,128,256]{3,2,1,0:T(8,128)(2,1)S(1)}, bf16[2,2,128,256]{3,2,1,0:T(8,128)(2,1)S(1)}, u32[]{:S(2)}, u32[]{:S(2)}) %collective-permute-start.11) | collective-permute-done | bytes 262176 | tf_op jit(solution)/shard_map/ppermute | solution.py:170
  102.9 1.8 %collective-permute-done.14.refs_1_ = bf16[2,2,128,256]{3,2,1,0:T(8,128)(2,1)S(1)} collective-permute-done((bf16[2,2,128,256]{3,2,1,0:T(8,128)(2,1)S(1)}, bf16[2,2,128,256]{3,2,1,0:T(8,128)(2,1)S(1)}, u32[]{:S(2)}, u32[]{:S(2)}) %collective-permute-start.14) | collective-permute-done | bytes 262176 | tf_op jit(solution)/shard_map/ppermute | solution.py:170
  104.8 12.5 %collective-permute-done.16.other_ref = bf16[2,2,128,256]{3,2,1,0:T(8,128)(2,1)S(1)} collective-permute-done((bf16[2,2,128,256]{3,2,1,0:T(8,128)(2,1)S(1)}, bf16[2,2,128,256]{3,2,1,0:T(8,128)(2,1)S(1)}, u32[]{:S(2)}, u32[]{:S(2)}) %collective-permute-start.16) | collective-permute-done | bytes 262176 | tf_op jit(solution)/shard_map/ppermute | solution.py:170
  117.5 1.5 %collective-permute-done.17 = bf16[2,128,512]{2,1,0:T(8,128)(2,1)S(1)} collective-permute-done((bf16[2,128,512]{2,1,0:T(8,128)(2,1)S(1)}, bf16[2,128,512]{2,1,0:T(8,128)(2,1)S(1)}, u32[]{:S(2)}, u32[]{:S(2)}) %collective-permute-start.17) | collective-permute-done | bytes 262176 | tf_op jit(solution)/shard_map/ppermute | solution.py:278
  119.1 0.8 pad_maximum_fusion
  (30 shorter events, 3.0 us)
Async XLA Ops:
  0.0 0.7 copy-start
  0.7 0.7 copy-start.1
  4.2 40.3 %collective-permute-start = (bf16[1024,1024]{1,0:T(8,128)(2,1)S(1)}, bf16[1024,1024]{1,0:T(8,128)(2,1)}, u32[]{:S(2)}, u32[]{:S(2)}) collective-permute-start(bf16[1024,1024]{1,0:T(8,128)(2,1)S(1)} %get-tuple-element.39.mine_ref), channel_id=1, source_target_pairs={{0,8},{8,0},{16,24},{24,16},{1,9},{9,1},{17,25},{25,17},{2,10},{10... | collective-permute-start | bytes 6291464 | tf_op jit(solution)/shard_map/ppermute | solution.py:239
  4.7 18.3 %collective-permute-start.1 = (bf16[2,512,256]{2,1,0:T(8,128)(2,1)}, bf16[2,512,256]{2,1,0:T(8,128)(2,1)}, u32[]{:S(2)}, u32[]{:S(2)}) collective-permute-start(bf16[2,512,256]{2,1,0:T(8,128)(2,1)} %get-tuple-element.40), channel_id=1, source_target_pairs={{0,1},{4,25},{8,3},{12,27},{16,5},{20,29},{24,7},{28,31},{2,2},{6,... | collective-permute-start | bytes 1572872 | tf_op jit(solution)/shard_map/ppermute | solution.py:232
  9.1 13.9 %collective-permute-start.2 = (bf16[2,512,256]{2,1,0:T(8,128)(2,1)}, bf16[2,512,256]{2,1,0:T(8,128)(2,1)}, u32[]{:S(2)}, u32[]{:S(2)}) collective-permute-start(bf16[2,512,256]{2,1,0:T(8,128)(2,1)} %get-tuple-element.41), channel_id=1, source_target_pairs={{0,0},{4,24},{8,2},{12,26},{16,4},{20,28},{24,6},{28,30},{1,1},{3,... | collective-permute-start | bytes 1572872 | tf_op jit(solution)/shard_map/ppermute | solution.py:232
  14.4 19.0 %collective-permute-start.3 = (bf16[2,512,256]{2,1,0:T(8,128)(2,1)S(1)}, bf16[2,512,256]{2,1,0:T(8,128)(2,1)}, u32[]{:S(2)}, u32[]{:S(2)}) collective-permute-start(bf16[2,512,256]{2,1,0:T(8,128)(2,1)S(1)} %get-tuple-element.42), channel_id=1, source_target_pairs={{0,1},{1,0},{2,2},{3,3},{4,5},{5,4},{6,6},{7,7},{8,9},{9,8},{10,10... | collective-permute-start | bytes 1572872 | tf_op jit(solution)/shard_map/ppermute | solution.py:236
  33.4 11.1 %collective-permute-start.4 = (bf16[2,512,256]{2,1,0:T(8,128)(2,1)S(1)}, bf16[2,512,256]{2,1,0:T(8,128)(2,1)S(1)}, u32[]{:S(2)}, u32[]{:S(2)}) collective-permute-start(bf16[2,512,256]{2,1,0:T(8,128)(2,1)S(1)} %broadcast_select_fusion.1.here_ref), channel_id=1, source_target_pairs={{0,16},{8,0},{16,24},{24,8},{1,17},{9,1},{17,25},{25,9},{2,18},{10... | collective-permute-start | bytes 1572872 | tf_op jit(solution)/shard_map/ppermute | solution.py:214
  37.2 11.3 %collective-permute-start.6 = (bf16[2,512,256]{2,1,0:T(8,128)(2,1)S(1)}, bf16[2,512,256]{2,1,0:T(8,128)(2,1)S(1)}, u32[]{:S(2)}, u32[]{:S(2)}) collective-permute-start(bf16[2,512,256]{2,1,0:T(8,128)(2,1)S(1)} %broadcast_select_fusion), channel_id=1, source_target_pairs={{0,0},{1,1},{4,24},{5,25},{8,2},{9,3},{12,26},{13,27},{16,4},{17,5... | collective-permute-start | bytes 1572872 | tf_op jit(solution)/shard_map/ppermute | solution.py:241
  48.5 13.2 %collective-permute-start.7 = (bf16[2,512,256]{2,1,0:T(8,128)(2,1)S(1)}, bf16[2,512,256]{2,1,0:T(8,128)(2,1)S(1)}, u32[]{:S(2)}, u32[]{:S(2)}) collective-permute-start(bf16[2,512,256]{2,1,0:T(8,128)(2,1)S(1)} %collective-permute-done.6.here_ref), channel_id=1, source_target_pairs={{0,16},{8,0},{16,24},{24,8},{1,17},{9,1},{17,25},{25,9},{2,18},{10... | collective-permute-start | bytes 1572872 | tf_op jit(solution)/shard_map/ppermute | solution.py:214
  55.1 10.9 %collective-permute-start.8 = (bf16[4,2,128,256]{3,2,1,0:T(8,128)(2,1)S(1)}, bf16[4,2,128,256]{3,2,1,0:T(8,128)(2,1)S(1)}, u32[]{:S(2)}, u32[]{:S(2)}) collective-permute-start(bf16[4,2,128,256]{3,2,1,0:T(8,128)(2,1)S(1)} %get-tuple-element.52), channel_id=1, source_target_pairs={{0,2},{1,3},{2,0},{3,1},{4,6},{5,7},{6,4},{7,5},{8,10},{9,11},{10,... | collective-permute-start | bytes 1572872 | tf_op jit(solution)/shard_map/ppermute | solution.py:170
  55.1 10.9 %collective-permute-start.5 = (bf16[4,2,128,256]{3,2,1,0:T(8,128)(2,1)S(1)}, bf16[4,2,128,256]{3,2,1,0:T(8,128)(2,1)S(1)}, u32[]{:S(2)}, u32[]{:S(2)}) collective-permute-start(bf16[4,2,128,256]{3,2,1,0:T(8,128)(2,1)S(1)} %get-tuple-element.46), channel_id=1, source_target_pairs={{0,1},{1,0},{2,3},{3,2},{4,5},{5,4},{6,7},{7,6},{8,9},{9,8},{10,11... | collective-permute-start | bytes 1572872 | tf_op jit(solution)/shard_map/ppermute | solution.py:170
  65.8 25.5 %collective-permute-start.13 = (bf16[4,2,128,256]{3,2,1,0:T(8,128)(2,1)S(1)}, bf16[4,2,128,256]{3,2,1,0:T(8,128)(2,1)S(1)}, u32[]{:S(2)}, u32[]{:S(2)}) collective-permute-start(bf16[4,2,128,256]{3,2,1,0:T(8,128)(2,1)S(1)} %get-tuple-element.63), channel_id=1, source_target_pairs={{0,2},{1,3},{2,0},{3,1},{4,6},{5,7},{6,4},{7,5},{8,10},{9,11},{10,... | collective-permute-start | bytes 1572872 | tf_op jit(solution)/shard_map/ppermute | solution.py:170
  65.9 25.4 %collective-permute-start.12 = (bf16[4,2,128,256]{3,2,1,0:T(8,128)(2,1)S(1)}, bf16[4,2,128,256]{3,2,1,0:T(8,128)(2,1)S(1)}, u32[]{:S(2)}, u32[]{:S(2)}) collective-permute-start(bf16[4,2,128,256]{3,2,1,0:T(8,128)(2,1)S(1)} %get-tuple-element.49), channel_id=1, source_target_pairs={{0,1},{1,0},{2,3},{3,2},{4,5},{5,4},{6,7},{7,6},{8,9},{9,8},{10,11... | collective-permute-start | bytes 1572872 | tf_op jit(solution)/shard_map/ppermute | solution.py:170
  66.2 19.8 %collective-permute-start.9 = (bf16[2,2,128,256]{3,2,1,0:T(8,128)(2,1)S(1)}, bf16[2,2,128,256]{3,2,1,0:T(8,128)(2,1)S(1)}, u32[]{:S(2)}, u32[]{:S(2)}) collective-permute-start(bf16[2,2,128,256]{3,2,1,0:T(8,128)(2,1)S(1)} %get-tuple-element.55), channel_id=1, source_target_pairs={{0,2},{1,3},{2,0},{3,1},{4,6},{5,7},{6,4},{7,5},{8,10},{9,11},{10,... | collective-permute-start | bytes 786440 | tf_op jit(solution)/shard_map/ppermute | solution.py:170
  68.2 17.9 %collective-permute-start.10 = (bf16[2,2,128,256]{3,2,1,0:T(8,128)(2,1)S(1)}, bf16[2,2,128,256]{3,2,1,0:T(8,128)(2,1)S(1)}, u32[]{:S(2)}, u32[]{:S(2)}) collective-permute-start(bf16[2,2,128,256]{3,2,1,0:T(8,128)(2,1)S(1)} %get-tuple-element.57), channel_id=1, source_target_pairs={{0,1},{1,0},{2,3},{3,2},{4,5},{5,4},{6,7},{7,6},{8,9},{9,8},{10,11... | collective-permute-start | bytes 786440 | tf_op jit(solution)/shard_map/ppermute | solution.py:170
  86.1 16.7 %collective-permute-start.11 = (bf16[2,2,128,256]{3,2,1,0:T(8,128)(2,1)S(1)}, bf16[2,2,128,256]{3,2,1,0:T(8,128)(2,1)S(1)}, u32[]{:S(2)}, u32[]{:S(2)}) collective-permute-start(bf16[2,2,128,256]{3,2,1,0:T(8,128)(2,1)S(1)} %get-tuple-element.59), channel_id=1, source_target_pairs={{0,4},{1,5},{2,6},{3,7},{4,0},{5,1},{6,2},{7,3},{8,12},{9,13},{10,... | collective-permute-start | bytes 786440 | tf_op jit(solution)/shard_map/ppermute | solution.py:170
  91.5 11.4 %collective-permute-start.15 = (bf16[2,2,128,256]{3,2,1,0:T(8,128)(2,1)S(1)}, bf16[2,2,128,256]{3,2,1,0:T(8,128)(2,1)S(1)}, u32[]{:S(2)}, u32[]{:S(2)}) collective-permute-start(bf16[2,2,128,256]{3,2,1,0:T(8,128)(2,1)S(1)} %get-tuple-element.69), channel_id=1, source_target_pairs={{0,1},{1,0},{2,3},{3,2},{4,5},{5,4},{6,7},{7,6},{8,9},{9,8},{10,11... | collective-permute-start | bytes 786440 | tf_op jit(solution)/shard_map/ppermute | solution.py:170
  91.8 12.9 %collective-permute-start.14 = (bf16[2,2,128,256]{3,2,1,0:T(8,128)(2,1)S(1)}, bf16[2,2,128,256]{3,2,1,0:T(8,128)(2,1)S(1)}, u32[]{:S(2)}, u32[]{:S(2)}) collective-permute-start(bf16[2,2,128,256]{3,2,1,0:T(8,128)(2,1)S(1)} %get-tuple-element.66), channel_id=1, source_target_pairs={{0,2},{1,3},{2,0},{3,1},{4,6},{5,7},{6,4},{7,5},{8,10},{9,11},{10,... | collective-permute-start | bytes 786440 | tf_op jit(solution)/shard_map/ppermute | solution.py:170
  104.8 12.6 %collective-permute-start.16 = (bf16[2,2,128,256]{3,2,1,0:T(8,128)(2,1)S(1)}, bf16[2,2,128,256]{3,2,1,0:T(8,128)(2,1)S(1)}, u32[]{:S(2)}, u32[]{:S(2)}) collective-permute-start(bf16[2,2,128,256]{3,2,1,0:T(8,128)(2,1)S(1)} %get-tuple-element.72), channel_id=1, source_target_pairs={{0,4},{1,5},{2,6},{3,7},{4,0},{5,1},{6,2},{7,3},{8,12},{9,13},{10,... | collective-permute-start | bytes 786440 | tf_op jit(solution)/shard_map/ppermute | solution.py:170
  117.5 1.6 %collective-permute-start.17 = (bf16[2,128,512]{2,1,0:T(8,128)(2,1)S(1)}, bf16[2,128,512]{2,1,0:T(8,128)(2,1)S(1)}, u32[]{:S(2)}, u32[]{:S(2)}) collective-permute-start(bf16[2,128,512]{2,1,0:T(8,128)(2,1)S(1)} %fusion.2), channel_id=1, source_target_pairs={{0,8},{8,0},{16,24},{24,16},{1,9},{9,1},{17,25},{25,17},{2,10},{10... | collective-permute-start | bytes 786440 | tf_op jit(solution)/shard_map/ppermute | solution.py:278

commit v2 on v1

--- a/solution.py
+++ b/solution.py
@@ -72,7 +72,7 @@
 def product_kernel(orders, mine_ref, theirs_ref, here_ref, across_ref, *refs):
     outs, slab_ref = refs[:-1], refs[-1]
     row = lax.axis_index("row")
-    holds = row // 2 == row % 2
+    holds = row // 2 + row % 2 == 1
     depth, width = here_ref.shape[1:]
 
     def build(piece_ref):
@@ -173,17 +173,19 @@
         def apart(a, b):
             (row_a, col_a), (row_b, col_b) = divmod(a, col_count), divmod(b, col_count)
             far = abs(col_a // x_count - col_b // x_count) + abs(col_a % x_count - col_b % x_count)
-            return 4 * far + 4 * abs(row_a // 2 - row_b // 2) + abs(row_a - row_b)
-
-        free = sorted(set(every) - {s for s, _ in pairs})
-        for d in sorted(set(every) - {t for _, t in pairs}, key=lambda d: (d not in free, d)):
-            nearest = min(free, key=lambda s: (apart(s, d), s))
-            free.remove(nearest)
-            pairs = pairs + [(nearest, d)]
+            return 2 if a == b else 4 * far + 4 * abs(row_a // 2 - row_b // 2) + abs(row_a - row_b)
+
+        senders = set(every) - {s for s, _ in pairs}
+        receivers = set(every) - {t for _, t in pairs}
+        while receivers:
+            _, s, t = min((apart(s, t), s, t) for s in senders for t in receivers)
+            senders.remove(s)
+            receivers.remove(t)
+            pairs = pairs + [(s, t)]
         return pairs
 
     def target(s, panel, h):
-        return 3 * panel * col_count + s * x_count + h
+        return (2 - panel) * col_count + s * x_count + h
 
     def straight_pairs(h):
         return filled(
@@ -191,7 +193,7 @@
         )
 
     def hop_pairs(h):
-        return [(d, d ^ h if d % col_count % half_cols in (0, h) else d) for d in every]
+        return [(d, d ^ h if d % col_count % half_cols in (0, h) else d ^ col_count) for d in every]
 
     def spread_pairs():
         return filled(
@@ -207,14 +209,14 @@
         pairs = []
         for r in range(row_count):
             y, core = divmod(r, 2)
-            pairs.append((r, r if y > 1 else r ^ 2 if y == core else r ^ 1))
+            pairs.append((r, r ^ 1 if y > 1 or y == core else r ^ 2))
         return pairs
 
     def to_all_y(here):
         across = lax.ppermute(here, "row", across_pairs())
         y = lax.axis_index("row") // 2
         if y_count > 2:
-            slab = jnp.where(y == lax.axis_index("row") % 2, here, across)
+            slab = jnp.where(y + lax.axis_index("row") % 2 == 1, here, across)
             for bit in range(1, y_count.bit_length() - 1):
                 got = lax.ppermute(slab, "row", [(r, r ^ (2 << bit)) for r in range(row_count)])
                 slab = jnp.where((y >> bit) & 1 == 1, got, slab)
@@ -227,21 +229,20 @@
         x = my_col % x_count
         pieces, left = lay_out(raw_blocks, occupancy, exponent, x_count)
 
-        first = None
-        for h in range(x_count):
-            got = lax.ppermute(pieces[h], ("row", "col"), straight_pairs(h))
-            first = got if h == 0 else jnp.where(x == h, got, first)
+        straight = [lax.ppermute(pieces[h], ("row", "col"), straight_pairs(h)) for h in range(x_count)]
         second = pieces[x_count]
         for h in range(1, x_count):
             got = lax.ppermute(pieces[x_count + h], ("row", "col"), hop_pairs(h))
             second = jnp.where(my_col % half_cols == h, got, second)
-        first, second = lax.optimization_barrier((first, second))
+        straight = [after(got, second) for got in straight]
+        first = straight[0]
+        for h in range(1, x_count):
+            first = jnp.where(x == h, straight[h], first)
         theirs = lax.ppermute(left, "row", swap_core)
 
         second = lax.ppermute(second, ("row", "col"), spread_pairs())
         slabs = to_all_y(first)
         outs = products(orders, left, theirs, *slabs, col_count)
-        second = after(second, outs[0])
         slabs = to_all_y(second)
 
         sums = [None] * WAVES

time: 121 us -> 112 us (0.926)
  the two profiles are of different devices: /device:TPU:0 before, /device:TPU:7 now
where the time goes in v2:
time: 112 us; the launch traced here: 110 us
  waiting for transfers between devices  64.9 us (58%)
  starting transfers between devices  29.3 us (26%)
  Pallas kernels  11.5 us (10%)
  other arithmetic  3.15 us (3%)
  local copies, waits for them, and re-layouts  1.34 us (1%)
    ppermute x10, waiting for transfers between devices, exchange(): lax.ppermute(value, 'col', [(c, c ^ 1 << bit) for c in range(col_count)])  41.4 us
    ppermute x1, waiting for transfers between devices, on_device(): got = lax.ppermute(pieces[x_count + h], ('row', 'col'), hop_pairs(h))  16.1 us
    ppermute x10, starting transfers between devices, exchange(): lax.ppermute(value, 'col', [(c, c ^ 1 << bit) for c in range(col_count)])  14.3 us
    ppermute x2, starting transfers between devices, to_all_y(): across = lax.ppermute(here, 'row', across_pairs())  10.2 us
    pallas_call x2, Pallas kernels, products(): pl.pallas_call(functools.partial(product_kernel, orders), out_shape=[out]...  7.97 us
    ppermute x2, waiting for transfers between devices, on_device(): lax.ppermute(pieces[h], ('row', 'col'), straight_pairs(h))  4.84 us
    pallas_call x1, Pallas kernels, lay_out(): pl.pallas_call(functools.partial(layout_kernel, x_count), out_shape=[piec...  2.87 us
    ppermute x1, starting transfers between devices, on_device(): back = lax.ppermute(total[1], 'row', swap_core)  2.64 us
  transfers between devices with their start and end apart: 18, of which 9 were waited for; matrix products, arithmetic and copies ran while one was open for 2% of the time, Pallas kernels for 8%

profile of v2, /device:TPU:7, one launch (start us, length us, event | category | flops | bytes accessed | tf_op | source)
XLA Modules:
  0.0 110.4 jit_solution(9580571479802164486)
XLA Ops:
  1.3 2.9 %shard_map.37 = (bf16[2,512,256]{2,1,0:T(8,128)(2,1)S(1)}, bf16[2,512,256]{2,1,0:T(8,128)(2,1)}, bf16[2,512,256]{2,1,0:T(8,128)(2,1)S(1)}, bf16[2,512,256]{2,1,0:T(8,128)(2,1)}, bf16[1024,1024]{1,0:T(8,128)(2,1)S(1)}) custom-call(bf16[2,1024,512]{2,1,0:T(8,128)(2,1)} %raw_ref.1, s32[2,512]{1,0:T(2,128)S(1)} %copy-done, s32[1,2]{1,0:T(1,128)S(1)} %bitcast.13), custom_call_target="tpu_custom_call" | custom-call | tf_op jit(solution)/shard_map/pallas_call | solution.py:56
  5.1 1.2 %collective-permute-start.1 = (bf16[2,512,256]{2,1,0:T(8,128)(2,1)}, bf16[2,512,256]{2,1,0:T(8,128)(2,1)}, u32[]{:S(2)}, u32[]{:S(2)}) collective-permute-start(bf16[2,512,256]{2,1,0:T(8,128)(2,1)} %get-tuple-element.39), channel_id=1, source_target_pairs={{0,17},{4,9},{8,19},{12,11},{16,21},{20,13},{24,23},{28,15},{2,10}... | collective-permute-start | bytes 1572872 | tf_op jit(solution)/shard_map/ppermute | solution.py:232
  6.4 16.1 %collective-permute-done.2 = bf16[2,512,256]{2,1,0:T(8,128)(2,1)} collective-permute-done((bf16[2,512,256]{2,1,0:T(8,128)(2,1)}, bf16[2,512,256]{2,1,0:T(8,128)(2,1)}, u32[]{:S(2)}, u32[]{:S(2)}) %collective-permute-start.2) | collective-permute-done | bytes 524320 | tf_op jit(solution)/shard_map/ppermute | solution.py:235
  22.4 1.1 broadcast_select_fusion
  23.6 4.8 %collective-permute-done.1 = bf16[2,512,256]{2,1,0:T(8,128)(2,1)} collective-permute-done((bf16[2,512,256]{2,1,0:T(8,128)(2,1)}, bf16[2,512,256]{2,1,0:T(8,128)(2,1)}, u32[]{:S(2)}, u32[]{:S(2)}) %collective-permute-start.1) | collective-permute-done | bytes 524320 | tf_op jit(solution)/shard_map/ppermute | solution.py:232
  28.4 1.1 broadcast_select_fusion.1.here_ref
  29.5 2.4 %collective-permute-start.4 = (bf16[2,512,256]{2,1,0:T(8,128)(2,1)S(1)}, bf16[2,512,256]{2,1,0:T(8,128)(2,1)S(1)}, u32[]{:S(2)}, u32[]{:S(2)}) collective-permute-start(bf16[2,512,256]{2,1,0:T(8,128)(2,1)S(1)} %broadcast_select_fusion.1.here_ref), channel_id=1, source_target_pairs={{0,8},{8,24},{16,0},{24,16},{1,9},{9,25},{17,1},{25,17},{2,10},{10... | collective-permute-start | bytes 1572872 | tf_op jit(solution)/shard_map/ppermute | solution.py:216
  32.0 7.8 %collective-permute-start.7 = (bf16[2,512,256]{2,1,0:T(8,128)(2,1)S(1)}, bf16[2,512,256]{2,1,0:T(8,128)(2,1)S(1)}, u32[]{:S(2)}, u32[]{:S(2)}) collective-permute-start(bf16[2,512,256]{2,1,0:T(8,128)(2,1)S(1)} %collective-permute-done.6.here_ref), channel_id=1, source_target_pairs={{0,8},{8,24},{16,0},{24,16},{1,9},{9,25},{17,1},{25,17},{2,10},{10... | collective-permute-start | bytes 1572872 | tf_op jit(solution)/shard_map/ppermute | solution.py:216
  39.7 1.4 %collective-permute-done.4.across_ref = bf16[2,512,256]{2,1,0:T(8,128)(2,1)S(1)} collective-permute-done((bf16[2,512,256]{2,1,0:T(8,128)(2,1)S(1)}, bf16[2,512,256]{2,1,0:T(8,128)(2,1)S(1)}, u32[]{:S(2)}, u32[]{:S(2)}) %collective-permute-start.4) | collective-permute-done | bytes 524320 | tf_op jit(solution)/shard_map/ppermute | solution.py:216
  41.2 4.0 %shard_map.38 = (bf16[4,2,128,256]{3,2,1,0:T(8,128)(2,1)S(1)}, bf16[4,2,128,256]{3,2,1,0:T(8,128)(2,1)S(1)}, bf16[4,2,128,256]{3,2,1,0:T(8,128)(2,1)S(1)}, bf16[4,2,128,256]{3,2,1,0:T(8,128)(2,1)S(1)}) custom-call(bf16[1024,1024]{1,0:T(8,128)(2,1)S(1)} %get-tuple-element.38.mine_ref, bf16[1024,1024]{1,0:T(8,128)(2,1)} %collective-permute-done.theirs_ref, ...), custom_call_target="tpu_custom_call" | custom-call | tf_op jit(solution)/shard_map/pallas_call | solution.py:100
  45.2 2.8 %collective-permute-start.5 = (bf16[4,2,128,256]{3,2,1,0:T(8,128)(2,1)S(1)}, bf16[4,2,128,256]{3,2,1,0:T(8,128)(2,1)S(1)}, u32[]{:S(2)}, u32[]{:S(2)}) collective-permute-start(bf16[4,2,128,256]{3,2,1,0:T(8,128)(2,1)S(1)} %get-tuple-element.46), channel_id=1, source_target_pairs={{0,1},{1,0},{2,3},{3,2},{4,5},{5,4},{6,7},{7,6},{8,9},{9,8},{10,11... | collective-permute-start | bytes 1572872 | tf_op jit(solution)/shard_map/ppermute | solution.py:170
  47.9 4.0 %shard_map.39 = (bf16[4,2,128,256]{3,2,1,0:T(8,128)(2,1)S(1)}, bf16[4,2,128,256]{3,2,1,0:T(8,128)(2,1)S(1)}, bf16[4,2,128,256]{3,2,1,0:T(8,128)(2,1)S(1)}, bf16[4,2,128,256]{3,2,1,0:T(8,128)(2,1)S(1)}) custom-call(bf16[1024,1024]{1,0:T(8,128)(2,1)S(1)} %get-tuple-element.38.mine_ref, bf16[1024,1024]{1,0:T(8,128)(2,1)} %collective-permute-done.theirs_ref, ...), custom_call_target="tpu_custom_call" | custom-call | tf_op jit(solution)/shard_map/pallas_call | solution.py:100
  51.9 1.5 %collective-permute-start.13 = (bf16[4,2,128,256]{3,2,1,0:T(8,128)(2,1)S(1)}, bf16[4,2,128,256]{3,2,1,0:T(8,128)(2,1)S(1)}, u32[]{:S(2)}, u32[]{:S(2)}) collective-permute-start(bf16[4,2,128,256]{3,2,1,0:T(8,128)(2,1)S(1)} %get-tuple-element.61), channel_id=1, source_target_pairs={{0,2},{1,3},{2,0},{3,1},{4,6},{5,7},{6,4},{7,5},{8,10},{9,11},{10,... | collective-permute-start | bytes 1572872 | tf_op jit(solution)/shard_map/ppermute | solution.py:170
  53.5 2.8 %collective-permute-start.12 = (bf16[4,2,128,256]{3,2,1,0:T(8,128)(2,1)S(1)}, bf16[4,2,128,256]{3,2,1,0:T(8,128)(2,1)S(1)}, u32[]{:S(2)}, u32[]{:S(2)}) collective-permute-start(bf16[4,2,128,256]{3,2,1,0:T(8,128)(2,1)S(1)} %get-tuple-element.47), channel_id=1, source_target_pairs={{0,1},{1,0},{2,3},{3,2},{4,5},{5,4},{6,7},{7,6},{8,9},{9,8},{10,11... | collective-permute-start | bytes 1572872 | tf_op jit(solution)/shard_map/ppermute | solution.py:170
  56.3 4.0 %collective-permute-done.5.refs_1_ = bf16[4,2,128,256]{3,2,1,0:T(8,128)(2,1)S(1)} collective-permute-done((bf16[4,2,128,256]{3,2,1,0:T(8,128)(2,1)S(1)}, bf16[4,2,128,256]{3,2,1,0:T(8,128)(2,1)S(1)}, u32[]{:S(2)}, u32[]{:S(2)}) %collective-permute-start.5) | collective-permute-done | bytes 524320 | tf_op jit(solution)/shard_map/ppermute | solution.py:170
  60.2 0.9 collective-permute-done.8.refs_3_
  62.1 16.0 %collective-permute-done.9.refs_1_ = bf16[2,2,128,256]{3,2,1,0:T(8,128)(2,1)S(1)} collective-permute-done((bf16[2,2,128,256]{3,2,1,0:T(8,128)(2,1)S(1)}, bf16[2,2,128,256]{3,2,1,0:T(8,128)(2,1)S(1)}, u32[]{:S(2)}, u32[]{:S(2)}) %collective-permute-start.9) | collective-permute-done | bytes 262176 | tf_op jit(solution)/shard_map/ppermute | solution.py:170
  78.1 3.3 %collective-permute-start.11 = (bf16[2,2,128,256]{3,2,1,0:T(8,128)(2,1)S(1)}, bf16[2,2,128,256]{3,2,1,0:T(8,128)(2,1)S(1)}, u32[]{:S(2)}, u32[]{:S(2)}) collective-permute-start(bf16[2,2,128,256]{3,2,1,0:T(8,128)(2,1)S(1)} %get-tuple-element.57), channel_id=1, source_target_pairs={{0,4},{1,5},{2,6},{3,7},{4,0},{5,1},{6,2},{7,3},{8,12},{9,13},{10,... | collective-permute-start | bytes 786440 | tf_op jit(solution)/shard_map/ppermute | solution.py:170
  81.6 1.5 %collective-permute-start.14 = (bf16[2,2,128,256]{3,2,1,0:T(8,128)(2,1)S(1)}, bf16[2,2,128,256]{3,2,1,0:T(8,128)(2,1)S(1)}, u32[]{:S(2)}, u32[]{:S(2)}) collective-permute-start(bf16[2,2,128,256]{3,2,1,0:T(8,128)(2,1)S(1)} %get-tuple-element.64), channel_id=1, source_target_pairs={{0,2},{1,3},{2,0},{3,1},{4,6},{5,7},{6,4},{7,5},{8,10},{9,11},{10,... | collective-permute-start | bytes 786440 | tf_op jit(solution)/shard_map/ppermute | solution.py:170
  83.5 9.2 %collective-permute-done.11.other_ref = bf16[2,2,128,256]{3,2,1,0:T(8,128)(2,1)S(1)} collective-permute-done((bf16[2,2,128,256]{3,2,1,0:T(8,128)(2,1)S(1)}, bf16[2,2,128,256]{3,2,1,0:T(8,128)(2,1)S(1)}, u32[]{:S(2)}, u32[]{:S(2)}) %collective-permute-start.11) | collective-permute-done | bytes 262176 | tf_op jit(solution)/shard_map/ppermute | solution.py:170
  92.8 1.4 %collective-permute-start.16 = (bf16[2,2,128,256]{3,2,1,0:T(8,128)(2,1)S(1)}, bf16[2,2,128,256]{3,2,1,0:T(8,128)(2,1)S(1)}, u32[]{:S(2)}, u32[]{:S(2)}) collective-permute-start(bf16[2,2,128,256]{3,2,1,0:T(8,128)(2,1)S(1)} %get-tuple-element.70), channel_id=1, source_target_pairs={{0,4},{1,5},{2,6},{3,7},{4,0},{5,1},{6,2},{7,3},{8,12},{9,13},{10,... | collective-permute-start | bytes 786440 | tf_op jit(solution)/shard_map/ppermute | solution.py:170
  94.2 11.4 %collective-permute-done.16.other_ref = bf16[2,2,128,256]{3,2,1,0:T(8,128)(2,1)S(1)} collective-permute-done((bf16[2,2,128,256]{3,2,1,0:T(8,128)(2,1)S(1)}, bf16[2,2,128,256]{3,2,1,0:T(8,128)(2,1)S(1)}, u32[]{:S(2)}, u32[]{:S(2)}) %collective-permute-start.16) | collective-permute-done | bytes 262176 | tf_op jit(solution)/shard_map/ppermute | solution.py:170
  105.6 2.6 %collective-permute-start.17 = (bf16[2,128,512]{2,1,0:T(8,128)(2,1)S(1)}, bf16[2,128,512]{2,1,0:T(8,128)(2,1)S(1)}, u32[]{:S(2)}, u32[]{:S(2)}) collective-permute-start(bf16[2,128,512]{2,1,0:T(8,128)(2,1)S(1)} %fusion.2), channel_id=1, source_target_pairs={{0,8},{8,0},{16,24},{24,16},{1,9},{9,1},{17,25},{25,17},{2,10},{10... | collective-permute-start | bytes 786440 | tf_op jit(solution)/shard_map/ppermute | solution.py:279
  108.3 1.2 %collective-permute-done.17 = bf16[2,128,512]{2,1,0:T(8,128)(2,1)S(1)} collective-permute-done((bf16[2,128,512]{2,1,0:T(8,128)(2,1)S(1)}, bf16[2,128,512]{2,1,0:T(8,128)(2,1)S(1)}, u32[]{:S(2)}, u32[]{:S(2)}) %collective-permute-start.17) | collective-permute-done | bytes 262176 | tf_op jit(solution)/shard_map/ppermute | solution.py:279
  (30 shorter events, 5.1 us)
Async XLA Ops:
  0.0 0.7 copy-start
  0.7 0.7 copy-start.1
  4.2 37.0 %collective-permute-start = (bf16[1024,1024]{1,0:T(8,128)(2,1)S(1)}, bf16[1024,1024]{1,0:T(8,128)(2,1)}, u32[]{:S(2)}, u32[]{:S(2)}) collective-permute-start(bf16[1024,1024]{1,0:T(8,128)(2,1)S(1)} %get-tuple-element.38.mine_ref), channel_id=1, source_target_pairs={{0,8},{8,0},{16,24},{24,16},{1,9},{9,1},{17,25},{25,17},{2,10},{10... | collective-permute-start | bytes 6291464 | tf_op jit(solution)/shard_map/ppermute | solution.py:241
  4.9 17.5 %collective-permute-start.2 = (bf16[2,512,256]{2,1,0:T(8,128)(2,1)}, bf16[2,512,256]{2,1,0:T(8,128)(2,1)}, u32[]{:S(2)}, u32[]{:S(2)}) collective-permute-start(bf16[2,512,256]{2,1,0:T(8,128)(2,1)} %get-tuple-element.40), channel_id=1, source_target_pairs={{0,1},{1,0},{2,10},{3,11},{4,5},{5,4},{6,14},{7,15},{8,9},{9,8},{1... | collective-permute-start | bytes 1572872 | tf_op jit(solution)/shard_map/ppermute | solution.py:235
  5.1 23.3 %collective-permute-start.1 = (bf16[2,512,256]{2,1,0:T(8,128)(2,1)}, bf16[2,512,256]{2,1,0:T(8,128)(2,1)}, u32[]{:S(2)}, u32[]{:S(2)}) collective-permute-start(bf16[2,512,256]{2,1,0:T(8,128)(2,1)} %get-tuple-element.39), channel_id=1, source_target_pairs={{0,17},{4,9},{8,19},{12,11},{16,21},{20,13},{24,23},{28,15},{2,10}... | collective-permute-start | bytes 1572872 | tf_op jit(solution)/shard_map/ppermute | solution.py:232
  6.4 22.1 %collective-permute-start.3 = (bf16[2,512,256]{2,1,0:T(8,128)(2,1)S(1)}, bf16[2,512,256]{2,1,0:T(8,128)(2,1)}, u32[]{:S(2)}, u32[]{:S(2)}) collective-permute-start(bf16[2,512,256]{2,1,0:T(8,128)(2,1)S(1)} %get-tuple-element.43), channel_id=1, source_target_pairs={{0,16},{4,8},{8,18},{12,10},{16,20},{20,12},{24,22},{28,14},{1,9},... | collective-permute-start | bytes 1572872 | tf_op jit(solution)/shard_map/ppermute | solution.py:232
  23.5 8.4 %collective-permute-start.6 = (bf16[2,512,256]{2,1,0:T(8,128)(2,1)S(1)}, bf16[2,512,256]{2,1,0:T(8,128)(2,1)S(1)}, u32[]{:S(2)}, u32[]{:S(2)}) collective-permute-start(bf16[2,512,256]{2,1,0:T(8,128)(2,1)S(1)} %broadcast_select_fusion), channel_id=1, source_target_pairs={{0,16},{1,17},{4,8},{5,9},{8,18},{9,19},{12,10},{13,11},{16,20},{1... | collective-permute-start | bytes 1572872 | tf_op jit(solution)/shard_map/ppermute | solution.py:243
  29.5 11.6 %collective-permute-start.4 = (bf16[2,512,256]{2,1,0:T(8,128)(2,1)S(1)}, bf16[2,512,256]{2,1,0:T(8,128)(2,1)S(1)}, u32[]{:S(2)}, u32[]{:S(2)}) collective-permute-start(bf16[2,512,256]{2,1,0:T(8,128)(2,1)S(1)} %broadcast_select_fusion.1.here_ref), channel_id=1, source_target_pairs={{0,8},{8,24},{16,0},{24,16},{1,9},{9,25},{17,1},{25,17},{2,10},{10... | collective-permute-start | bytes 1572872 | tf_op jit(solution)/shard_map/ppermute | solution.py:216
  32.0 16.0 %collective-permute-start.7 = (bf16[2,512,256]{2,1,0:T(8,128)(2,1)S(1)}, bf16[2,512,256]{2,1,0:T(8,128)(2,1)S(1)}, u32[]{:S(2)}, u32[]{:S(2)}) collective-permute-start(bf16[2,512,256]{2,1,0:T(8,128)(2,1)S(1)} %collective-permute-done.6.here_ref), channel_id=1, source_target_pairs={{0,8},{8,24},{16,0},{24,16},{1,9},{9,25},{17,1},{25,17},{2,10},{10... | collective-permute-start | bytes 1572872 | tf_op jit(solution)/shard_map/ppermute | solution.py:216
  45.2 15.1 %collective-permute-start.5 = (bf16[4,2,128,256]{3,2,1,0:T(8,128)(2,1)S(1)}, bf16[4,2,128,256]{3,2,1,0:T(8,128)(2,1)S(1)}, u32[]{:S(2)}, u32[]{:S(2)}) collective-permute-start(bf16[4,2,128,256]{3,2,1,0:T(8,128)(2,1)S(1)} %get-tuple-element.46), channel_id=1, source_target_pairs={{0,1},{1,0},{2,3},{3,2},{4,5},{5,4},{6,7},{7,6},{8,9},{9,8},{10,11... | collective-permute-start | bytes 1572872 | tf_op jit(solution)/shard_map/ppermute | solution.py:170
  47.9 13.2 %collective-permute-start.8 = (bf16[4,2,128,256]{3,2,1,0:T(8,128)(2,1)S(1)}, bf16[4,2,128,256]{3,2,1,0:T(8,128)(2,1)S(1)}, u32[]{:S(2)}, u32[]{:S(2)}) collective-permute-start(bf16[4,2,128,256]{3,2,1,0:T(8,128)(2,1)S(1)} %get-tuple-element.50), channel_id=1, source_target_pairs={{0,2},{1,3},{2,0},{3,1},{4,6},{5,7},{6,4},{7,5},{8,10},{9,11},{10,... | collective-permute-start | bytes 1572872 | tf_op jit(solution)/shard_map/ppermute | solution.py:170
  51.9 26.2 %collective-permute-start.13 = (bf16[4,2,128,256]{3,2,1,0:T(8,128)(2,1)S(1)}, bf16[4,2,128,256]{3,2,1,0:T(8,128)(2,1)S(1)}, u32[]{:S(2)}, u32[]{:S(2)}) collective-permute-start(bf16[4,2,128,256]{3,2,1,0:T(8,128)(2,1)S(1)} %get-tuple-element.61), channel_id=1, source_target_pairs={{0,2},{1,3},{2,0},{3,1},{4,6},{5,7},{6,4},{7,5},{8,10},{9,11},{10,... | collective-permute-start | bytes 1572872 | tf_op jit(solution)/shard_map/ppermute | solution.py:170
  53.5 27.9 %collective-permute-start.12 = (bf16[4,2,128,256]{3,2,1,0:T(8,128)(2,1)S(1)}, bf16[4,2,128,256]{3,2,1,0:T(8,128)(2,1)S(1)}, u32[]{:S(2)}, u32[]{:S(2)}) collective-permute-start(bf16[4,2,128,256]{3,2,1,0:T(8,128)(2,1)S(1)} %get-tuple-element.47), channel_id=1, source_target_pairs={{0,1},{1,0},{2,3},{3,2},{4,5},{5,4},{6,7},{7,6},{8,9},{9,8},{10,11... | collective-permute-start | bytes 1572872 | tf_op jit(solution)/shard_map/ppermute | solution.py:170
  61.4 16.6 %collective-permute-start.9 = (bf16[2,2,128,256]{3,2,1,0:T(8,128)(2,1)S(1)}, bf16[2,2,128,256]{3,2,1,0:T(8,128)(2,1)S(1)}, u32[]{:S(2)}, u32[]{:S(2)}) collective-permute-start(bf16[2,2,128,256]{3,2,1,0:T(8,128)(2,1)S(1)} %get-tuple-element.53), channel_id=1, source_target_pairs={{0,2},{1,3},{2,0},{3,1},{4,6},{5,7},{6,4},{7,5},{8,10},{9,11},{10,... | collective-permute-start | bytes 786440 | tf_op jit(solution)/shard_map/ppermute | solution.py:170
  61.8 16.2 %collective-permute-start.10 = (bf16[2,2,128,256]{3,2,1,0:T(8,128)(2,1)S(1)}, bf16[2,2,128,256]{3,2,1,0:T(8,128)(2,1)S(1)}, u32[]{:S(2)}, u32[]{:S(2)}) collective-permute-start(bf16[2,2,128,256]{3,2,1,0:T(8,128)(2,1)S(1)} %get-tuple-element.55), channel_id=1, source_target_pairs={{0,1},{1,0},{2,3},{3,2},{4,5},{5,4},{6,7},{7,6},{8,9},{9,8},{10,11... | collective-permute-start | bytes 786440 | tf_op jit(solution)/shard_map/ppermute | solution.py:170
  78.1 14.5 %collective-permute-start.11 = (bf16[2,2,128,256]{3,2,1,0:T(8,128)(2,1)S(1)}, bf16[2,2,128,256]{3,2,1,0:T(8,128)(2,1)S(1)}, u32[]{:S(2)}, u32[]{:S(2)}) collective-permute-start(bf16[2,2,128,256]{3,2,1,0:T(8,128)(2,1)S(1)} %get-tuple-element.57), channel_id=1, source_target_pairs={{0,4},{1,5},{2,6},{3,7},{4,0},{5,1},{6,2},{7,3},{8,12},{9,13},{10,... | collective-permute-start | bytes 786440 | tf_op jit(solution)/shard_map/ppermute | solution.py:170
  81.6 11.1 %collective-permute-start.14 = (bf16[2,2,128,256]{3,2,1,0:T(8,128)(2,1)S(1)}, bf16[2,2,128,256]{3,2,1,0:T(8,128)(2,1)S(1)}, u32[]{:S(2)}, u32[]{:S(2)}) collective-permute-start(bf16[2,2,128,256]{3,2,1,0:T(8,128)(2,1)S(1)} %get-tuple-element.64), channel_id=1, source_target_pairs={{0,2},{1,3},{2,0},{3,1},{4,6},{5,7},{6,4},{7,5},{8,10},{9,11},{10,... | collective-permute-start | bytes 786440 | tf_op jit(solution)/shard_map/ppermute | solution.py:170
  83.1 9.6 %collective-permute-start.15 = (bf16[2,2,128,256]{3,2,1,0:T(8,128)(2,1)S(1)}, bf16[2,2,128,256]{3,2,1,0:T(8,128)(2,1)S(1)}, u32[]{:S(2)}, u32[]{:S(2)}) collective-permute-start(bf16[2,2,128,256]{3,2,1,0:T(8,128)(2,1)S(1)} %get-tuple-element.67), channel_id=1, source_target_pairs={{0,1},{1,0},{2,3},{3,2},{4,5},{5,4},{6,7},{7,6},{8,9},{9,8},{10,11... | collective-permute-start | bytes 786440 | tf_op jit(solution)/shard_map/ppermute | solution.py:170
  92.8 12.7 %collective-permute-start.16 = (bf16[2,2,128,256]{3,2,1,0:T(8,128)(2,1)S(1)}, bf16[2,2,128,256]{3,2,1,0:T(8,128)(2,1)S(1)}, u32[]{:S(2)}, u32[]{:S(2)}) collective-permute-start(bf16[2,2,128,256]{3,2,1,0:T(8,128)(2,1)S(1)} %get-tuple-element.70), channel_id=1, source_target_pairs={{0,4},{1,5},{2,6},{3,7},{4,0},{5,1},{6,2},{7,3},{8,12},{9,13},{10,... | collective-permute-start | bytes 786440 | tf_op jit(solution)/shard_map/ppermute | solution.py:170
  105.6 3.8 %collective-permute-start.17 = (bf16[2,128,512]{2,1,0:T(8,128)(2,1)S(1)}, bf16[2,128,512]{2,1,0:T(8,128)(2,1)S(1)}, u32[]{:S(2)}, u32[]{:S(2)}) collective-permute-start(bf16[2,128,512]{2,1,0:T(8,128)(2,1)S(1)} %fusion.2), channel_id=1, source_target_pairs={{0,8},{8,0},{16,24},{24,16},{1,9},{9,1},{17,25},{25,17},{2,10},{10... | collective-permute-start | bytes 786440 | tf_op jit(solution)/shard_map/ppermute | solution.py:279

commit v3 on v2

--- a/solution.py
+++ b/solution.py
@@ -69,7 +69,7 @@
     return [block | 1 << bit for block in keep], keep
 
 
-def product_kernel(orders, mine_ref, theirs_ref, here_ref, across_ref, *refs):
+def product_kernel(orders, index, mine_ref, theirs_ref, here_ref, across_ref, *refs):
     outs, slab_ref = refs[:-1], refs[-1]
     row = lax.axis_index("row")
     holds = row // 2 + row % 2 == 1
@@ -84,24 +84,23 @@
 
     pl.when(holds)(lambda: build(here_ref))
     pl.when(jnp.logical_not(holds))(lambda: build(across_ref))
-    for chain, left_ref in enumerate((mine_ref, theirs_ref)):
-        send_ref, keep_ref = outs[2 * chain : 2 * chain + 2]
-        blocks, _, rows, _ = send_ref.shape
-        send, keep = halves(range(2 * blocks), orders[chain][0])
-        value = jnp.dot(left_ref[...], slab_ref[...], preferred_element_type=jnp.float32).astype(send_ref.dtype)
-        for out_ref, kept in ((send_ref, send), (keep_ref, keep)):
-            for place, block in enumerate(kept):
-                for part in range(2):
-                    out_ref[place, part] = value[block * rows : (block + 1) * rows, part * width : (part + 1) * width]
-
-
-def products(orders, mine, theirs, here, across, col_count):
+    for order, left_ref, out_ref in zip(orders, (mine_ref, theirs_ref), outs):
+        count, _, rows, _ = out_ref.shape
+        blocks = halves(range(2 * count), order[0])[index]
+        left = jnp.concatenate([left_ref[block * rows : (block + 1) * rows, :] for block in blocks])
+        value = jnp.dot(left, slab_ref[...], preferred_element_type=jnp.float32).astype(out_ref.dtype)
+        for place in range(count):
+            for part in range(2):
+                out_ref[place, part] = value[place * rows : (place + 1) * rows, part * width : (part + 1) * width]
+
+
+def products(orders, index, mine, theirs, here, across, col_count):
     out = jax.ShapeDtypeStruct((col_count // 2, 2, mine.shape[0] // col_count, here.shape[2]), jnp.bfloat16)
     return pl.pallas_call(
-        functools.partial(product_kernel, orders),
-        out_shape=[out] * 4,
+        functools.partial(product_kernel, orders, index),
+        out_shape=[out] * 2,
         in_specs=[VMEM] * 4,
-        out_specs=[VMEM] * 4,
+        out_specs=[VMEM] * 2,
         scratch_shapes=[pltpu.VMEM((2 * here.shape[1], 2 * here.shape[2]), jnp.bfloat16)],
         compiler_params=PARAMS,
     )(mine, theirs, here, across)
@@ -140,18 +139,40 @@
     return outs[0::2], outs[1::2]
 
 
-def add_kernel(keep_ref, other_ref, out_ref):
-    out_ref[...] = (keep_ref[...] + other_ref[...].astype(jnp.float32)).astype(out_ref.dtype)
+def add_kernel(keep_ref, other_ref, *out_refs):
+    for chain, out_ref in enumerate(out_refs):
+        out_ref[...] = (keep_ref[chain] + other_ref[chain].astype(jnp.float32)).astype(out_ref.dtype)
 
 
 def add(keep, other):
     return pl.pallas_call(
         add_kernel,
-        out_shape=jax.ShapeDtypeStruct(keep.shape, jnp.bfloat16),
+        out_shape=[jax.ShapeDtypeStruct(keep.shape[1:], jnp.bfloat16)] * 2,
         in_specs=[VMEM] * 2,
+        out_specs=[VMEM] * 2,
+        compiler_params=PARAMS,
+    )(keep, other)
+
+
+def place_kernel(*refs):
+    out_ref = refs[-1]
+    core = lax.axis_index("row") % 2
+    for half, panel in enumerate((core, 1 - core)):
+        begin = 0
+        for ref in refs[half * WAVES : (half + 1) * WAVES]:
+            width = ref.shape[-1]
+            out_ref[panel, :, :, begin : begin + width] = ref[...]
+            begin += width
+
+
+def place(own, back, depth):
+    return pl.pallas_call(
+        place_kernel,
+        out_shape=jax.ShapeDtypeStruct((2, *own[0].shape[:-1], depth), jnp.bfloat16),
+        in_specs=[VMEM] * (2 * WAVES),
         out_specs=VMEM,
         compiler_params=PARAMS,
-    )(keep, other)
+    )(*own, *back)
 
 
 def solution(mesh):
@@ -223,9 +244,13 @@
             return slab, slab
         return here, across
 
+    def exchange_step(sends, step):
+        if len(sends) == 1:
+            return [exchange(sends[0], orders[0][step])]
+        return [exchange(send, order[step]) for send, order in zip(sends, orders)]
+
     def on_device(raw_blocks, occupancy, exponent):
         my_col = lax.axis_index("col")
-        core = lax.axis_index("row") % 2
         x = my_col % x_count
         pieces, left = lay_out(raw_blocks, occupancy, exponent, x_count)
 
@@ -241,43 +266,37 @@
         theirs = lax.ppermute(left, "row", swap_core)
 
         second = lax.ppermute(second, ("row", "col"), spread_pairs())
-        slabs = to_all_y(first)
-        outs = products(orders, left, theirs, *slabs, col_count)
-        slabs = to_all_y(second)
-
-        sums = [None] * WAVES
-        state = [None] * WAVES
-
-        def send_step(wave, sends, keeps, step):
-            if len(sends) == 1:
-                state[wave] = (keeps, [exchange(sends[0], orders[0][step])])
-            else:
-                state[wave] = (keeps, [exchange(send, order[step]) for send, order in zip(sends, orders)])
-
-        def next_step(wave, step):
-            keeps, others = state[wave]
-            if step == steps:
-                sums[wave] = add(keeps[0], others[0])
-            else:
-                sends, keeps = halve(orders, step, keeps, others)
-                send_step(wave, sends, keeps, step)
-
-        send_step(0, outs[0::2], outs[1::2], 0)
-        outs = products(orders, left, theirs, *slabs, col_count)
-        send_step(1, outs[0::2], outs[1::2], 0)
-        state[0] = (state[0][0], [after(other, outs[0]) for other in state[0][1]])
-        for step in range(1, steps + 1):
-            next_step(0, step)
+        slabs = [to_all_y(first), to_all_y(second)]
+
+        sends = [[], []]
+        sends[0] = products(orders, 0, left, theirs, *slabs[0], col_count)
+        others = exchange_step(sends[0], 0)
+        keeps = products(orders, 1, left, theirs, *[after(slab, sends[0][0]) for slab in slabs[0]], col_count)
+        sends[1] = products(orders, 0, left, theirs, *[after(slab, keeps[0]) for slab in slabs[1]], col_count)
+        later = exchange_step(sends[1], 0)
+        others = [after(other, sends[1][0]) for other in others]
+        sends[0], keeps = halve(orders, 1, keeps, others)
+        others = exchange_step(sends[0], 1)
+        stay = products(orders, 1, left, theirs, *[after(slab, sends[0][0]) for slab in slabs[1]], col_count)
+        sends[0], keeps = halve(orders, 2, keeps, [after(other, stay[0]) for other in others])
+        others = exchange_step(sends[0], 2)
+        for step in range(1, steps):
+            if step + 1 == steps - 1:
+                mine, other_rows = add(keeps[0], others[0])
+                own, back = [mine], [lax.ppermute(other_rows, "row", swap_core)]
+                mark = mine
+            elif step + 1 < steps - 1:
+                sends[0], keeps = halve(orders, step + 2, keeps, others)
+                others = exchange_step(sends[0], step + 2)
+                mark = sends[0][0]
             if step > 1:
-                mark = sums[0] if step == steps else state[0][0][0]
-                keeps, others = state[1]
-                state[1] = (keeps, [after(other, mark) for other in others])
-                next_step(1, step - 1)
-        next_step(1, steps)
-
-        total = jnp.concatenate(sums, axis=-1)
-        back = lax.ppermute(total[1], "row", swap_core)
-        return jnp.stack([jnp.where(core == 0, total[0], back), jnp.where(core == 0, back, total[0])])
+                later = [after(other, mark) for other in later]
+            sends[1], stay = halve(orders, step, stay, later)
+            later = exchange_step(sends[1], step)
+        mine, other_rows = add(stay[0], later[0])
+        own.append(mine)
+        back.append(lax.ppermute(other_rows, "row", swap_core))
+        return place(own, back, raw_blocks.shape[2])
 
     placed = (P(None, "row", "col"), P("row", "col"), P("row", "col"))
     return jax.shard_map(

time: 112 us -> 111 us (level)
  Pallas kernels: 11.5 us -> 16.1 us
  waiting for transfers between devices: 64.9 us -> 62 us
    pallas_call x4 -> x7, Pallas kernels: 8.06 us -> 12.6 us  [the longest x4 11.6 us: products(): pl.pallas_call(functools.partial(product_kernel, orders, index), out_shap...]
    ppermute x10, waiting for transfers between devices: 41.4 us -> 38.7 us  [exchange(): lax.ppermute(value, 'col', [(c, c ^ 1 << bit) for c in range(col_count)])]
    ppermute x1 -> x2, starting transfers between devices: 2.64 us -> 2.62 us  [the longest x1 2.06 us: on_device(): own, back = ([mine], [lax.ppermute(other_rows, 'row', swap_core)])]
  transfers between devices with their start and end apart: 18 -> 19, of which waited for: 9 -> 10; matrix products, arithmetic and copies ran while one was open for 2% -> 2% of each run, Pallas kernels for 8% -> 11%
where the time goes in v3:
time: 111 us; the launch traced here: 110 us
  waiting for transfers between devices  62 us (56%)
  starting transfers between devices  28.6 us (26%)
  Pallas kernels  16.1 us (15%)
  other arithmetic  2.2 us (2%)
  local copies, waits for them, and re-layouts  1.34 us (1%)
    ppermute x10, waiting for transfers between devices, exchange(): lax.ppermute(value, 'col', [(c, c ^ 1 << bit) for c in range(col_count)])  38.7 us
    ppermute x1, waiting for transfers between devices, on_device(): got = lax.ppermute(pieces[x_count + h], ('row', 'col'), hop_pairs(h))  16.1 us
    ppermute x10, starting transfers between devices, exchange(): lax.ppermute(value, 'col', [(c, c ^ 1 << bit) for c in range(col_count)])  13.6 us
    pallas_call x4, Pallas kernels, products(): pl.pallas_call(functools.partial(product_kernel, orders, index), out_shap...  11.6 us
    ppermute x2, starting transfers between devices, to_all_y(): across = lax.ppermute(here, 'row', across_pairs())  10.2 us
    ppermute x2, waiting for transfers between devices, on_device(): lax.ppermute(pieces[h], ('row', 'col'), straight_pairs(h))  4.84 us
    pallas_call x1, Pallas kernels, lay_out(): pl.pallas_call(functools.partial(layout_kernel, x_count), out_shape=[piec...  2.88 us
  transfers between devices with their start and end apart: 19, of which 10 were waited for; matrix products, arithmetic and copies ran while one was open for 2% of the time, Pallas kernels for 11%

profile of v3, /device:TPU:7, one launch (start us, length us, event | category | flops | bytes accessed | tf_op | source)
XLA Modules:
  0.0 110.4 jit_solution(2244788292643853522)
XLA Ops:
  1.3 2.9 %shard_map.37 = (bf16[2,512,256]{2,1,0:T(8,128)(2,1)S(1)}, bf16[2,512,256]{2,1,0:T(8,128)(2,1)}, bf16[2,512,256]{2,1,0:T(8,128)(2,1)S(1)}, bf16[2,512,256]{2,1,0:T(8,128)(2,1)}, bf16[1024,1024]{1,0:T(8,128)(2,1)S(1)}) custom-call(bf16[2,1024,512]{2,1,0:T(8,128)(2,1)} %raw_ref.1, s32[2,512]{1,0:T(2,128)S(1)} %copy-done, s32[1,2]{1,0:T(1,128)S(1)} %bitcast.1), custom_call_target="tpu_custom_call" | custom-call | tf_op jit(solution)/shard_map/pallas_call | solution.py:56
  5.2 1.2 %collective-permute-start.1 = (bf16[2,512,256]{2,1,0:T(8,128)(2,1)}, bf16[2,512,256]{2,1,0:T(8,128)(2,1)}, u32[]{:S(2)}, u32[]{:S(2)}) collective-permute-start(bf16[2,512,256]{2,1,0:T(8,128)(2,1)} %get-tuple-element.49), channel_id=1, source_target_pairs={{0,17},{4,9},{8,19},{12,11},{16,21},{20,13},{24,23},{28,15},{2,10}... | collective-permute-start | bytes 1572872 | tf_op jit(solution)/shard_map/ppermute | solution.py:257
  6.4 16.1 %collective-permute-done.2 = bf16[2,512,256]{2,1,0:T(8,128)(2,1)} collective-permute-done((bf16[2,512,256]{2,1,0:T(8,128)(2,1)}, bf16[2,512,256]{2,1,0:T(8,128)(2,1)}, u32[]{:S(2)}, u32[]{:S(2)}) %collective-permute-start.2) | collective-permute-done | bytes 524320 | tf_op jit(solution)/shard_map/ppermute | solution.py:260
  22.4 1.1 broadcast_select_fusion
  23.6 4.8 %collective-permute-done.1 = bf16[2,512,256]{2,1,0:T(8,128)(2,1)} collective-permute-done((bf16[2,512,256]{2,1,0:T(8,128)(2,1)}, bf16[2,512,256]{2,1,0:T(8,128)(2,1)}, u32[]{:S(2)}, u32[]{:S(2)}) %collective-permute-start.1) | collective-permute-done | bytes 524320 | tf_op jit(solution)/shard_map/ppermute | solution.py:257
  28.4 1.1 broadcast_select_fusion.1.here_ref
  29.6 2.4 %collective-permute-start.4 = (bf16[2,512,256]{2,1,0:T(8,128)(2,1)S(1)}, bf16[2,512,256]{2,1,0:T(8,128)(2,1)S(1)}, u32[]{:S(2)}, u32[]{:S(2)}) collective-permute-start(bf16[2,512,256]{2,1,0:T(8,128)(2,1)S(1)} %broadcast_select_fusion.1.here_ref), channel_id=1, source_target_pairs={{0,8},{8,24},{16,0},{24,16},{1,9},{9,25},{17,1},{25,17},{2,10},{10... | collective-permute-start | bytes 1572872 | tf_op jit(solution)/shard_map/ppermute | solution.py:237
  32.0 7.8 %collective-permute-start.7 = (bf16[2,512,256]{2,1,0:T(8,128)(2,1)S(1)}, bf16[2,512,256]{2,1,0:T(8,128)(2,1)S(1)}, u32[]{:S(2)}, u32[]{:S(2)}) collective-permute-start(bf16[2,512,256]{2,1,0:T(8,128)(2,1)S(1)} %collective-permute-done.6.here_ref), channel_id=1, source_target_pairs={{0,8},{8,24},{16,0},{24,16},{1,9},{9,25},{17,1},{25,17},{2,10},{10... | collective-permute-start | bytes 1572872 | tf_op jit(solution)/shard_map/ppermute | solution.py:237
  39.7 1.4 %collective-permute-done.4.across_ref = bf16[2,512,256]{2,1,0:T(8,128)(2,1)S(1)} collective-permute-done((bf16[2,512,256]{2,1,0:T(8,128)(2,1)S(1)}, bf16[2,512,256]{2,1,0:T(8,128)(2,1)S(1)}, u32[]{:S(2)}, u32[]{:S(2)}) %collective-permute-start.4) | collective-permute-done | bytes 524320 | tf_op jit(solution)/shard_map/ppermute | solution.py:237
  41.2 2.9 %shard_map.38 = (bf16[4,2,128,256]{3,2,1,0:T(8,128)(2,1)S(1)}, bf16[4,2,128,256]{3,2,1,0:T(8,128)(2,1)S(1)}) custom-call(bf16[1024,1024]{1,0:T(8,128)(2,1)S(1)} %get-tuple-element.48.mine_ref, bf16[1024,1024]{1,0:T(8,128)(2,1)} %collective-permute-done.theirs_ref, bf16[2,512,256]{2,1,0:T(8,128)(2,1)S(1)} %broadcast_select_fusion.1.here_ref, ...), custom_call_target="tpu_custom_call" | custom-call | tf_op jit(solution)/shard_map/pallas_call | solution.py:99
  44.2 2.8 %collective-permute-start.5 = (bf16[4,2,128,256]{3,2,1,0:T(8,128)(2,1)S(1)}, bf16[4,2,128,256]{3,2,1,0:T(8,128)(2,1)S(1)}, u32[]{:S(2)}, u32[]{:S(2)}) collective-permute-start(bf16[4,2,128,256]{3,2,1,0:T(8,128)(2,1)S(1)} %get-tuple-element.55), channel_id=1, source_target_pairs={{0,1},{1,0},{2,3},{3,2},{4,5},{5,4},{6,7},{7,6},{8,9},{9,8},{10,11... | collective-permute-start | bytes 1572872 | tf_op jit(solution)/shard_map/ppermute | solution.py:191
  46.9 2.9 %shard_map.39 = (bf16[4,2,128,256]{3,2,1,0:T(8,128)(2,1)S(1)}, bf16[4,2,128,256]{3,2,1,0:T(8,128)(2,1)S(1)}) custom-call(bf16[1024,1024]{1,0:T(8,128)(2,1)S(1)} %get-tuple-element.48.mine_ref, bf16[1024,1024]{1,0:T(8,128)(2,1)} %collective-permute-done.theirs_ref, bf16[2,512,256]{2,1,0:T(8,128)(2,1)S(1)} %broadcast_select_fusion.1.here_ref, ...), custom_call_target="tpu_custom_call" | custom-call | tf_op jit(solution)/shard_map/pallas_call | solution.py:99
  49.9 2.9 %shard_map.40 = (bf16[4,2,128,256]{3,2,1,0:T(8,128)(2,1)S(1)}, bf16[4,2,128,256]{3,2,1,0:T(8,128)(2,1)S(1)}) custom-call(bf16[1024,1024]{1,0:T(8,128)(2,1)S(1)} %get-tuple-element.48.mine_ref, bf16[1024,1024]{1,0:T(8,128)(2,1)} %collective-permute-done.theirs_ref, bf16[2,512,256]{2,1,0:T(8,128)(2,1)S(1)} %collective-permute-done.6.here_ref, ...), custom_call_target="tpu_custom_call" | custom-call | tf_op jit(solution)/shard_map/pallas_call | solution.py:99
  52.8 1.5 %collective-permute-start.13 = (bf16[4,2,128,256]{3,2,1,0:T(8,128)(2,1)S(1)}, bf16[4,2,128,256]{3,2,1,0:T(8,128)(2,1)S(1)}, u32[]{:S(2)}, u32[]{:S(2)}) collective-permute-start(bf16[4,2,128,256]{3,2,1,0:T(8,128)(2,1)S(1)} %get-tuple-element.79), channel_id=1, source_target_pairs={{0,2},{1,3},{2,0},{3,1},{4,6},{5,7},{6,4},{7,5},{8,10},{9,11},{10,... | collective-permute-start | bytes 1572872 | tf_op jit(solution)/shard_map/ppermute | solution.py:191
  55.2 2.0 %collective-permute-done.8.refs_3_ = bf16[4,2,128,256]{3,2,1,0:T(8,128)(2,1)S(1)} collective-permute-done((bf16[4,2,128,256]{3,2,1,0:T(8,128)(2,1)S(1)}, bf16[4,2,128,256]{3,2,1,0:T(8,128)(2,1)S(1)}, u32[]{:S(2)}, u32[]{:S(2)}) %collective-permute-start.8) | collective-permute-done | bytes 524320 | tf_op jit(solution)/shard_map/ppermute | solution.py:191
  57.2 2.1 %collective-permute-done.5.refs_1_ = bf16[4,2,128,256]{3,2,1,0:T(8,128)(2,1)S(1)} collective-permute-done((bf16[4,2,128,256]{3,2,1,0:T(8,128)(2,1)S(1)}, bf16[4,2,128,256]{3,2,1,0:T(8,128)(2,1)S(1)}, u32[]{:S(2)}, u32[]{:S(2)}) %collective-permute-start.5) | collective-permute-done | bytes 524320 | tf_op jit(solution)/shard_map/ppermute | solution.py:191
  59.5 1.3 %collective-permute-start.10 = (bf16[2,2,128,256]{3,2,1,0:T(8,128)(2,1)S(1)}, bf16[2,2,128,256]{3,2,1,0:T(8,128)(2,1)S(1)}, u32[]{:S(2)}, u32[]{:S(2)}) collective-permute-start(bf16[2,2,128,256]{3,2,1,0:T(8,128)(2,1)S(1)} %get-tuple-element.73), channel_id=1, source_target_pairs={{0,1},{1,0},{2,3},{3,2},{4,5},{5,4},{6,7},{7,6},{8,9},{9,8},{10,11... | collective-permute-start | bytes 786440 | tf_op jit(solution)/shard_map/ppermute | solution.py:191
  61.9 2.9 %shard_map.42 = (bf16[4,2,128,256]{3,2,1,0:T(8,128)(2,1)S(1)}, bf16[4,2,128,256]{3,2,1,0:T(8,128)(2,1)S(1)}) custom-call(bf16[1024,1024]{1,0:T(8,128)(2,1)S(1)} %get-tuple-element.48.mine_ref, bf16[1024,1024]{1,0:T(8,128)(2,1)} %collective-permute-done.theirs_ref, bf16[2,512,256]{2,1,0:T(8,128)(2,1)S(1)} %collective-permute-done.6.here_ref, ...), custom_call_target="tpu_custom_call" | custom-call | tf_op jit(solution)/shard_map/pallas_call | solution.py:99
  64.8 11.3 %collective-permute-done.10.refs_3_ = bf16[2,2,128,256]{3,2,1,0:T(8,128)(2,1)S(1)} collective-permute-done((bf16[2,2,128,256]{3,2,1,0:T(8,128)(2,1)S(1)}, bf16[2,2,128,256]{3,2,1,0:T(8,128)(2,1)S(1)}, u32[]{:S(2)}, u32[]{:S(2)}) %collective-permute-start.10) | collective-permute-done | bytes 262176 | tf_op jit(solution)/shard_map/ppermute | solution.py:191
  76.2 4.4 %collective-permute-start.11 = (bf16[2,2,128,256]{3,2,1,0:T(8,128)(2,1)S(1)}, bf16[2,2,128,256]{3,2,1,0:T(8,128)(2,1)S(1)}, u32[]{:S(2)}, u32[]{:S(2)}) collective-permute-start(bf16[2,2,128,256]{3,2,1,0:T(8,128)(2,1)S(1)} %get-tuple-element.76), channel_id=1, source_target_pairs={{0,4},{1,5},{2,6},{3,7},{4,0},{5,1},{6,2},{7,3},{8,12},{9,13},{10,... | collective-permute-start | bytes 786440 | tf_op jit(solution)/shard_map/ppermute | solution.py:191
  81.0 1.3 %collective-permute-start.15 = (bf16[2,2,128,256]{3,2,1,0:T(8,128)(2,1)S(1)}, bf16[2,2,128,256]{3,2,1,0:T(8,128)(2,1)S(1)}, u32[]{:S(2)}, u32[]{:S(2)}) collective-permute-start(bf16[2,2,128,256]{3,2,1,0:T(8,128)(2,1)S(1)} %get-tuple-element.84), channel_id=1, source_target_pairs={{0,1},{1,0},{2,3},{3,2},{4,5},{5,4},{6,7},{7,6},{8,9},{9,8},{10,11... | collective-permute-start | bytes 786440 | tf_op jit(solution)/shard_map/ppermute | solution.py:191
  82.3 10.5 %collective-permute-done.11.other_ref = bf16[2,2,128,256]{3,2,1,0:T(8,128)(2,1)S(1)} collective-permute-done((bf16[2,2,128,256]{3,2,1,0:T(8,128)(2,1)S(1)}, bf16[2,2,128,256]{3,2,1,0:T(8,128)(2,1)S(1)}, u32[]{:S(2)}, u32[]{:S(2)}) %collective-permute-start.11) | collective-permute-done | bytes 262176 | tf_op jit(solution)/shard_map/ppermute | solution.py:191
  93.3 2.1 %collective-permute-start.17 = (bf16[2,128,256]{2,1,0:T(8,128)(2,1)S(1)}, bf16[2,128,256]{2,1,0:T(8,128)(2,1)S(1)}, u32[]{:S(2)}, u32[]{:S(2)}) collective-permute-start(bf16[2,128,256]{2,1,0:T(8,128)(2,1)S(1)} %get-tuple-element.89), channel_id=1, source_target_pairs={{0,8},{8,0},{16,24},{24,16},{1,9},{9,1},{17,25},{25,17},{2,10},{10... | collective-permute-start | bytes 393224 | tf_op jit(solution)/shard_map/ppermute | solution.py:286
  95.3 12.6 %collective-permute-done.16.other_ref = bf16[2,2,128,256]{3,2,1,0:T(8,128)(2,1)S(1)} collective-permute-done((bf16[2,2,128,256]{3,2,1,0:T(8,128)(2,1)S(1)}, bf16[2,2,128,256]{3,2,1,0:T(8,128)(2,1)S(1)}, u32[]{:S(2)}, u32[]{:S(2)}) %collective-permute-start.16) | collective-permute-done | bytes 262176 | tf_op jit(solution)/shard_map/ppermute | solution.py:191
  (32 shorter events, 8.0 us)
Async XLA Ops:
  0.0 0.7 copy-start
  0.7 0.7 copy-start.1
  4.2 37.0 %collective-permute-start = (bf16[1024,1024]{1,0:T(8,128)(2,1)S(1)}, bf16[1024,1024]{1,0:T(8,128)(2,1)}, u32[]{:S(2)}, u32[]{:S(2)}) collective-permute-start(bf16[1024,1024]{1,0:T(8,128)(2,1)S(1)} %get-tuple-element.48.mine_ref), channel_id=1, source_target_pairs={{0,8},{8,0},{16,24},{24,16},{1,9},{9,1},{17,25},{25,17},{2,10},{10... | collective-permute-start | bytes 6291464 | tf_op jit(solution)/shard_map/ppermute | solution.py:266
  4.9 17.5 %collective-permute-start.2 = (bf16[2,512,256]{2,1,0:T(8,128)(2,1)}, bf16[2,512,256]{2,1,0:T(8,128)(2,1)}, u32[]{:S(2)}, u32[]{:S(2)}) collective-permute-start(bf16[2,512,256]{2,1,0:T(8,128)(2,1)} %get-tuple-element.50), channel_id=1, source_target_pairs={{0,1},{1,0},{2,10},{3,11},{4,5},{5,4},{6,14},{7,15},{8,9},{9,8},{1... | collective-permute-start | bytes 1572872 | tf_op jit(solution)/shard_map/ppermute | solution.py:260
  5.2 23.3 %collective-permute-start.1 = (bf16[2,512,256]{2,1,0:T(8,128)(2,1)}, bf16[2,512,256]{2,1,0:T(8,128)(2,1)}, u32[]{:S(2)}, u32[]{:S(2)}) collective-permute-start(bf16[2,512,256]{2,1,0:T(8,128)(2,1)} %get-tuple-element.49), channel_id=1, source_target_pairs={{0,17},{4,9},{8,19},{12,11},{16,21},{20,13},{24,23},{28,15},{2,10}... | collective-permute-start | bytes 1572872 | tf_op jit(solution)/shard_map/ppermute | solution.py:257
  6.4 22.1 %collective-permute-start.3 = (bf16[2,512,256]{2,1,0:T(8,128)(2,1)S(1)}, bf16[2,512,256]{2,1,0:T(8,128)(2,1)}, u32[]{:S(2)}, u32[]{:S(2)}) collective-permute-start(bf16[2,512,256]{2,1,0:T(8,128)(2,1)S(1)} %get-tuple-element.53), channel_id=1, source_target_pairs={{0,16},{4,8},{8,18},{12,10},{16,20},{20,12},{24,22},{28,14},{1,9},... | collective-permute-start | bytes 1572872 | tf_op jit(solution)/shard_map/ppermute | solution.py:257
  23.5 8.4 %collective-permute-start.6 = (bf16[2,512,256]{2,1,0:T(8,128)(2,1)S(1)}, bf16[2,512,256]{2,1,0:T(8,128)(2,1)S(1)}, u32[]{:S(2)}, u32[]{:S(2)}) collective-permute-start(bf16[2,512,256]{2,1,0:T(8,128)(2,1)S(1)} %broadcast_select_fusion), channel_id=1, source_target_pairs={{0,16},{1,17},{4,8},{5,9},{8,18},{9,19},{12,10},{13,11},{16,20},{1... | collective-permute-start | bytes 1572872 | tf_op jit(solution)/shard_map/ppermute | solution.py:268
  29.6 11.6 %collective-permute-start.4 = (bf16[2,512,256]{2,1,0:T(8,128)(2,1)S(1)}, bf16[2,512,256]{2,1,0:T(8,128)(2,1)S(1)}, u32[]{:S(2)}, u32[]{:S(2)}) collective-permute-start(bf16[2,512,256]{2,1,0:T(8,128)(2,1)S(1)} %broadcast_select_fusion.1.here_ref), channel_id=1, source_target_pairs={{0,8},{8,24},{16,0},{24,16},{1,9},{9,25},{17,1},{25,17},{2,10},{10... | collective-permute-start | bytes 1572872 | tf_op jit(solution)/shard_map/ppermute | solution.py:237
  32.0 17.9 %collective-permute-start.7 = (bf16[2,512,256]{2,1,0:T(8,128)(2,1)S(1)}, bf16[2,512,256]{2,1,0:T(8,128)(2,1)S(1)}, u32[]{:S(2)}, u32[]{:S(2)}) collective-permute-start(bf16[2,512,256]{2,1,0:T(8,128)(2,1)S(1)} %collective-permute-done.6.here_ref), channel_id=1, source_target_pairs={{0,8},{8,24},{16,0},{24,16},{1,9},{9,25},{17,1},{25,17},{2,10},{10... | collective-permute-start | bytes 1572872 | tf_op jit(solution)/shard_map/ppermute | solution.py:237
  44.1 13.1 %collective-permute-start.8 = (bf16[4,2,128,256]{3,2,1,0:T(8,128)(2,1)S(1)}, bf16[4,2,128,256]{3,2,1,0:T(8,128)(2,1)S(1)}, u32[]{:S(2)}, u32[]{:S(2)}) collective-permute-start(bf16[4,2,128,256]{3,2,1,0:T(8,128)(2,1)S(1)} %get-tuple-element.64), channel_id=1, source_target_pairs={{0,2},{1,3},{2,0},{3,1},{4,6},{5,7},{6,4},{7,5},{8,10},{9,11},{10,... | collective-permute-start | bytes 1572872 | tf_op jit(solution)/shard_map/ppermute | solution.py:191
  44.2 15.1 %collective-permute-start.5 = (bf16[4,2,128,256]{3,2,1,0:T(8,128)(2,1)S(1)}, bf16[4,2,128,256]{3,2,1,0:T(8,128)(2,1)S(1)}, u32[]{:S(2)}, u32[]{:S(2)}) collective-permute-start(bf16[4,2,128,256]{3,2,1,0:T(8,128)(2,1)S(1)} %get-tuple-element.55), channel_id=1, source_target_pairs={{0,1},{1,0},{2,3},{3,2},{4,5},{5,4},{6,7},{7,6},{8,9},{9,8},{10,11... | collective-permute-start | bytes 1572872 | tf_op jit(solution)/shard_map/ppermute | solution.py:191
  52.8 27.8 %collective-permute-start.13 = (bf16[4,2,128,256]{3,2,1,0:T(8,128)(2,1)S(1)}, bf16[4,2,128,256]{3,2,1,0:T(8,128)(2,1)S(1)}, u32[]{:S(2)}, u32[]{:S(2)}) collective-permute-start(bf16[4,2,128,256]{3,2,1,0:T(8,128)(2,1)S(1)} %get-tuple-element.79), channel_id=1, source_target_pairs={{0,2},{1,3},{2,0},{3,1},{4,6},{5,7},{6,4},{7,5},{8,10},{9,11},{10,... | collective-permute-start | bytes 1572872 | tf_op jit(solution)/shard_map/ppermute | solution.py:191
  54.2 26.3 %collective-permute-start.12 = (bf16[4,2,128,256]{3,2,1,0:T(8,128)(2,1)S(1)}, bf16[4,2,128,256]{3,2,1,0:T(8,128)(2,1)S(1)}, u32[]{:S(2)}, u32[]{:S(2)}) collective-permute-start(bf16[4,2,128,256]{3,2,1,0:T(8,128)(2,1)S(1)} %get-tuple-element.61), channel_id=1, source_target_pairs={{0,1},{1,0},{2,3},{3,2},{4,5},{5,4},{6,7},{7,6},{8,9},{9,8},{10,11... | collective-permute-start | bytes 1572872 | tf_op jit(solution)/shard_map/ppermute | solution.py:191
  59.5 16.6 %collective-permute-start.10 = (bf16[2,2,128,256]{3,2,1,0:T(8,128)(2,1)S(1)}, bf16[2,2,128,256]{3,2,1,0:T(8,128)(2,1)S(1)}, u32[]{:S(2)}, u32[]{:S(2)}) collective-permute-start(bf16[2,2,128,256]{3,2,1,0:T(8,128)(2,1)S(1)} %get-tuple-element.73), channel_id=1, source_target_pairs={{0,1},{1,0},{2,3},{3,2},{4,5},{5,4},{6,7},{7,6},{8,9},{9,8},{10,11... | collective-permute-start | bytes 786440 | tf_op jit(solution)/shard_map/ppermute | solution.py:191
  60.8 15.3 %collective-permute-start.9 = (bf16[2,2,128,256]{3,2,1,0:T(8,128)(2,1)S(1)}, bf16[2,2,128,256]{3,2,1,0:T(8,128)(2,1)S(1)}, u32[]{:S(2)}, u32[]{:S(2)}) collective-permute-start(bf16[2,2,128,256]{3,2,1,0:T(8,128)(2,1)S(1)} %get-tuple-element.67), channel_id=1, source_target_pairs={{0,2},{1,3},{2,0},{3,1},{4,6},{5,7},{6,4},{7,5},{8,10},{9,11},{10,... | collective-permute-start | bytes 786440 | tf_op jit(solution)/shard_map/ppermute | solution.py:191
  76.2 16.7 %collective-permute-start.11 = (bf16[2,2,128,256]{3,2,1,0:T(8,128)(2,1)S(1)}, bf16[2,2,128,256]{3,2,1,0:T(8,128)(2,1)S(1)}, u32[]{:S(2)}, u32[]{:S(2)}) collective-permute-start(bf16[2,2,128,256]{3,2,1,0:T(8,128)(2,1)S(1)} %get-tuple-element.76), channel_id=1, source_target_pairs={{0,4},{1,5},{2,6},{3,7},{4,0},{5,1},{6,2},{7,3},{8,12},{9,13},{10,... | collective-permute-start | bytes 786440 | tf_op jit(solution)/shard_map/ppermute | solution.py:191
  80.8 12.3 %collective-permute-start.14 = (bf16[2,2,128,256]{3,2,1,0:T(8,128)(2,1)S(1)}, bf16[2,2,128,256]{3,2,1,0:T(8,128)(2,1)S(1)}, u32[]{:S(2)}, u32[]{:S(2)}) collective-permute-start(bf16[2,2,128,256]{3,2,1,0:T(8,128)(2,1)S(1)} %get-tuple-element.81), channel_id=1, source_target_pairs={{0,2},{1,3},{2,0},{3,1},{4,6},{5,7},{6,4},{7,5},{8,10},{9,11},{10,... | collective-permute-start | bytes 786440 | tf_op jit(solution)/shard_map/ppermute | solution.py:191
  81.0 12.1 %collective-permute-start.15 = (bf16[2,2,128,256]{3,2,1,0:T(8,128)(2,1)S(1)}, bf16[2,2,128,256]{3,2,1,0:T(8,128)(2,1)S(1)}, u32[]{:S(2)}, u32[]{:S(2)}) collective-permute-start(bf16[2,2,128,256]{3,2,1,0:T(8,128)(2,1)S(1)} %get-tuple-element.84), channel_id=1, source_target_pairs={{0,1},{1,0},{2,3},{3,2},{4,5},{5,4},{6,7},{7,6},{8,9},{9,8},{10,11... | collective-permute-start | bytes 786440 | tf_op jit(solution)/shard_map/ppermute | solution.py:191
  93.2 14.7 %collective-permute-start.16 = (bf16[2,2,128,256]{3,2,1,0:T(8,128)(2,1)S(1)}, bf16[2,2,128,256]{3,2,1,0:T(8,128)(2,1)S(1)}, u32[]{:S(2)}, u32[]{:S(2)}) collective-permute-start(bf16[2,2,128,256]{3,2,1,0:T(8,128)(2,1)S(1)} %get-tuple-element.87), channel_id=1, source_target_pairs={{0,4},{1,5},{2,6},{3,7},{4,0},{5,1},{6,2},{7,3},{8,12},{9,13},{10,... | collective-permute-start | bytes 786440 | tf_op jit(solution)/shard_map/ppermute | solution.py:191
  93.3 15.3 %collective-permute-start.17 = (bf16[2,128,256]{2,1,0:T(8,128)(2,1)S(1)}, bf16[2,128,256]{2,1,0:T(8,128)(2,1)S(1)}, u32[]{:S(2)}, u32[]{:S(2)}) collective-permute-start(bf16[2,128,256]{2,1,0:T(8,128)(2,1)S(1)} %get-tuple-element.89), channel_id=1, source_target_pairs={{0,8},{8,0},{16,24},{24,16},{1,9},{9,1},{17,25},{25,17},{2,10},{10... | collective-permute-start | bytes 393224 | tf_op jit(solution)/shard_map/ppermute | solution.py:286
  108.0 1.5 %collective-permute-start.18 = (bf16[2,128,256]{2,1,0:T(8,128)(2,1)S(1)}, bf16[2,128,256]{2,1,0:T(8,128)(2,1)S(1)}, u32[]{:S(2)}, u32[]{:S(2)}) collective-permute-start(bf16[2,128,256]{2,1,0:T(8,128)(2,1)S(1)} %get-tuple-element.90), channel_id=1, source_target_pairs={{0,8},{8,0},{16,24},{24,16},{1,9},{9,1},{17,25},{25,17},{2,10},{10... | collective-permute-start | bytes 393224 | tf_op jit(solution)/shard_map/ppermute | solution.py:298

commit v4 on v3

--- a/solution.py
+++ b/solution.py
@@ -126,7 +126,7 @@
 
 def halve(orders, step, keeps, others):
     blocks, *rest = keeps[0].shape
-    joined = step == len(orders[0]) - 1
+    joined = step == len(orders[0]) - 1 and orders[0][step] == orders[1][step]
     send = jax.ShapeDtypeStruct((2 if joined else blocks // 2, *rest), jnp.bfloat16)
     keep = jax.ShapeDtypeStruct(send.shape, jnp.float32)
     outs = pl.pallas_call(
@@ -139,19 +139,22 @@
     return outs[0::2], outs[1::2]
 
 
-def add_kernel(keep_ref, other_ref, *out_refs):
-    for chain, out_ref in enumerate(out_refs):
-        out_ref[...] = (keep_ref[chain] + other_ref[chain].astype(jnp.float32)).astype(out_ref.dtype)
-
-
-def add(keep, other):
+def add_kernel(joined, *refs):
+    ins, outs = refs[:-2], refs[-2:]
+    for chain, out_ref in enumerate(outs):
+        keep_ref, other_ref = ins if joined else ins[2 * chain : 2 * chain + 2]
+        at = chain if joined else 0
+        out_ref[...] = (keep_ref[at] + other_ref[at].astype(jnp.float32)).astype(out_ref.dtype)
+
+
+def add(keeps, others):
     return pl.pallas_call(
-        add_kernel,
-        out_shape=[jax.ShapeDtypeStruct(keep.shape[1:], jnp.bfloat16)] * 2,
-        in_specs=[VMEM] * 2,
+        functools.partial(add_kernel, len(keeps) == 1),
+        out_shape=[jax.ShapeDtypeStruct(keeps[0].shape[1:], jnp.bfloat16)] * 2,
+        in_specs=[VMEM] * (2 * len(keeps)),
         out_specs=[VMEM] * 2,
         compiler_params=PARAMS,
-    )(keep, other)
+    )(*[value for pair in zip(keeps, others) for value in pair])
 
 
 def place_kernel(*refs):
@@ -183,8 +186,11 @@
     every = range(row_count * col_count)
     x_bits = bits_of(x_count)
     z_bits = [bit for bit in bits_of(col_count) if bit not in x_bits]
-    orders = (x_bits + z_bits, z_bits[:1] + x_bits + z_bits[1:])
-    steps = len(orders[0])
+    orders = (
+        (x_bits + z_bits, z_bits[:1] + x_bits + z_bits[1:]),
+        (x_bits + z_bits, z_bits[-1:] + x_bits + z_bits[:-1]),
+    )
+    steps = len(x_bits + z_bits)
     swap_core = [(r, r ^ 1) for r in range(row_count)]
 
     def exchange(value, bit):
@@ -244,10 +250,8 @@
             return slab, slab
         return here, across
 
-    def exchange_step(sends, step):
-        if len(sends) == 1:
-            return [exchange(sends[0], orders[0][step])]
-        return [exchange(send, order[step]) for send, order in zip(sends, orders)]
+    def exchange_step(wave, sends, step):
+        return [exchange(send, order[step]) for send, order in zip(sends, orders[wave])]
 
     def on_device(raw_blocks, occupancy, exponent):
         my_col = lax.axis_index("col")
@@ -269,31 +273,31 @@
         slabs = [to_all_y(first), to_all_y(second)]
 
         sends = [[], []]
-        sends[0] = products(orders, 0, left, theirs, *slabs[0], col_count)
-        others = exchange_step(sends[0], 0)
-        keeps = products(orders, 1, left, theirs, *[after(slab, sends[0][0]) for slab in slabs[0]], col_count)
-        sends[1] = products(orders, 0, left, theirs, *[after(slab, keeps[0]) for slab in slabs[1]], col_count)
-        later = exchange_step(sends[1], 0)
+        sends[0] = products(orders[0], 0, left, theirs, *slabs[0], col_count)
+        others = exchange_step(0, sends[0], 0)
+        keeps = products(orders[0], 1, left, theirs, *[after(slab, sends[0][0]) for slab in slabs[0]], col_count)
+        sends[1] = products(orders[1], 0, left, theirs, *[after(slab, keeps[0]) for slab in slabs[1]], col_count)
+        later = exchange_step(1, sends[1], 0)
         others = [after(other, sends[1][0]) for other in others]
-        sends[0], keeps = halve(orders, 1, keeps, others)
-        others = exchange_step(sends[0], 1)
-        stay = products(orders, 1, left, theirs, *[after(slab, sends[0][0]) for slab in slabs[1]], col_count)
-        sends[0], keeps = halve(orders, 2, keeps, [after(other, stay[0]) for other in others])
-        others = exchange_step(sends[0], 2)
+        sends[0], keeps = halve(orders[0], 1, keeps, others)
+        others = exchange_step(0, sends[0], 1)
+        stay = products(orders[1], 1, left, theirs, *[after(slab, sends[0][0]) for slab in slabs[1]], col_count)
+        sends[0], keeps = halve(orders[0], 2, keeps, [after(other, stay[0]) for other in others])
+        others = exchange_step(0, sends[0], 2)
         for step in range(1, steps):
             if step + 1 == steps - 1:
-                mine, other_rows = add(keeps[0], others[0])
+                mine, other_rows = add(keeps, others)
                 own, back = [mine], [lax.ppermute(other_rows, "row", swap_core)]
                 mark = mine
             elif step + 1 < steps - 1:
-                sends[0], keeps = halve(orders, step + 2, keeps, others)
-                others = exchange_step(sends[0], step + 2)
+                sends[0], keeps = halve(orders[0], step + 2, keeps, others)
+                others = exchange_step(0, sends[0], step + 2)
                 mark = sends[0][0]
             if step > 1:
                 later = [after(other, mark) for other in later]
-            sends[1], stay = halve(orders, step, stay, later)
-            later = exchange_step(sends[1], step)
-        mine, other_rows = add(stay[0], later[0])
+            sends[1], stay = halve(orders[1], step, stay, later)
+            later = exchange_step(1, sends[1], step)
+        mine, other_rows = add(stay, later)
         own.append(mine)
         back.append(lax.ppermute(other_rows, "row", swap_core))
         return place(own, back, raw_blocks.shape[2])

time: 111 us -> 109 us (0.982)
  waiting for transfers between devices: 62 us -> 58.3 us
  starting transfers between devices: 28.6 us -> 30.7 us
    ppermute x10 -> x11, waiting for transfers between devices: 38.7 us -> 35 us  [exchange(): lax.ppermute(value, 'col', [(c, c ^ 1 << bit) for c in range(col_count)])]
    ppermute x1, starting transfers between devices: 0.56 us -> 1.91 us  [on_device(): back.append(lax.ppermute(other_rows, 'row', swap_core))]
    ppermute x10 -> x11, starting transfers between devices: 13.6 us -> 14.1 us  [exchange(): lax.ppermute(value, 'col', [(c, c ^ 1 << bit) for c in range(col_count)])]
  transfers between devices with their start and end apart: 19 -> 20, of which waited for: 10 -> 9; matrix products, arithmetic and copies ran while one was open for 2% -> 2% of each run, Pallas kernels for 11% -> 11%
where the time goes in v4:
time: 109 us
  waiting for transfers between devices  58.3 us (53%)
  starting transfers between devices  30.7 us (28%)
  Pallas kernels  16.1 us (15%)
  other arithmetic  2.2 us (2%)
  local copies, waits for them, and re-layouts  1.34 us (1%)
    ppermute x11, waiting for transfers between devices, exchange(): lax.ppermute(value, 'col', [(c, c ^ 1 << bit) for c in range(col_count)])  35 us
    ppermute x1, waiting for transfers between devices, on_device(): got = lax.ppermute(pieces[x_count + h], ('row', 'col'), hop_pairs(h))  16.1 us
    ppermute x11, starting transfers between devices, exchange(): lax.ppermute(value, 'col', [(c, c ^ 1 << bit) for c in range(col_count)])  14.1 us
    pallas_call x4, Pallas kernels, products(): pl.pallas_call(functools.partial(product_kernel, orders, index), out_shap...  11.6 us
    ppermute x2, starting transfers between devices, to_all_y(): across = lax.ppermute(here, 'row', across_pairs())  10.2 us
    ppermute x2, waiting for transfers between devices, on_device(): lax.ppermute(pieces[h], ('row', 'col'), straight_pairs(h))  4.84 us
    pallas_call x1, Pallas kernels, lay_out(): pl.pallas_call(functools.partial(layout_kernel, x_count), out_shape=[piec...  2.87 us
    ppermute x1, starting transfers between devices, on_device(): own, back = ([mine], [lax.ppermute(other_rows, 'row', swap_core)])  2.35 us
  transfers between devices with their start and end apart: 20, of which 9 were waited for; matrix products, arithmetic and copies ran while one was open for 2% of the time, Pallas kernels for 11%

profile of v4, /device:TPU:7, one launch (start us, length us, event | category | flops | bytes accessed | tf_op | source)
XLA Modules:
  0.0 108.8 jit_solution(809250808658507306)
XLA Ops:
  1.3 2.9 %shard_map.37 = (bf16[2,512,256]{2,1,0:T(8,128)(2,1)S(1)}, bf16[2,512,256]{2,1,0:T(8,128)(2,1)}, bf16[2,512,256]{2,1,0:T(8,128)(2,1)S(1)}, bf16[2,512,256]{2,1,0:T(8,128)(2,1)}, bf16[1024,1024]{1,0:T(8,128)(2,1)S(1)}) custom-call(bf16[2,1024,512]{2,1,0:T(8,128)(2,1)} %raw_ref.1, s32[2,512]{1,0:T(2,128)S(1)} %copy-done, s32[1,2]{1,0:T(1,128)S(1)} %bitcast.1), custom_call_target="tpu_custom_call" | custom-call | tf_op jit(solution)/shard_map/pallas_call | solution.py:56
  5.1 1.2 %collective-permute-start.1 = (bf16[2,512,256]{2,1,0:T(8,128)(2,1)}, bf16[2,512,256]{2,1,0:T(8,128)(2,1)}, u32[]{:S(2)}, u32[]{:S(2)}) collective-permute-start(bf16[2,512,256]{2,1,0:T(8,128)(2,1)} %get-tuple-element.51), channel_id=1, source_target_pairs={{0,17},{4,9},{8,19},{12,11},{16,21},{20,13},{24,23},{28,15},{2,10}... | collective-permute-start | bytes 1572872 | tf_op jit(solution)/shard_map/ppermute | solution.py:261
  6.4 16.1 %collective-permute-done.2 = bf16[2,512,256]{2,1,0:T(8,128)(2,1)} collective-permute-done((bf16[2,512,256]{2,1,0:T(8,128)(2,1)}, bf16[2,512,256]{2,1,0:T(8,128)(2,1)}, u32[]{:S(2)}, u32[]{:S(2)}) %collective-permute-start.2) | collective-permute-done | bytes 524320 | tf_op jit(solution)/shard_map/ppermute | solution.py:264
  22.4 1.1 %broadcast_select_fusion = bf16[2,512,256]{2,1,0:T(8,128)(2,1)S(1)} fusion(bf16[2,512,256]{2,1,0:T(8,128)(2,1)} %collective-permute-done.2, bf16[2,512,256]{2,1,0:T(8,128)(2,1)S(1)} %get-tuple-element.53, pred[]{:T(512)S(6)} %eq.10), kind=kLoop, calls=%fused_computation | loop fusion | flops 262144 | bytes 1572865 | tf_op jit(solution)/shard_map/jit(_where)/select_n | solution.py:265
  23.6 4.8 %collective-permute-done.1 = bf16[2,512,256]{2,1,0:T(8,128)(2,1)} collective-permute-done((bf16[2,512,256]{2,1,0:T(8,128)(2,1)}, bf16[2,512,256]{2,1,0:T(8,128)(2,1)}, u32[]{:S(2)}, u32[]{:S(2)}) %collective-permute-start.1) | collective-permute-done | bytes 524320 | tf_op jit(solution)/shard_map/ppermute | solution.py:261
  28.4 1.1 %broadcast_select_fusion.1.here_ref = bf16[2,512,256]{2,1,0:T(8,128)(2,1)S(1)} fusion(bf16[2,512,256]{2,1,0:T(8,128)(2,1)} %collective-permute-done.1, bf16[2,512,256]{2,1,0:T(8,128)(2,1)} %collective-permute-done.3, pred[]{:T(512)S(6)} %eq.9), kind=kLoop, calls=%fused_computation.1 | loop fusion | flops 262144 | bytes 1572865 | tf_op jit(solution)/shard_map/jit(_where)/select_n | solution.py:269
  29.6 2.4 %collective-permute-start.4 = (bf16[2,512,256]{2,1,0:T(8,128)(2,1)S(1)}, bf16[2,512,256]{2,1,0:T(8,128)(2,1)S(1)}, u32[]{:S(2)}, u32[]{:S(2)}) collective-permute-start(bf16[2,512,256]{2,1,0:T(8,128)(2,1)S(1)} %broadcast_select_fusion.1.here_ref), channel_id=1, source_target_pairs={{0,8},{8,24},{16,0},{24,16},{1,9},{9,25},{17,1},{25,17},{2,10},{10... | collective-permute-start | bytes 1572872 | tf_op jit(solution)/shard_map/ppermute | solution.py:243
  32.0 7.8 %collective-permute-start.7 = (bf16[2,512,256]{2,1,0:T(8,128)(2,1)S(1)}, bf16[2,512,256]{2,1,0:T(8,128)(2,1)S(1)}, u32[]{:S(2)}, u32[]{:S(2)}) collective-permute-start(bf16[2,512,256]{2,1,0:T(8,128)(2,1)S(1)} %collective-permute-done.6.here_ref), channel_id=1, source_target_pairs={{0,8},{8,24},{16,0},{24,16},{1,9},{9,25},{17,1},{25,17},{2,10},{10... | collective-permute-start | bytes 1572872 | tf_op jit(solution)/shard_map/ppermute | solution.py:243
  39.7 1.4 %collective-permute-done.4.across_ref = bf16[2,512,256]{2,1,0:T(8,128)(2,1)S(1)} collective-permute-done((bf16[2,512,256]{2,1,0:T(8,128)(2,1)S(1)}, bf16[2,512,256]{2,1,0:T(8,128)(2,1)S(1)}, u32[]{:S(2)}, u32[]{:S(2)}) %collective-permute-start.4) | collective-permute-done | bytes 524320 | tf_op jit(solution)/shard_map/ppermute | solution.py:243
  41.2 2.9 %shard_map.38 = (bf16[4,2,128,256]{3,2,1,0:T(8,128)(2,1)S(1)}, bf16[4,2,128,256]{3,2,1,0:T(8,128)(2,1)S(1)}) custom-call(bf16[1024,1024]{1,0:T(8,128)(2,1)S(1)} %get-tuple-element.50.mine_ref, bf16[1024,1024]{1,0:T(8,128)(2,1)} %collective-permute-done.theirs_ref, bf16[2,512,256]{2,1,0:T(8,128)(2,1)S(1)} %broadcast_select_fusion.1.here_ref, ...), custom_call_target="tpu_custom_call" | custom-call | tf_op jit(solution)/shard_map/pallas_call | solution.py:99
  44.2 2.8 %collective-permute-start.5 = (bf16[4,2,128,256]{3,2,1,0:T(8,128)(2,1)S(1)}, bf16[4,2,128,256]{3,2,1,0:T(8,128)(2,1)S(1)}, u32[]{:S(2)}, u32[]{:S(2)}) collective-permute-start(bf16[4,2,128,256]{3,2,1,0:T(8,128)(2,1)S(1)} %get-tuple-element.57), channel_id=1, source_target_pairs={{0,1},{1,0},{2,3},{3,2},{4,5},{5,4},{6,7},{7,6},{8,9},{9,8},{10,11... | collective-permute-start | bytes 1572872 | tf_op jit(solution)/shard_map/ppermute | solution.py:197
  46.9 2.9 %shard_map.39 = (bf16[4,2,128,256]{3,2,1,0:T(8,128)(2,1)S(1)}, bf16[4,2,128,256]{3,2,1,0:T(8,128)(2,1)S(1)}) custom-call(bf16[1024,1024]{1,0:T(8,128)(2,1)S(1)} %get-tuple-element.50.mine_ref, bf16[1024,1024]{1,0:T(8,128)(2,1)} %collective-permute-done.theirs_ref, bf16[2,512,256]{2,1,0:T(8,128)(2,1)S(1)} %broadcast_select_fusion.1.here_ref, ...), custom_call_target="tpu_custom_call" | custom-call | tf_op jit(solution)/shard_map/pallas_call | solution.py:99
  49.9 2.9 %shard_map.40 = (bf16[4,2,128,256]{3,2,1,0:T(8,128)(2,1)S(1)}, bf16[4,2,128,256]{3,2,1,0:T(8,128)(2,1)S(1)}) custom-call(bf16[1024,1024]{1,0:T(8,128)(2,1)S(1)} %get-tuple-element.50.mine_ref, bf16[1024,1024]{1,0:T(8,128)(2,1)} %collective-permute-done.theirs_ref, bf16[2,512,256]{2,1,0:T(8,128)(2,1)S(1)} %collective-permute-done.6.here_ref, ...), custom_call_target="tpu_custom_call" | custom-call | tf_op jit(solution)/shard_map/pallas_call | solution.py:99
  52.8 4.6 %collective-permute-start.13 = (bf16[4,2,128,256]{3,2,1,0:T(8,128)(2,1)S(1)}, bf16[4,2,128,256]{3,2,1,0:T(8,128)(2,1)S(1)}, u32[]{:S(2)}, u32[]{:S(2)}) collective-permute-start(bf16[4,2,128,256]{3,2,1,0:T(8,128)(2,1)S(1)} %get-tuple-element.81), channel_id=1, source_target_pairs={{0,4},{1,5},{2,6},{3,7},{4,0},{5,1},{6,2},{7,3},{8,12},{9,13},{10,... | collective-permute-start | bytes 1572872 | tf_op jit(solution)/shard_map/ppermute | solution.py:197
  57.4 1.8 %collective-permute-done.5.refs_1_ = bf16[4,2,128,256]{3,2,1,0:T(8,128)(2,1)S(1)} collective-permute-done((bf16[4,2,128,256]{3,2,1,0:T(8,128)(2,1)S(1)}, bf16[4,2,128,256]{3,2,1,0:T(8,128)(2,1)S(1)}, u32[]{:S(2)}, u32[]{:S(2)}) %collective-permute-start.5) | collective-permute-done | bytes 524320 | tf_op jit(solution)/shard_map/ppermute | solution.py:197
  59.5 6.2 %collective-permute-start.10 = (bf16[2,2,128,256]{3,2,1,0:T(8,128)(2,1)S(1)}, bf16[2,2,128,256]{3,2,1,0:T(8,128)(2,1)S(1)}, u32[]{:S(2)}, u32[]{:S(2)}) collective-permute-start(bf16[2,2,128,256]{3,2,1,0:T(8,128)(2,1)S(1)} %get-tuple-element.75), channel_id=1, source_target_pairs={{0,1},{1,0},{2,3},{3,2},{4,5},{5,4},{6,7},{7,6},{8,9},{9,8},{10,11... | collective-permute-start | bytes 786440 | tf_op jit(solution)/shard_map/ppermute | solution.py:197
  65.7 2.9 %shard_map.42 = (bf16[4,2,128,256]{3,2,1,0:T(8,128)(2,1)S(1)}, bf16[4,2,128,256]{3,2,1,0:T(8,128)(2,1)S(1)}) custom-call(bf16[1024,1024]{1,0:T(8,128)(2,1)S(1)} %get-tuple-element.50.mine_ref, bf16[1024,1024]{1,0:T(8,128)(2,1)} %collective-permute-done.theirs_ref, bf16[2,512,256]{2,1,0:T(8,128)(2,1)S(1)} %collective-permute-done.6.here_ref, ...), custom_call_target="tpu_custom_call" | custom-call | tf_op jit(solution)/shard_map/pallas_call | solution.py:99
  68.6 7.0 %collective-permute-done.10.refs_3_ = bf16[2,2,128,256]{3,2,1,0:T(8,128)(2,1)S(1)} collective-permute-done((bf16[2,2,128,256]{3,2,1,0:T(8,128)(2,1)S(1)}, bf16[2,2,128,256]{3,2,1,0:T(8,128)(2,1)S(1)}, u32[]{:S(2)}, u32[]{:S(2)}) %collective-permute-start.10) | collective-permute-done | bytes 262176 | tf_op jit(solution)/shard_map/ppermute | solution.py:197
  75.6 8.3 %collective-permute-done.9.refs_1_ = bf16[2,2,128,256]{3,2,1,0:T(8,128)(2,1)S(1)} collective-permute-done((bf16[2,2,128,256]{3,2,1,0:T(8,128)(2,1)S(1)}, bf16[2,2,128,256]{3,2,1,0:T(8,128)(2,1)S(1)}, u32[]{:S(2)}, u32[]{:S(2)}) %collective-permute-start.9) | collective-permute-done | bytes 262176 | tf_op jit(solution)/shard_map/ppermute | solution.py:197
  84.5 13.3 %collective-permute-done.11.refs_1_ = bf16[2,2,128,256]{3,2,1,0:T(8,128)(2,1)S(1)} collective-permute-done((bf16[2,2,128,256]{3,2,1,0:T(8,128)(2,1)S(1)}, bf16[2,2,128,256]{3,2,1,0:T(8,128)(2,1)S(1)}, u32[]{:S(2)}, u32[]{:S(2)}) %collective-permute-start.11) | collective-permute-done | bytes 262176 | tf_op jit(solution)/shard_map/ppermute | solution.py:197
  98.2 2.4 %collective-permute-start.18 = (bf16[2,128,256]{2,1,0:T(8,128)(2,1)S(1)}, bf16[2,128,256]{2,1,0:T(8,128)(2,1)S(1)}, u32[]{:S(2)}, u32[]{:S(2)}) collective-permute-start(bf16[2,128,256]{2,1,0:T(8,128)(2,1)S(1)} %get-tuple-element.93), channel_id=1, source_target_pairs={{0,8},{8,0},{16,24},{24,16},{1,9},{9,1},{17,25},{25,17},{2,10},{10... | collective-permute-start | bytes 393224 | tf_op jit(solution)/shard_map/ppermute | solution.py:290
  100.5 4.5 %collective-permute-done.16.refs_1_ = bf16[1,2,128,256]{3,2,1,0:T(8,128)(2,1)S(1)} collective-permute-done((bf16[1,2,128,256]{3,2,1,0:T(8,128)(2,1)S(1)}, bf16[1,2,128,256]{3,2,1,0:T(8,128)(2,1)S(1)}, u32[]{:S(2)}, u32[]{:S(2)}) %collective-permute-start.16) | collective-permute-done | bytes 131104 | tf_op jit(solution)/shard_map/ppermute | solution.py:197
  105.1 1.9 %collective-permute-start.19 = (bf16[2,128,256]{2,1,0:T(8,128)(2,1)S(1)}, bf16[2,128,256]{2,1,0:T(8,128)(2,1)S(1)}, u32[]{:S(2)}, u32[]{:S(2)}) collective-permute-start(bf16[2,128,256]{2,1,0:T(8,128)(2,1)S(1)} %get-tuple-element.94), channel_id=1, source_target_pairs={{0,8},{8,0},{16,24},{24,16},{1,9},{9,1},{17,25},{25,17},{2,10},{10... | collective-permute-start | bytes 393224 | tf_op jit(solution)/shard_map/ppermute | solution.py:302
  107.0 1.0 collective-permute-done.19.refs_3_
  (34 shorter events, 4.3 us)
Async XLA Ops:
  0.0 0.7 copy-start
  0.7 0.7 copy-start.1
  4.2 37.0 %collective-permute-start = (bf16[1024,1024]{1,0:T(8,128)(2,1)S(1)}, bf16[1024,1024]{1,0:T(8,128)(2,1)}, u32[]{:S(2)}, u32[]{:S(2)}) collective-permute-start(bf16[1024,1024]{1,0:T(8,128)(2,1)S(1)} %get-tuple-element.50.mine_ref), channel_id=1, source_target_pairs={{0,8},{8,0},{16,24},{24,16},{1,9},{9,1},{17,25},{25,17},{2,10},{10... | collective-permute-start | bytes 6291464 | tf_op jit(solution)/shard_map/ppermute | solution.py:270
  4.9 17.5 %collective-permute-start.2 = (bf16[2,512,256]{2,1,0:T(8,128)(2,1)}, bf16[2,512,256]{2,1,0:T(8,128)(2,1)}, u32[]{:S(2)}, u32[]{:S(2)}) collective-permute-start(bf16[2,512,256]{2,1,0:T(8,128)(2,1)} %get-tuple-element.52), channel_id=1, source_target_pairs={{0,1},{1,0},{2,10},{3,11},{4,5},{5,4},{6,14},{7,15},{8,9},{9,8},{1... | collective-permute-start | bytes 1572872 | tf_op jit(solution)/shard_map/ppermute | solution.py:264
  5.1 23.3 %collective-permute-start.1 = (bf16[2,512,256]{2,1,0:T(8,128)(2,1)}, bf16[2,512,256]{2,1,0:T(8,128)(2,1)}, u32[]{:S(2)}, u32[]{:S(2)}) collective-permute-start(bf16[2,512,256]{2,1,0:T(8,128)(2,1)} %get-tuple-element.51), channel_id=1, source_target_pairs={{0,17},{4,9},{8,19},{12,11},{16,21},{20,13},{24,23},{28,15},{2,10}... | collective-permute-start | bytes 1572872 | tf_op jit(solution)/shard_map/ppermute | solution.py:261
  6.4 22.1 %collective-permute-start.3 = (bf16[2,512,256]{2,1,0:T(8,128)(2,1)S(1)}, bf16[2,512,256]{2,1,0:T(8,128)(2,1)}, u32[]{:S(2)}, u32[]{:S(2)}) collective-permute-start(bf16[2,512,256]{2,1,0:T(8,128)(2,1)S(1)} %get-tuple-element.55), channel_id=1, source_target_pairs={{0,16},{4,8},{8,18},{12,10},{16,20},{20,12},{24,22},{28,14},{1,9},... | collective-permute-start | bytes 1572872 | tf_op jit(solution)/shard_map/ppermute | solution.py:261
  23.5 8.4 %collective-permute-start.6 = (bf16[2,512,256]{2,1,0:T(8,128)(2,1)S(1)}, bf16[2,512,256]{2,1,0:T(8,128)(2,1)S(1)}, u32[]{:S(2)}, u32[]{:S(2)}) collective-permute-start(bf16[2,512,256]{2,1,0:T(8,128)(2,1)S(1)} %broadcast_select_fusion), channel_id=1, source_target_pairs={{0,16},{1,17},{4,8},{5,9},{8,18},{9,19},{12,10},{13,11},{16,20},{1... | collective-permute-start | bytes 1572872 | tf_op jit(solution)/shard_map/ppermute | solution.py:272
  29.6 11.6 %collective-permute-start.4 = (bf16[2,512,256]{2,1,0:T(8,128)(2,1)S(1)}, bf16[2,512,256]{2,1,0:T(8,128)(2,1)S(1)}, u32[]{:S(2)}, u32[]{:S(2)}) collective-permute-start(bf16[2,512,256]{2,1,0:T(8,128)(2,1)S(1)} %broadcast_select_fusion.1.here_ref), channel_id=1, source_target_pairs={{0,8},{8,24},{16,0},{24,16},{1,9},{9,25},{17,1},{25,17},{2,10},{10... | collective-permute-start | bytes 1572872 | tf_op jit(solution)/shard_map/ppermute | solution.py:243
  32.0 17.9 %collective-permute-start.7 = (bf16[2,512,256]{2,1,0:T(8,128)(2,1)S(1)}, bf16[2,512,256]{2,1,0:T(8,128)(2,1)S(1)}, u32[]{:S(2)}, u32[]{:S(2)}) collective-permute-start(bf16[2,512,256]{2,1,0:T(8,128)(2,1)S(1)} %collective-permute-done.6.here_ref), channel_id=1, source_target_pairs={{0,8},{8,24},{16,0},{24,16},{1,9},{9,25},{17,1},{25,17},{2,10},{10... | collective-permute-start | bytes 1572872 | tf_op jit(solution)/shard_map/ppermute | solution.py:243
  44.1 13.3 %collective-permute-start.8 = (bf16[4,2,128,256]{3,2,1,0:T(8,128)(2,1)S(1)}, bf16[4,2,128,256]{3,2,1,0:T(8,128)(2,1)S(1)}, u32[]{:S(2)}, u32[]{:S(2)}) collective-permute-start(bf16[4,2,128,256]{3,2,1,0:T(8,128)(2,1)S(1)} %get-tuple-element.66), channel_id=1, source_target_pairs={{0,2},{1,3},{2,0},{3,1},{4,6},{5,7},{6,4},{7,5},{8,10},{9,11},{10,... | collective-permute-start | bytes 1572872 | tf_op jit(solution)/shard_map/ppermute | solution.py:197
  44.2 15.1 %collective-permute-start.5 = (bf16[4,2,128,256]{3,2,1,0:T(8,128)(2,1)S(1)}, bf16[4,2,128,256]{3,2,1,0:T(8,128)(2,1)S(1)}, u32[]{:S(2)}, u32[]{:S(2)}) collective-permute-start(bf16[4,2,128,256]{3,2,1,0:T(8,128)(2,1)S(1)} %get-tuple-element.57), channel_id=1, source_target_pairs={{0,1},{1,0},{2,3},{3,2},{4,5},{5,4},{6,7},{7,6},{8,9},{9,8},{10,11... | collective-permute-start | bytes 1572872 | tf_op jit(solution)/shard_map/ppermute | solution.py:197
  52.8 31.3 %collective-permute-start.13 = (bf16[4,2,128,256]{3,2,1,0:T(8,128)(2,1)S(1)}, bf16[4,2,128,256]{3,2,1,0:T(8,128)(2,1)S(1)}, u32[]{:S(2)}, u32[]{:S(2)}) collective-permute-start(bf16[4,2,128,256]{3,2,1,0:T(8,128)(2,1)S(1)} %get-tuple-element.81), channel_id=1, source_target_pairs={{0,4},{1,5},{2,6},{3,7},{4,0},{5,1},{6,2},{7,3},{8,12},{9,13},{10,... | collective-permute-start | bytes 1572872 | tf_op jit(solution)/shard_map/ppermute | solution.py:197
  57.4 26.7 %collective-permute-start.12 = (bf16[4,2,128,256]{3,2,1,0:T(8,128)(2,1)S(1)}, bf16[4,2,128,256]{3,2,1,0:T(8,128)(2,1)S(1)}, u32[]{:S(2)}, u32[]{:S(2)}) collective-permute-start(bf16[4,2,128,256]{3,2,1,0:T(8,128)(2,1)S(1)} %get-tuple-element.63), channel_id=1, source_target_pairs={{0,1},{1,0},{2,3},{3,2},{4,5},{5,4},{6,7},{7,6},{8,9},{9,8},{10,11... | collective-permute-start | bytes 1572872 | tf_op jit(solution)/shard_map/ppermute | solution.py:197
  59.5 16.1 %collective-permute-start.10 = (bf16[2,2,128,256]{3,2,1,0:T(8,128)(2,1)S(1)}, bf16[2,2,128,256]{3,2,1,0:T(8,128)(2,1)S(1)}, u32[]{:S(2)}, u32[]{:S(2)}) collective-permute-start(bf16[2,2,128,256]{3,2,1,0:T(8,128)(2,1)S(1)} %get-tuple-element.75), channel_id=1, source_target_pairs={{0,1},{1,0},{2,3},{3,2},{4,5},{5,4},{6,7},{7,6},{8,9},{9,8},{10,11... | collective-permute-start | bytes 786440 | tf_op jit(solution)/shard_map/ppermute | solution.py:197
  65.7 18.2 %collective-permute-start.9 = (bf16[2,2,128,256]{3,2,1,0:T(8,128)(2,1)S(1)}, bf16[2,2,128,256]{3,2,1,0:T(8,128)(2,1)S(1)}, u32[]{:S(2)}, u32[]{:S(2)}) collective-permute-start(bf16[2,2,128,256]{3,2,1,0:T(8,128)(2,1)S(1)} %get-tuple-element.69), channel_id=1, source_target_pairs={{0,2},{1,3},{2,0},{3,1},{4,6},{5,7},{6,4},{7,5},{8,10},{9,11},{10,... | collective-permute-start | bytes 786440 | tf_op jit(solution)/shard_map/ppermute | solution.py:197
  84.0 13.8 %collective-permute-start.11 = (bf16[2,2,128,256]{3,2,1,0:T(8,128)(2,1)S(1)}, bf16[2,2,128,256]{3,2,1,0:T(8,128)(2,1)S(1)}, u32[]{:S(2)}, u32[]{:S(2)}) collective-permute-start(bf16[2,2,128,256]{3,2,1,0:T(8,128)(2,1)S(1)} %get-tuple-element.78), channel_id=1, source_target_pairs={{0,4},{1,5},{2,6},{3,7},{4,0},{5,1},{6,2},{7,3},{8,12},{9,13},{10,... | collective-permute-start | bytes 786440 | tf_op jit(solution)/shard_map/ppermute | solution.py:197
  84.3 13.6 %collective-permute-start.14 = (bf16[2,2,128,256]{3,2,1,0:T(8,128)(2,1)S(1)}, bf16[2,2,128,256]{3,2,1,0:T(8,128)(2,1)S(1)}, u32[]{:S(2)}, u32[]{:S(2)}) collective-permute-start(bf16[2,2,128,256]{3,2,1,0:T(8,128)(2,1)S(1)} %get-tuple-element.83), channel_id=1, source_target_pairs={{0,2},{1,3},{2,0},{3,1},{4,6},{5,7},{6,4},{7,5},{8,10},{9,11},{10,... | collective-permute-start | bytes 786440 | tf_op jit(solution)/shard_map/ppermute | solution.py:197
  84.4 13.5 %collective-permute-start.15 = (bf16[2,2,128,256]{3,2,1,0:T(8,128)(2,1)S(1)}, bf16[2,2,128,256]{3,2,1,0:T(8,128)(2,1)S(1)}, u32[]{:S(2)}, u32[]{:S(2)}) collective-permute-start(bf16[2,2,128,256]{3,2,1,0:T(8,128)(2,1)S(1)} %get-tuple-element.86), channel_id=1, source_target_pairs={{0,1},{1,0},{2,3},{3,2},{4,5},{5,4},{6,7},{7,6},{8,9},{9,8},{10,11... | collective-permute-start | bytes 786440 | tf_op jit(solution)/shard_map/ppermute | solution.py:197
  98.0 7.0 %collective-permute-start.16 = (bf16[1,2,128,256]{3,2,1,0:T(8,128)(2,1)S(1)}, bf16[1,2,128,256]{3,2,1,0:T(8,128)(2,1)S(1)}, u32[]{:S(2)}, u32[]{:S(2)}) collective-permute-start(bf16[1,2,128,256]{3,2,1,0:T(8,128)(2,1)S(1)} %get-tuple-element.89), channel_id=1, source_target_pairs={{0,4},{1,5},{2,6},{3,7},{4,0},{5,1},{6,2},{7,3},{8,12},{9,13},{10,... | collective-permute-start | bytes 393224 | tf_op jit(solution)/shard_map/ppermute | solution.py:197
  98.1 6.9 %collective-permute-start.17 = (bf16[1,2,128,256]{3,2,1,0:T(8,128)(2,1)S(1)}, bf16[1,2,128,256]{3,2,1,0:T(8,128)(2,1)S(1)}, u32[]{:S(2)}, u32[]{:S(2)}) collective-permute-start(bf16[1,2,128,256]{3,2,1,0:T(8,128)(2,1)S(1)} %get-tuple-element.91), channel_id=1, source_target_pairs={{0,2},{1,3},{2,0},{3,1},{4,6},{5,7},{6,4},{7,5},{8,10},{9,11},{10,... | collective-permute-start | bytes 393224 | tf_op jit(solution)/shard_map/ppermute | solution.py:197
  98.2 8.8 %collective-permute-start.18 = (bf16[2,128,256]{2,1,0:T(8,128)(2,1)S(1)}, bf16[2,128,256]{2,1,0:T(8,128)(2,1)S(1)}, u32[]{:S(2)}, u32[]{:S(2)}) collective-permute-start(bf16[2,128,256]{2,1,0:T(8,128)(2,1)S(1)} %get-tuple-element.93), channel_id=1, source_target_pairs={{0,8},{8,0},{16,24},{24,16},{1,9},{9,1},{17,25},{25,17},{2,10},{10... | collective-permute-start | bytes 393224 | tf_op jit(solution)/shard_map/ppermute | solution.py:290
  105.1 2.9 %collective-permute-start.19 = (bf16[2,128,256]{2,1,0:T(8,128)(2,1)S(1)}, bf16[2,128,256]{2,1,0:T(8,128)(2,1)S(1)}, u32[]{:S(2)}, u32[]{:S(2)}) collective-permute-start(bf16[2,128,256]{2,1,0:T(8,128)(2,1)S(1)} %get-tuple-element.94), channel_id=1, source_target_pairs={{0,8},{8,0},{16,24},{24,16},{1,9},{9,1},{17,25},{25,17},{2,10},{10... | collective-permute-start | bytes 393224 | tf_op jit(solution)/shard_map/ppermute | solution.py:302

commit v5 on v4

--- a/solution.py
+++ b/solution.py
@@ -10,7 +10,6 @@
 WAVES = 2
 VMEM_BYTES = 48 * 1024 * 1024
 VMEM = pl.BlockSpec(memory_space=pltpu.VMEM)
-SMEM = pl.BlockSpec(memory_space=pltpu.SMEM)
 PARAMS = pltpu.CompilerParams(vmem_limit_bytes=VMEM_BYTES)
 
 
@@ -22,20 +21,34 @@
     return list(range(count.bit_length() - 1))
 
 
-def layout_kernel(x_count, raw_ref, occupancy_ref, exponent_ref, *refs):
-    piece_refs, left_ref, factor_ref = refs[:-2], refs[-2], refs[-1]
-    tiles = []
+def layout_kernel(x_count, raw_hbm, occupancy_hbm, exponent_hbm, *refs):
+    count = WAVES * x_count
+    piece_refs, left_ref = refs[:count], refs[count]
+    raw_ref, occupancy_ref, exponent_ref, factor_ref, small, large = refs[count + 1 :]
+    _, share, width = piece_refs[0].shape
+    occupancy_copy = pltpu.make_async_copy(occupancy_hbm, occupancy_ref, small.at[0])
+    exponent_copy = pltpu.make_async_copy(exponent_hbm, exponent_ref, small.at[1])
+    copies = []
     for tile in range(x_count):
+        rows = pl.ds(tile * share, share)
+        copies.append(pltpu.make_async_copy(raw_hbm.at[:, rows], raw_ref.at[:, rows], large.at[tile]))
+    occupancy_copy.start()
+    exponent_copy.start()
+    for copy in copies:
+        copy.start()
+    occupancy_copy.wait()
+    exponent_copy.wait()
+    for tile, copy in enumerate(copies):
         row = occupancy_ref[tile : tile + 1, :].astype(jnp.float32)
-        power = jnp.exp2(jnp.full(row.shape, exponent_ref[0, tile], jnp.int32).astype(jnp.float32))
-        tiles.append((row * power).astype(jnp.bfloat16))
-        factor_ref[tile] = tiles[tile].astype(jnp.float32)
-    _, share, width = piece_refs[0].shape
-    for index, out_ref in enumerate(piece_refs):
-        wave, tile = divmod(index, x_count)
-        columns = slice(wave * width, (wave + 1) * width)
-        for part in range(2):
-            out_ref[part] = raw_ref[part, tile * share : (tile + 1) * share, columns] * tiles[tile][:, columns]
+        power = jnp.exp2(jnp.broadcast_to(exponent_ref[:, tile : tile + 1], row.shape).astype(jnp.float32))
+        factor = (row * power).astype(jnp.bfloat16)
+        factor_ref[tile] = factor.astype(jnp.float32)
+        copy.wait()
+        for wave in range(WAVES):
+            columns = slice(wave * width, (wave + 1) * width)
+            for part in range(2):
+                value = raw_ref[part, tile * share : (tile + 1) * share, columns]
+                piece_refs[wave * x_count + tile][part] = value * factor[:, columns]
     col, col_count = lax.axis_index("col"), lax.axis_size("col")
     depth = raw_ref.shape[2]
     rows = raw_ref.shape[1] // col_count
@@ -56,12 +69,39 @@
     out = pl.pallas_call(
         functools.partial(layout_kernel, x_count),
         out_shape=[piece] * count + [left],
-        in_specs=[VMEM, VMEM, SMEM],
+        in_specs=[pl.BlockSpec(memory_space=pl.ANY)] * 3,
         out_specs=[VMEM] * (count + 1),
-        scratch_shapes=[pltpu.VMEM((x_count, 1, depth), jnp.float32)],
+        scratch_shapes=[
+            pltpu.VMEM(raw_blocks.shape, jnp.bfloat16),
+            pltpu.VMEM(occupancy.shape, jnp.int32),
+            pltpu.VMEM(exponent.shape[::-1], jnp.int32),
+            pltpu.VMEM((x_count, 1, depth), jnp.float32),
+            pltpu.SemaphoreType.DMA((2,)),
+            pltpu.SemaphoreType.DMA((x_count,)),
+        ],
         compiler_params=PARAMS,
     )(raw_blocks, occupancy, exponent.T)
     return out[:count], out[count]
+
+
+def pick_kernel(*refs):
+    options, out_ref = refs[:-1], refs[-1]
+    x = lax.axis_index("col") % len(options)
+    for place, option_ref in enumerate(options):
+
+        @pl.when(x == place)
+        def _(option_ref=option_ref):
+            out_ref[...] = option_ref[...]
+
+
+def pick(options):
+    return pl.pallas_call(
+        pick_kernel,
+        out_shape=jax.ShapeDtypeStruct(options[0].shape, options[0].dtype),
+        in_specs=[VMEM] * len(options),
+        out_specs=VMEM,
+        compiler_params=PARAMS,
+    )(*options)
 
 
 def halves(blocks, bit):
@@ -255,7 +295,6 @@
 
     def on_device(raw_blocks, occupancy, exponent):
         my_col = lax.axis_index("col")
-        x = my_col % x_count
         pieces, left = lay_out(raw_blocks, occupancy, exponent, x_count)
 
         straight = [lax.ppermute(pieces[h], ("row", "col"), straight_pairs(h)) for h in range(x_count)]
@@ -263,10 +302,7 @@
         for h in range(1, x_count):
             got = lax.ppermute(pieces[x_count + h], ("row", "col"), hop_pairs(h))
             second = jnp.where(my_col % half_cols == h, got, second)
-        straight = [after(got, second) for got in straight]
-        first = straight[0]
-        for h in range(1, x_count):
-            first = jnp.where(x == h, straight[h], first)
+        first = pick([after(got, second) for got in straight])
         theirs = lax.ppermute(left, "row", swap_core)
 
         second = lax.ppermute(second, ("row", "col"), spread_pairs())

time: 109 us -> 110 us (level)
  waiting for transfers between devices: 58.3 us -> 62.9 us
  starting transfers between devices: 30.7 us -> 27.7 us
  other arithmetic: 2.2 us -> 1.1 us
    ppermute x2, starting transfers between devices: 10.2 us -> 3.84 us  [to_all_y(): across = lax.ppermute(here, 'row', across_pairs())]
    ppermute x1, waiting for transfers between devices: 0.01 us -> 3.41 us  [on_device(): second = lax.ppermute(second, ('row', 'col'), spread_pairs())]
    ppermute x1, waiting for transfers between devices: 16.1 us -> 13.6 us  [on_device(): got = lax.ppermute(pieces[x_count + h], ('row', 'col'), hop_pairs(h))]
    ppermute x2, starting transfers between devices: 1.21 us -> 3.72 us  [on_device(): lax.ppermute(pieces[h], ('row', 'col'), straight_pairs(h))]
    ppermute x2, waiting for transfers between devices: 1.43 us -> 3.7 us  [to_all_y(): across = lax.ppermute(here, 'row', across_pairs())]
    ppermute x11, starting transfers between devices: 14.1 us -> 15.5 us  [exchange(): lax.ppermute(value, 'col', [(c, c ^ 1 << bit) for c in range(col_count)])]
    ppermute x11, waiting for transfers between devices: 35 us -> 36.5 us  [exchange(): lax.ppermute(value, 'col', [(c, c ^ 1 << bit) for c in range(col_count)])]
    select_n x1 -> x0, other arithmetic: 1.1 us -> none  [on_device(): first = jnp.where(x == h, straight[h], first)]
  transfers between devices with their start and end apart: 20 -> 20, of which waited for: 9 -> 10; matrix products, arithmetic and copies ran while one was open for 2% -> 1% of each run, Pallas kernels for 11% -> 11%
where the time goes in v5:
time: 110 us
  waiting for transfers between devices  62.9 us (57%)
  starting transfers between devices  27.7 us (25%)
  Pallas kernels  16 us (15%)
  local copies, waits for them, and re-layouts  2.13 us (2%)
  other arithmetic  1.1 us (1%)
    ppermute x11, waiting for transfers between devices, exchange(): lax.ppermute(value, 'col', [(c, c ^ 1 << bit) for c in range(col_count)])  36.5 us
    ppermute x11, starting transfers between devices, exchange(): lax.ppermute(value, 'col', [(c, c ^ 1 << bit) for c in range(col_count)])  15.5 us
    ppermute x1, waiting for transfers between devices, on_device(): got = lax.ppermute(pieces[x_count + h], ('row', 'col'), hop_pairs(h))  13.6 us
    pallas_call x4, Pallas kernels, products(): pl.pallas_call(functools.partial(product_kernel, orders, index), out_shap...  11.6 us
    ppermute x2, waiting for transfers between devices, on_device(): lax.ppermute(pieces[h], ('row', 'col'), straight_pairs(h))  4.82 us
    ppermute x2, starting transfers between devices, to_all_y(): across = lax.ppermute(here, 'row', across_pairs())  3.84 us
    ppermute x2, starting transfers between devices, on_device(): lax.ppermute(pieces[h], ('row', 'col'), straight_pairs(h))  3.72 us
    ppermute x2, waiting for transfers between devices, to_all_y(): across = lax.ppermute(here, 'row', across_pairs())  3.7 us
  transfers between devices with their start and end apart: 20, of which 10 were waited for; matrix products, arithmetic and copies ran while one was open for 1% of the time, Pallas kernels for 11%

profile of v5, /device:TPU:7, one launch (start us, length us, event | category | flops | bytes accessed | tf_op | source)
XLA Modules:
  0.0 110.0 jit_solution(5210227734747464950)
XLA Ops:
  1.3 2.8 %shard_map.37 = (bf16[2,512,256]{2,1,0:T(8,128)(2,1)}, bf16[2,512,256]{2,1,0:T(8,128)(2,1)}, bf16[2,512,256]{2,1,0:T(8,128)(2,1)S(1)}, bf16[2,512,256]{2,1,0:T(8,128)(2,1)}, bf16[1024,1024]{1,0:T(8,128)(2,1)S(1)}) custom-call(bf16[2,1024,512]{2,1,0:T(8,128)(2,1)} %raw_hbm.1, s32[2,512]{1,0:T(2,128)S(1)} %copy-done.1, s32[1,2]{1,0:T(1,128)S(1)} %bitcast.1), custom_call_target="tpu_custom_call" | custom-call | tf_op jit(solution)/shard_map/pallas_call | solution.py:69
  6.1 3.4 %collective-permute-start.3 = (bf16[2,512,256]{2,1,0:T(8,128)(2,1)}, bf16[2,512,256]{2,1,0:T(8,128)(2,1)S(1)}, u32[]{:S(2)}, u32[]{:S(2)}) collective-permute-start(bf16[2,512,256]{2,1,0:T(8,128)(2,1)} %get-tuple-element.55), channel_id=1, source_target_pairs={{0,17},{4,9},{8,19},{12,11},{16,21},{20,13},{24,23},{28,15},{2,10}... | collective-permute-start | bytes 1572872 | tf_op jit(solution)/shard_map/ppermute | solution.py:300
  9.6 13.6 %collective-permute-done.2 = bf16[2,512,256]{2,1,0:T(8,128)(2,1)} collective-permute-done((bf16[2,512,256]{2,1,0:T(8,128)(2,1)}, bf16[2,512,256]{2,1,0:T(8,128)(2,1)}, u32[]{:S(2)}, u32[]{:S(2)}) %collective-permute-start.2) | collective-permute-done | bytes 524320 | tf_op jit(solution)/shard_map/ppermute | solution.py:303
  23.1 1.1 broadcast_select_fusion
  24.3 4.8 %collective-permute-done.3.refs_1_ = bf16[2,512,256]{2,1,0:T(8,128)(2,1)S(1)} collective-permute-done((bf16[2,512,256]{2,1,0:T(8,128)(2,1)}, bf16[2,512,256]{2,1,0:T(8,128)(2,1)S(1)}, u32[]{:S(2)}, u32[]{:S(2)}) %collective-permute-start.3) | collective-permute-done | bytes 524320 | tf_op jit(solution)/shard_map/ppermute | solution.py:300
  29.2 3.4 %collective-permute-done.6.here_ref = bf16[2,512,256]{2,1,0:T(8,128)(2,1)S(1)} collective-permute-done((bf16[2,512,256]{2,1,0:T(8,128)(2,1)S(1)}, bf16[2,512,256]{2,1,0:T(8,128)(2,1)S(1)}, u32[]{:S(2)}, u32[]{:S(2)}) %collective-permute-start.6) | collective-permute-done | bytes 524320 | tf_op jit(solution)/shard_map/ppermute | solution.py:308
  32.6 3.8 %collective-permute-start.7 = (bf16[2,512,256]{2,1,0:T(8,128)(2,1)S(1)}, bf16[2,512,256]{2,1,0:T(8,128)(2,1)S(1)}, u32[]{:S(2)}, u32[]{:S(2)}) collective-permute-start(bf16[2,512,256]{2,1,0:T(8,128)(2,1)S(1)} %collective-permute-done.6.here_ref), channel_id=1, source_target_pairs={{0,8},{8,24},{16,0},{24,16},{1,9},{9,25},{17,1},{25,17},{2,10},{10... | collective-permute-start | bytes 1572872 | tf_op jit(solution)/shard_map/ppermute | solution.py:283
  36.4 3.7 %collective-permute-done.4.across_ref = bf16[2,512,256]{2,1,0:T(8,128)(2,1)S(1)} collective-permute-done((bf16[2,512,256]{2,1,0:T(8,128)(2,1)S(1)}, bf16[2,512,256]{2,1,0:T(8,128)(2,1)S(1)}, u32[]{:S(2)}, u32[]{:S(2)}) %collective-permute-start.4) | collective-permute-done | bytes 524320 | tf_op jit(solution)/shard_map/ppermute | solution.py:283
  40.1 2.9 %shard_map.39 = (bf16[4,2,128,256]{3,2,1,0:T(8,128)(2,1)S(1)}, bf16[4,2,128,256]{3,2,1,0:T(8,128)(2,1)S(1)}) custom-call(bf16[1024,1024]{1,0:T(8,128)(2,1)S(1)} %get-tuple-element.50.mine_ref, bf16[1024,1024]{1,0:T(8,128)(2,1)} %collective-permute-done.theirs_ref, bf16[2,512,256]{2,1,0:T(8,128)(2,1)S(1)} %shard_map.38.here_ref, ...), custom_call_target="tpu_custom_call" | custom-call | tf_op jit(solution)/shard_map/pallas_call | solution.py:139
  43.1 4.3 %collective-permute-start.5 = (bf16[4,2,128,256]{3,2,1,0:T(8,128)(2,1)S(1)}, bf16[4,2,128,256]{3,2,1,0:T(8,128)(2,1)S(1)}, u32[]{:S(2)}, u32[]{:S(2)}) collective-permute-start(bf16[4,2,128,256]{3,2,1,0:T(8,128)(2,1)S(1)} %get-tuple-element.57), channel_id=1, source_target_pairs={{0,1},{1,0},{2,3},{3,2},{4,5},{5,4},{6,7},{7,6},{8,9},{9,8},{10,11... | collective-permute-start | bytes 1572872 | tf_op jit(solution)/shard_map/ppermute | solution.py:237
  47.4 2.9 %shard_map.40 = (bf16[4,2,128,256]{3,2,1,0:T(8,128)(2,1)S(1)}, bf16[4,2,128,256]{3,2,1,0:T(8,128)(2,1)S(1)}) custom-call(bf16[1024,1024]{1,0:T(8,128)(2,1)S(1)} %get-tuple-element.50.mine_ref, bf16[1024,1024]{1,0:T(8,128)(2,1)} %collective-permute-done.theirs_ref, bf16[2,512,256]{2,1,0:T(8,128)(2,1)S(1)} %shard_map.38.here_ref, ...), custom_call_target="tpu_custom_call" | custom-call | tf_op jit(solution)/shard_map/pallas_call | solution.py:139
  50.4 2.9 %shard_map.41 = (bf16[4,2,128,256]{3,2,1,0:T(8,128)(2,1)S(1)}, bf16[4,2,128,256]{3,2,1,0:T(8,128)(2,1)S(1)}) custom-call(bf16[1024,1024]{1,0:T(8,128)(2,1)S(1)} %get-tuple-element.50.mine_ref, bf16[1024,1024]{1,0:T(8,128)(2,1)} %collective-permute-done.theirs_ref, bf16[2,512,256]{2,1,0:T(8,128)(2,1)S(1)} %collective-permute-done.6.here_ref, ...), custom_call_target="tpu_custom_call" | custom-call | tf_op jit(solution)/shard_map/pallas_call | solution.py:139
  53.3 3.8 %collective-permute-start.13 = (bf16[4,2,128,256]{3,2,1,0:T(8,128)(2,1)S(1)}, bf16[4,2,128,256]{3,2,1,0:T(8,128)(2,1)S(1)}, u32[]{:S(2)}, u32[]{:S(2)}) collective-permute-start(bf16[4,2,128,256]{3,2,1,0:T(8,128)(2,1)S(1)} %get-tuple-element.81), channel_id=1, source_target_pairs={{0,4},{1,5},{2,6},{3,7},{4,0},{5,1},{6,2},{7,3},{8,12},{9,13},{10,... | collective-permute-start | bytes 1572872 | tf_op jit(solution)/shard_map/ppermute | solution.py:237
  57.1 2.7 %collective-permute-done.5.refs_1_ = bf16[4,2,128,256]{3,2,1,0:T(8,128)(2,1)S(1)} collective-permute-done((bf16[4,2,128,256]{3,2,1,0:T(8,128)(2,1)S(1)}, bf16[4,2,128,256]{3,2,1,0:T(8,128)(2,1)S(1)}, u32[]{:S(2)}, u32[]{:S(2)}) %collective-permute-start.5) | collective-permute-done | bytes 524320 | tf_op jit(solution)/shard_map/ppermute | solution.py:237
  60.0 7.0 %collective-permute-start.10 = (bf16[2,2,128,256]{3,2,1,0:T(8,128)(2,1)S(1)}, bf16[2,2,128,256]{3,2,1,0:T(8,128)(2,1)S(1)}, u32[]{:S(2)}, u32[]{:S(2)}) collective-permute-start(bf16[2,2,128,256]{3,2,1,0:T(8,128)(2,1)S(1)} %get-tuple-element.75), channel_id=1, source_target_pairs={{0,1},{1,0},{2,3},{3,2},{4,5},{5,4},{6,7},{7,6},{8,9},{9,8},{10,11... | collective-permute-start | bytes 786440 | tf_op jit(solution)/shard_map/ppermute | solution.py:237
  67.0 2.9 %shard_map.43 = (bf16[4,2,128,256]{3,2,1,0:T(8,128)(2,1)S(1)}, bf16[4,2,128,256]{3,2,1,0:T(8,128)(2,1)S(1)}) custom-call(bf16[1024,1024]{1,0:T(8,128)(2,1)S(1)} %get-tuple-element.50.mine_ref, bf16[1024,1024]{1,0:T(8,128)(2,1)} %collective-permute-done.theirs_ref, bf16[2,512,256]{2,1,0:T(8,128)(2,1)S(1)} %collective-permute-done.6.here_ref, ...), custom_call_target="tpu_custom_call" | custom-call | tf_op jit(solution)/shard_map/pallas_call | solution.py:139
  69.9 5.8 %collective-permute-done.10.refs_3_ = bf16[2,2,128,256]{3,2,1,0:T(8,128)(2,1)S(1)} collective-permute-done((bf16[2,2,128,256]{3,2,1,0:T(8,128)(2,1)S(1)}, bf16[2,2,128,256]{3,2,1,0:T(8,128)(2,1)S(1)}, u32[]{:S(2)}, u32[]{:S(2)}) %collective-permute-start.10) | collective-permute-done | bytes 262176 | tf_op jit(solution)/shard_map/ppermute | solution.py:237
  75.6 9.5 %collective-permute-done.9.refs_1_ = bf16[2,2,128,256]{3,2,1,0:T(8,128)(2,1)S(1)} collective-permute-done((bf16[2,2,128,256]{3,2,1,0:T(8,128)(2,1)S(1)}, bf16[2,2,128,256]{3,2,1,0:T(8,128)(2,1)S(1)}, u32[]{:S(2)}, u32[]{:S(2)}) %collective-permute-start.9) | collective-permute-done | bytes 262176 | tf_op jit(solution)/shard_map/ppermute | solution.py:237
  85.7 13.3 %collective-permute-done.11.refs_1_ = bf16[2,2,128,256]{3,2,1,0:T(8,128)(2,1)S(1)} collective-permute-done((bf16[2,2,128,256]{3,2,1,0:T(8,128)(2,1)S(1)}, bf16[2,2,128,256]{3,2,1,0:T(8,128)(2,1)S(1)}, u32[]{:S(2)}, u32[]{:S(2)}) %collective-permute-start.11) | collective-permute-done | bytes 262176 | tf_op jit(solution)/shard_map/ppermute | solution.py:237
  99.4 1.7 %collective-permute-start.18 = (bf16[2,128,256]{2,1,0:T(8,128)(2,1)S(1)}, bf16[2,128,256]{2,1,0:T(8,128)(2,1)S(1)}, u32[]{:S(2)}, u32[]{:S(2)}) collective-permute-start(bf16[2,128,256]{2,1,0:T(8,128)(2,1)S(1)} %get-tuple-element.93), channel_id=1, source_target_pairs={{0,8},{8,0},{16,24},{24,16},{1,9},{9,1},{17,25},{25,17},{2,10},{10... | collective-permute-start | bytes 393224 | tf_op jit(solution)/shard_map/ppermute | solution.py:326
  101.1 5.2 %collective-permute-done.16.refs_1_ = bf16[1,2,128,256]{3,2,1,0:T(8,128)(2,1)S(1)} collective-permute-done((bf16[1,2,128,256]{3,2,1,0:T(8,128)(2,1)S(1)}, bf16[1,2,128,256]{3,2,1,0:T(8,128)(2,1)S(1)}, u32[]{:S(2)}, u32[]{:S(2)}) %collective-permute-start.16) | collective-permute-done | bytes 131104 | tf_op jit(solution)/shard_map/ppermute | solution.py:237
  106.3 1.9 %collective-permute-start.19 = (bf16[2,128,256]{2,1,0:T(8,128)(2,1)S(1)}, bf16[2,128,256]{2,1,0:T(8,128)(2,1)S(1)}, u32[]{:S(2)}, u32[]{:S(2)}) collective-permute-start(bf16[2,128,256]{2,1,0:T(8,128)(2,1)S(1)} %get-tuple-element.94), channel_id=1, source_target_pairs={{0,8},{8,0},{16,24},{24,16},{1,9},{9,1},{17,25},{25,17},{2,10},{10... | collective-permute-start | bytes 393224 | tf_op jit(solution)/shard_map/ppermute | solution.py:338
  108.2 1.0 collective-permute-done.19.refs_3_
  109.2 0.8 shard_map.49
  (36 shorter events, 4.6 us)
Async XLA Ops:
  0.0 0.7 copy-start.1
  0.7 0.7 copy-start.2
  4.1 0.8 copy-start
  4.9 35.2 %collective-permute-start = (bf16[1024,1024]{1,0:T(8,128)(2,1)S(1)}, bf16[1024,1024]{1,0:T(8,128)(2,1)}, u32[]{:S(2)}, u32[]{:S(2)}) collective-permute-start(bf16[1024,1024]{1,0:T(8,128)(2,1)S(1)} %get-tuple-element.50.mine_ref), channel_id=1, source_target_pairs={{0,8},{8,0},{16,24},{24,16},{1,9},{9,1},{17,25},{25,17},{2,10},{10... | collective-permute-start | bytes 6291464 | tf_op jit(solution)/shard_map/ppermute | solution.py:306
  5.6 17.5 %collective-permute-start.2 = (bf16[2,512,256]{2,1,0:T(8,128)(2,1)}, bf16[2,512,256]{2,1,0:T(8,128)(2,1)}, u32[]{:S(2)}, u32[]{:S(2)}) collective-permute-start(bf16[2,512,256]{2,1,0:T(8,128)(2,1)} %get-tuple-element.52), channel_id=1, source_target_pairs={{0,1},{1,0},{2,10},{3,11},{4,5},{5,4},{6,14},{7,15},{8,9},{9,8},{1... | collective-permute-start | bytes 1572872 | tf_op jit(solution)/shard_map/ppermute | solution.py:303
  5.8 18.5 %collective-permute-start.1 = (bf16[2,512,256]{2,1,0:T(8,128)(2,1)}, bf16[2,512,256]{2,1,0:T(8,128)(2,1)S(1)}, u32[]{:S(2)}, u32[]{:S(2)}) collective-permute-start(bf16[2,512,256]{2,1,0:T(8,128)(2,1)} %get-tuple-element.51), channel_id=1, source_target_pairs={{0,16},{4,8},{8,18},{12,10},{16,20},{20,12},{24,22},{28,14},{1,9},... | collective-permute-start | bytes 1572872 | tf_op jit(solution)/shard_map/ppermute | solution.py:300
  6.1 23.0 %collective-permute-start.3 = (bf16[2,512,256]{2,1,0:T(8,128)(2,1)}, bf16[2,512,256]{2,1,0:T(8,128)(2,1)S(1)}, u32[]{:S(2)}, u32[]{:S(2)}) collective-permute-start(bf16[2,512,256]{2,1,0:T(8,128)(2,1)} %get-tuple-element.55), channel_id=1, source_target_pairs={{0,17},{4,9},{8,19},{12,11},{16,21},{20,13},{24,23},{28,15},{2,10}... | collective-permute-start | bytes 1572872 | tf_op jit(solution)/shard_map/ppermute | solution.py:300
  24.2 8.4 %collective-permute-start.6 = (bf16[2,512,256]{2,1,0:T(8,128)(2,1)S(1)}, bf16[2,512,256]{2,1,0:T(8,128)(2,1)S(1)}, u32[]{:S(2)}, u32[]{:S(2)}) collective-permute-start(bf16[2,512,256]{2,1,0:T(8,128)(2,1)S(1)} %broadcast_select_fusion), channel_id=1, source_target_pairs={{0,16},{1,17},{4,8},{5,9},{8,18},{9,19},{12,10},{13,11},{16,20},{1... | collective-permute-start | bytes 1572872 | tf_op jit(solution)/shard_map/ppermute | solution.py:308
  29.2 11.0 %collective-permute-start.4 = (bf16[2,512,256]{2,1,0:T(8,128)(2,1)S(1)}, bf16[2,512,256]{2,1,0:T(8,128)(2,1)S(1)}, u32[]{:S(2)}, u32[]{:S(2)}) collective-permute-start(bf16[2,512,256]{2,1,0:T(8,128)(2,1)S(1)} %shard_map.38.here_ref), channel_id=1, source_target_pairs={{0,8},{8,24},{16,0},{24,16},{1,9},{9,25},{17,1},{25,17},{2,10},{10... | collective-permute-start | bytes 1572872 | tf_op jit(solution)/shard_map/ppermute | solution.py:283
  32.6 17.7 %collective-permute-start.7 = (bf16[2,512,256]{2,1,0:T(8,128)(2,1)S(1)}, bf16[2,512,256]{2,1,0:T(8,128)(2,1)S(1)}, u32[]{:S(2)}, u32[]{:S(2)}) collective-permute-start(bf16[2,512,256]{2,1,0:T(8,128)(2,1)S(1)} %collective-permute-done.6.here_ref), channel_id=1, source_target_pairs={{0,8},{8,24},{16,0},{24,16},{1,9},{9,25},{17,1},{25,17},{2,10},{10... | collective-permute-start | bytes 1572872 | tf_op jit(solution)/shard_map/ppermute | solution.py:283
  43.1 14.0 %collective-permute-start.8 = (bf16[4,2,128,256]{3,2,1,0:T(8,128)(2,1)S(1)}, bf16[4,2,128,256]{3,2,1,0:T(8,128)(2,1)S(1)}, u32[]{:S(2)}, u32[]{:S(2)}) collective-permute-start(bf16[4,2,128,256]{3,2,1,0:T(8,128)(2,1)S(1)} %get-tuple-element.66), channel_id=1, source_target_pairs={{0,2},{1,3},{2,0},{3,1},{4,6},{5,7},{6,4},{7,5},{8,10},{9,11},{10,... | collective-permute-start | bytes 1572872 | tf_op jit(solution)/shard_map/ppermute | solution.py:237
  43.1 16.6 %collective-permute-start.5 = (bf16[4,2,128,256]{3,2,1,0:T(8,128)(2,1)S(1)}, bf16[4,2,128,256]{3,2,1,0:T(8,128)(2,1)S(1)}, u32[]{:S(2)}, u32[]{:S(2)}) collective-permute-start(bf16[4,2,128,256]{3,2,1,0:T(8,128)(2,1)S(1)} %get-tuple-element.57), channel_id=1, source_target_pairs={{0,1},{1,0},{2,3},{3,2},{4,5},{5,4},{6,7},{7,6},{8,9},{9,8},{10,11... | collective-permute-start | bytes 1572872 | tf_op jit(solution)/shard_map/ppermute | solution.py:237
  53.3 32.0 %collective-permute-start.13 = (bf16[4,2,128,256]{3,2,1,0:T(8,128)(2,1)S(1)}, bf16[4,2,128,256]{3,2,1,0:T(8,128)(2,1)S(1)}, u32[]{:S(2)}, u32[]{:S(2)}) collective-permute-start(bf16[4,2,128,256]{3,2,1,0:T(8,128)(2,1)S(1)} %get-tuple-element.81), channel_id=1, source_target_pairs={{0,4},{1,5},{2,6},{3,7},{4,0},{5,1},{6,2},{7,3},{8,12},{9,13},{10,... | collective-permute-start | bytes 1572872 | tf_op jit(solution)/shard_map/ppermute | solution.py:237
  57.1 28.2 %collective-permute-start.12 = (bf16[4,2,128,256]{3,2,1,0:T(8,128)(2,1)S(1)}, bf16[4,2,128,256]{3,2,1,0:T(8,128)(2,1)S(1)}, u32[]{:S(2)}, u32[]{:S(2)}) collective-permute-start(bf16[4,2,128,256]{3,2,1,0:T(8,128)(2,1)S(1)} %get-tuple-element.63), channel_id=1, source_target_pairs={{0,1},{1,0},{2,3},{3,2},{4,5},{5,4},{6,7},{7,6},{8,9},{9,8},{10,11... | collective-permute-start | bytes 1572872 | tf_op jit(solution)/shard_map/ppermute | solution.py:237
  60.0 15.7 %collective-permute-start.10 = (bf16[2,2,128,256]{3,2,1,0:T(8,128)(2,1)S(1)}, bf16[2,2,128,256]{3,2,1,0:T(8,128)(2,1)S(1)}, u32[]{:S(2)}, u32[]{:S(2)}) collective-permute-start(bf16[2,2,128,256]{3,2,1,0:T(8,128)(2,1)S(1)} %get-tuple-element.75), channel_id=1, source_target_pairs={{0,1},{1,0},{2,3},{3,2},{4,5},{5,4},{6,7},{7,6},{8,9},{9,8},{10,11... | collective-permute-start | bytes 786440 | tf_op jit(solution)/shard_map/ppermute | solution.py:237
  67.0 18.2 %collective-permute-start.9 = (bf16[2,2,128,256]{3,2,1,0:T(8,128)(2,1)S(1)}, bf16[2,2,128,256]{3,2,1,0:T(8,128)(2,1)S(1)}, u32[]{:S(2)}, u32[]{:S(2)}) collective-permute-start(bf16[2,2,128,256]{3,2,1,0:T(8,128)(2,1)S(1)} %get-tuple-element.69), channel_id=1, source_target_pairs={{0,2},{1,3},{2,0},{3,1},{4,6},{5,7},{6,4},{7,5},{8,10},{9,11},{10,... | collective-permute-start | bytes 786440 | tf_op jit(solution)/shard_map/ppermute | solution.py:237
  85.2 13.8 %collective-permute-start.11 = (bf16[2,2,128,256]{3,2,1,0:T(8,128)(2,1)S(1)}, bf16[2,2,128,256]{3,2,1,0:T(8,128)(2,1)S(1)}, u32[]{:S(2)}, u32[]{:S(2)}) collective-permute-start(bf16[2,2,128,256]{3,2,1,0:T(8,128)(2,1)S(1)} %get-tuple-element.78), channel_id=1, source_target_pairs={{0,4},{1,5},{2,6},{3,7},{4,0},{5,1},{6,2},{7,3},{8,12},{9,13},{10,... | collective-permute-start | bytes 786440 | tf_op jit(solution)/shard_map/ppermute | solution.py:237
  85.6 13.6 %collective-permute-start.14 = (bf16[2,2,128,256]{3,2,1,0:T(8,128)(2,1)S(1)}, bf16[2,2,128,256]{3,2,1,0:T(8,128)(2,1)S(1)}, u32[]{:S(2)}, u32[]{:S(2)}) collective-permute-start(bf16[2,2,128,256]{3,2,1,0:T(8,128)(2,1)S(1)} %get-tuple-element.83), channel_id=1, source_target_pairs={{0,2},{1,3},{2,0},{3,1},{4,6},{5,7},{6,4},{7,5},{8,10},{9,11},{10,... | collective-permute-start | bytes 786440 | tf_op jit(solution)/shard_map/ppermute | solution.py:237
  85.6 13.5 %collective-permute-start.15 = (bf16[2,2,128,256]{3,2,1,0:T(8,128)(2,1)S(1)}, bf16[2,2,128,256]{3,2,1,0:T(8,128)(2,1)S(1)}, u32[]{:S(2)}, u32[]{:S(2)}) collective-permute-start(bf16[2,2,128,256]{3,2,1,0:T(8,128)(2,1)S(1)} %get-tuple-element.86), channel_id=1, source_target_pairs={{0,1},{1,0},{2,3},{3,2},{4,5},{5,4},{6,7},{7,6},{8,9},{9,8},{10,11... | collective-permute-start | bytes 786440 | tf_op jit(solution)/shard_map/ppermute | solution.py:237
  99.2 7.0 %collective-permute-start.16 = (bf16[1,2,128,256]{3,2,1,0:T(8,128)(2,1)S(1)}, bf16[1,2,128,256]{3,2,1,0:T(8,128)(2,1)S(1)}, u32[]{:S(2)}, u32[]{:S(2)}) collective-permute-start(bf16[1,2,128,256]{3,2,1,0:T(8,128)(2,1)S(1)} %get-tuple-element.89), channel_id=1, source_target_pairs={{0,4},{1,5},{2,6},{3,7},{4,0},{5,1},{6,2},{7,3},{8,12},{9,13},{10,... | collective-permute-start | bytes 393224 | tf_op jit(solution)/shard_map/ppermute | solution.py:237
  99.3 6.9 %collective-permute-start.17 = (bf16[1,2,128,256]{3,2,1,0:T(8,128)(2,1)S(1)}, bf16[1,2,128,256]{3,2,1,0:T(8,128)(2,1)S(1)}, u32[]{:S(2)}, u32[]{:S(2)}) collective-permute-start(bf16[1,2,128,256]{3,2,1,0:T(8,128)(2,1)S(1)} %get-tuple-element.91), channel_id=1, source_target_pairs={{0,2},{1,3},{2,0},{3,1},{4,6},{5,7},{6,4},{7,5},{8,10},{9,11},{10,... | collective-permute-start | bytes 393224 | tf_op jit(solution)/shard_map/ppermute | solution.py:237
  99.4 8.8 %collective-permute-start.18 = (bf16[2,128,256]{2,1,0:T(8,128)(2,1)S(1)}, bf16[2,128,256]{2,1,0:T(8,128)(2,1)S(1)}, u32[]{:S(2)}, u32[]{:S(2)}) collective-permute-start(bf16[2,128,256]{2,1,0:T(8,128)(2,1)S(1)} %get-tuple-element.93), channel_id=1, source_target_pairs={{0,8},{8,0},{16,24},{24,16},{1,9},{9,1},{17,25},{25,17},{2,10},{10... | collective-permute-start | bytes 393224 | tf_op jit(solution)/shard_map/ppermute | solution.py:326
  106.3 2.9 %collective-permute-start.19 = (bf16[2,128,256]{2,1,0:T(8,128)(2,1)S(1)}, bf16[2,128,256]{2,1,0:T(8,128)(2,1)S(1)}, u32[]{:S(2)}, u32[]{:S(2)}) collective-permute-start(bf16[2,128,256]{2,1,0:T(8,128)(2,1)S(1)} %get-tuple-element.94), channel_id=1, source_target_pairs={{0,8},{8,0},{16,24},{24,16},{1,9},{9,1},{17,25},{25,17},{2,10},{10... | collective-permute-start | bytes 393224 | tf_op jit(solution)/shard_map/ppermute | solution.py:338

commit v6 on v5

--- a/solution.py
+++ b/solution.py
@@ -8,7 +8,7 @@
 from jax.sharding import PartitionSpec as P
 
 WAVES = 2
-VMEM_BYTES = 48 * 1024 * 1024
+VMEM_BYTES = 20 * 1024 * 1024
 VMEM = pl.BlockSpec(memory_space=pltpu.VMEM)
 PARAMS = pltpu.CompilerParams(vmem_limit_bytes=VMEM_BYTES)
 
@@ -69,7 +69,7 @@
     out = pl.pallas_call(
         functools.partial(layout_kernel, x_count),
         out_shape=[piece] * count + [left],
-        in_specs=[pl.BlockSpec(memory_space=pl.ANY)] * 3,
+        in_specs=[pl.BlockSpec(memory_space=pltpu.HBM)] * 3,
         out_specs=[VMEM] * (count + 1),
         scratch_shapes=[
             pltpu.VMEM(raw_blocks.shape, jnp.bfloat16),

time: 110 us -> 111 us (level)
  local copies, waits for them, and re-layouts: 2.13 us -> 3.72 us
  Pallas kernels: 16 us -> 14.8 us
    unnamed x6 -> x8, local copies, waits for them, and re-layouts: 2.13 us -> 3.72 us
    pallas_call x1, Pallas kernels: 2.76 us -> 1.54 us  [lay_out(): pl.pallas_call(functools.partial(layout_kernel, x_count), out_shape=[piec...]
where the time goes in v6:
time: 111 us; the launch traced here: 110 us
  waiting for transfers between devices  63 us (57%)
  starting transfers between devices  27.7 us (25%)
  Pallas kernels  14.8 us (13%)
  local copies, waits for them, and re-layouts  3.72 us (3%)
    ppermute x11, waiting for transfers between devices, exchange(): lax.ppermute(value, 'col', [(c, c ^ 1 << bit) for c in range(col_count)])  36.5 us
    ppermute x11, starting transfers between devices, exchange(): lax.ppermute(value, 'col', [(c, c ^ 1 << bit) for c in range(col_count)])  15.5 us
    ppermute x1, waiting for transfers between devices, on_device(): got = lax.ppermute(pieces[x_count + h], ('row', 'col'), hop_pairs(h))  13.6 us
    pallas_call x4, Pallas kernels, products(): pl.pallas_call(functools.partial(product_kernel, orders, index), out_shap...  11.6 us
    ppermute x2, waiting for transfers between devices, on_device(): lax.ppermute(pieces[h], ('row', 'col'), straight_pairs(h))  4.82 us
    ppermute x2, starting transfers between devices, to_all_y(): across = lax.ppermute(here, 'row', across_pairs())  3.84 us
    unnamed x8, local copies, waits for them, and re-layouts  3.72 us
    ppermute x2, starting transfers between devices, on_device(): lax.ppermute(pieces[h], ('row', 'col'), straight_pairs(h))  3.72 us
  transfers between devices with their start and end apart: 20, of which 10 were waited for; matrix products, arithmetic and copies ran while one was open for 1% of the time, Pallas kernels for 11%

profile of v6, /device:TPU:7, one launch (start us, length us, event | category | flops | bytes accessed | tf_op | source)
XLA Modules:
  0.0 110.4 jit_solution(10002222390515268956)
XLA Ops:
  0.0 1.6 %copy-done = bf16[2,1024,512]{2,1,0:T(8,128)(2,1)S(1)} copy-done((bf16[2,1024,512]{2,1,0:T(8,128)(2,1)S(1)}, bf16[2,1024,512]{2,1,0:T(8,128)(2,1)}, u32[]{:S(2)}) %copy-start) | copy-done | bytes 2097176
  2.9 1.5 %shard_map.37 = (bf16[2,512,256]{2,1,0:T(8,128)(2,1)}, bf16[2,512,256]{2,1,0:T(8,128)(2,1)}, bf16[2,512,256]{2,1,0:T(8,128)(2,1)S(1)}, bf16[2,512,256]{2,1,0:T(8,128)(2,1)}, bf16[1024,1024]{1,0:T(8,128)(2,1)S(1)}) custom-call(bf16[2,1024,512]{2,1,0:T(8,128)(2,1)S(1)} %copy-done, s32[2,512]{1,0:T(2,128)S(1)} %copy-done.2, s32[1,2]{1,0:T(1,128)S(1)} %bitcast.1), custom_call_target="tpu_custom_call" | custom-call | tf_op jit(solution)/shard_map/pallas_call | solution.py:69
  6.5 3.4 %collective-permute-start.3 = (bf16[2,512,256]{2,1,0:T(8,128)(2,1)}, bf16[2,512,256]{2,1,0:T(8,128)(2,1)S(1)}, u32[]{:S(2)}, u32[]{:S(2)}) collective-permute-start(bf16[2,512,256]{2,1,0:T(8,128)(2,1)} %get-tuple-element.55), channel_id=1, source_target_pairs={{0,17},{4,9},{8,19},{12,11},{16,21},{20,13},{24,23},{28,15},{2,10}... | collective-permute-start | bytes 1572872 | tf_op jit(solution)/shard_map/ppermute | solution.py:300
  9.9 13.6 %collective-permute-done.2 = bf16[2,512,256]{2,1,0:T(8,128)(2,1)} collective-permute-done((bf16[2,512,256]{2,1,0:T(8,128)(2,1)}, bf16[2,512,256]{2,1,0:T(8,128)(2,1)}, u32[]{:S(2)}, u32[]{:S(2)}) %collective-permute-start.2) | collective-permute-done | bytes 524320 | tf_op jit(solution)/shard_map/ppermute | solution.py:303
  23.5 1.1 broadcast_select_fusion
  24.7 4.8 %collective-permute-done.3.refs_1_ = bf16[2,512,256]{2,1,0:T(8,128)(2,1)S(1)} collective-permute-done((bf16[2,512,256]{2,1,0:T(8,128)(2,1)}, bf16[2,512,256]{2,1,0:T(8,128)(2,1)S(1)}, u32[]{:S(2)}, u32[]{:S(2)}) %collective-permute-start.3) | collective-permute-done | bytes 524320 | tf_op jit(solution)/shard_map/ppermute | solution.py:300
  29.6 3.4 %collective-permute-done.6.here_ref = bf16[2,512,256]{2,1,0:T(8,128)(2,1)S(1)} collective-permute-done((bf16[2,512,256]{2,1,0:T(8,128)(2,1)S(1)}, bf16[2,512,256]{2,1,0:T(8,128)(2,1)S(1)}, u32[]{:S(2)}, u32[]{:S(2)}) %collective-permute-start.6) | collective-permute-done | bytes 524320 | tf_op jit(solution)/shard_map/ppermute | solution.py:308
  33.0 3.8 %collective-permute-start.7 = (bf16[2,512,256]{2,1,0:T(8,128)(2,1)S(1)}, bf16[2,512,256]{2,1,0:T(8,128)(2,1)S(1)}, u32[]{:S(2)}, u32[]{:S(2)}) collective-permute-start(bf16[2,512,256]{2,1,0:T(8,128)(2,1)S(1)} %collective-permute-done.6.here_ref), channel_id=1, source_target_pairs={{0,8},{8,24},{16,0},{24,16},{1,9},{9,25},{17,1},{25,17},{2,10},{10... | collective-permute-start | bytes 1572872 | tf_op jit(solution)/shard_map/ppermute | solution.py:283
  36.8 3.7 %collective-permute-done.4.across_ref = bf16[2,512,256]{2,1,0:T(8,128)(2,1)S(1)} collective-permute-done((bf16[2,512,256]{2,1,0:T(8,128)(2,1)S(1)}, bf16[2,512,256]{2,1,0:T(8,128)(2,1)S(1)}, u32[]{:S(2)}, u32[]{:S(2)}) %collective-permute-start.4) | collective-permute-done | bytes 524320 | tf_op jit(solution)/shard_map/ppermute | solution.py:283
  40.5 2.9 %shard_map.39 = (bf16[4,2,128,256]{3,2,1,0:T(8,128)(2,1)S(1)}, bf16[4,2,128,256]{3,2,1,0:T(8,128)(2,1)S(1)}) custom-call(bf16[1024,1024]{1,0:T(8,128)(2,1)S(1)} %get-tuple-element.50.mine_ref, bf16[1024,1024]{1,0:T(8,128)(2,1)} %collective-permute-done.theirs_ref, bf16[2,512,256]{2,1,0:T(8,128)(2,1)S(1)} %shard_map.38.here_ref, ...), custom_call_target="tpu_custom_call" | custom-call | tf_op jit(solution)/shard_map/pallas_call | solution.py:139
  43.5 4.3 %collective-permute-start.5 = (bf16[4,2,128,256]{3,2,1,0:T(8,128)(2,1)S(1)}, bf16[4,2,128,256]{3,2,1,0:T(8,128)(2,1)S(1)}, u32[]{:S(2)}, u32[]{:S(2)}) collective-permute-start(bf16[4,2,128,256]{3,2,1,0:T(8,128)(2,1)S(1)} %get-tuple-element.57), channel_id=1, source_target_pairs={{0,1},{1,0},{2,3},{3,2},{4,5},{5,4},{6,7},{7,6},{8,9},{9,8},{10,11... | collective-permute-start | bytes 1572872 | tf_op jit(solution)/shard_map/ppermute | solution.py:237
  47.8 2.9 %shard_map.40 = (bf16[4,2,128,256]{3,2,1,0:T(8,128)(2,1)S(1)}, bf16[4,2,128,256]{3,2,1,0:T(8,128)(2,1)S(1)}) custom-call(bf16[1024,1024]{1,0:T(8,128)(2,1)S(1)} %get-tuple-element.50.mine_ref, bf16[1024,1024]{1,0:T(8,128)(2,1)} %collective-permute-done.theirs_ref, bf16[2,512,256]{2,1,0:T(8,128)(2,1)S(1)} %shard_map.38.here_ref, ...), custom_call_target="tpu_custom_call" | custom-call | tf_op jit(solution)/shard_map/pallas_call | solution.py:139
  50.7 2.9 %shard_map.41 = (bf16[4,2,128,256]{3,2,1,0:T(8,128)(2,1)S(1)}, bf16[4,2,128,256]{3,2,1,0:T(8,128)(2,1)S(1)}) custom-call(bf16[1024,1024]{1,0:T(8,128)(2,1)S(1)} %get-tuple-element.50.mine_ref, bf16[1024,1024]{1,0:T(8,128)(2,1)} %collective-permute-done.theirs_ref, bf16[2,512,256]{2,1,0:T(8,128)(2,1)S(1)} %collective-permute-done.6.here_ref, ...), custom_call_target="tpu_custom_call" | custom-call | tf_op jit(solution)/shard_map/pallas_call | solution.py:139
  53.7 3.8 %collective-permute-start.13 = (bf16[4,2,128,256]{3,2,1,0:T(8,128)(2,1)S(1)}, bf16[4,2,128,256]{3,2,1,0:T(8,128)(2,1)S(1)}, u32[]{:S(2)}, u32[]{:S(2)}) collective-permute-start(bf16[4,2,128,256]{3,2,1,0:T(8,128)(2,1)S(1)} %get-tuple-element.81), channel_id=1, source_target_pairs={{0,4},{1,5},{2,6},{3,7},{4,0},{5,1},{6,2},{7,3},{8,12},{9,13},{10,... | collective-permute-start | bytes 1572872 | tf_op jit(solution)/shard_map/ppermute | solution.py:237
  57.5 2.7 %collective-permute-done.5.refs_1_ = bf16[4,2,128,256]{3,2,1,0:T(8,128)(2,1)S(1)} collective-permute-done((bf16[4,2,128,256]{3,2,1,0:T(8,128)(2,1)S(1)}, bf16[4,2,128,256]{3,2,1,0:T(8,128)(2,1)S(1)}, u32[]{:S(2)}, u32[]{:S(2)}) %collective-permute-start.5) | collective-permute-done | bytes 524320 | tf_op jit(solution)/shard_map/ppermute | solution.py:237
  60.3 7.0 %collective-permute-start.10 = (bf16[2,2,128,256]{3,2,1,0:T(8,128)(2,1)S(1)}, bf16[2,2,128,256]{3,2,1,0:T(8,128)(2,1)S(1)}, u32[]{:S(2)}, u32[]{:S(2)}) collective-permute-start(bf16[2,2,128,256]{3,2,1,0:T(8,128)(2,1)S(1)} %get-tuple-element.75), channel_id=1, source_target_pairs={{0,1},{1,0},{2,3},{3,2},{4,5},{5,4},{6,7},{7,6},{8,9},{9,8},{10,11... | collective-permute-start | bytes 786440 | tf_op jit(solution)/shard_map/ppermute | solution.py:237
  67.4 2.9 %shard_map.43 = (bf16[4,2,128,256]{3,2,1,0:T(8,128)(2,1)S(1)}, bf16[4,2,128,256]{3,2,1,0:T(8,128)(2,1)S(1)}) custom-call(bf16[1024,1024]{1,0:T(8,128)(2,1)S(1)} %get-tuple-element.50.mine_ref, bf16[1024,1024]{1,0:T(8,128)(2,1)} %collective-permute-done.theirs_ref, bf16[2,512,256]{2,1,0:T(8,128)(2,1)S(1)} %collective-permute-done.6.here_ref, ...), custom_call_target="tpu_custom_call" | custom-call | tf_op jit(solution)/shard_map/pallas_call | solution.py:139
  70.3 5.8 %collective-permute-done.10.refs_3_ = bf16[2,2,128,256]{3,2,1,0:T(8,128)(2,1)S(1)} collective-permute-done((bf16[2,2,128,256]{3,2,1,0:T(8,128)(2,1)S(1)}, bf16[2,2,128,256]{3,2,1,0:T(8,128)(2,1)S(1)}, u32[]{:S(2)}, u32[]{:S(2)}) %collective-permute-start.10) | collective-permute-done | bytes 262176 | tf_op jit(solution)/shard_map/ppermute | solution.py:237
  76.0 9.5 %collective-permute-done.9.refs_1_ = bf16[2,2,128,256]{3,2,1,0:T(8,128)(2,1)S(1)} collective-permute-done((bf16[2,2,128,256]{3,2,1,0:T(8,128)(2,1)S(1)}, bf16[2,2,128,256]{3,2,1,0:T(8,128)(2,1)S(1)}, u32[]{:S(2)}, u32[]{:S(2)}) %collective-permute-start.9) | collective-permute-done | bytes 262176 | tf_op jit(solution)/shard_map/ppermute | solution.py:237
  86.1 13.3 %collective-permute-done.11.refs_1_ = bf16[2,2,128,256]{3,2,1,0:T(8,128)(2,1)S(1)} collective-permute-done((bf16[2,2,128,256]{3,2,1,0:T(8,128)(2,1)S(1)}, bf16[2,2,128,256]{3,2,1,0:T(8,128)(2,1)S(1)}, u32[]{:S(2)}, u32[]{:S(2)}) %collective-permute-start.11) | collective-permute-done | bytes 262176 | tf_op jit(solution)/shard_map/ppermute | solution.py:237
  99.8 1.7 %collective-permute-start.18 = (bf16[2,128,256]{2,1,0:T(8,128)(2,1)S(1)}, bf16[2,128,256]{2,1,0:T(8,128)(2,1)S(1)}, u32[]{:S(2)}, u32[]{:S(2)}) collective-permute-start(bf16[2,128,256]{2,1,0:T(8,128)(2,1)S(1)} %get-tuple-element.93), channel_id=1, source_target_pairs={{0,8},{8,0},{16,24},{24,16},{1,9},{9,1},{17,25},{25,17},{2,10},{10... | collective-permute-start | bytes 393224 | tf_op jit(solution)/shard_map/ppermute | solution.py:326
  101.4 5.2 %collective-permute-done.16.refs_1_ = bf16[1,2,128,256]{3,2,1,0:T(8,128)(2,1)S(1)} collective-permute-done((bf16[1,2,128,256]{3,2,1,0:T(8,128)(2,1)S(1)}, bf16[1,2,128,256]{3,2,1,0:T(8,128)(2,1)S(1)}, u32[]{:S(2)}, u32[]{:S(2)}) %collective-permute-start.16) | collective-permute-done | bytes 131104 | tf_op jit(solution)/shard_map/ppermute | solution.py:237
  106.7 1.9 %collective-permute-start.19 = (bf16[2,128,256]{2,1,0:T(8,128)(2,1)S(1)}, bf16[2,128,256]{2,1,0:T(8,128)(2,1)S(1)}, u32[]{:S(2)}, u32[]{:S(2)}) collective-permute-start(bf16[2,128,256]{2,1,0:T(8,128)(2,1)S(1)} %get-tuple-element.94), channel_id=1, source_target_pairs={{0,8},{8,0},{16,24},{24,16},{1,9},{9,1},{17,25},{25,17},{2,10},{10... | collective-permute-start | bytes 393224 | tf_op jit(solution)/shard_map/ppermute | solution.py:338
  108.6 1.0 collective-permute-done.19.refs_3_
  (38 shorter events, 5.5 us)
Async XLA Ops:
  0.0 1.6 %copy-start = (bf16[2,1024,512]{2,1,0:T(8,128)(2,1)S(1)}, bf16[2,1024,512]{2,1,0:T(8,128)(2,1)}, u32[]{:S(2)}) copy-start(bf16[2,1024,512]{2,1,0:T(8,128)(2,1)} %raw_hbm.1) | copy-start | bytes 6291460
  1.6 0.7 copy-start.2
  2.3 0.7 copy-start.3
  4.5 0.8 copy-start.1
  5.3 35.2 %collective-permute-start = (bf16[1024,1024]{1,0:T(8,128)(2,1)S(1)}, bf16[1024,1024]{1,0:T(8,128)(2,1)}, u32[]{:S(2)}, u32[]{:S(2)}) collective-permute-start(bf16[1024,1024]{1,0:T(8,128)(2,1)S(1)} %get-tuple-element.50.mine_ref), channel_id=1, source_target_pairs={{0,8},{8,0},{16,24},{24,16},{1,9},{9,1},{17,25},{25,17},{2,10},{10... | collective-permute-start | bytes 6291464 | tf_op jit(solution)/shard_map/ppermute | solution.py:306
  6.0 17.5 %collective-permute-start.2 = (bf16[2,512,256]{2,1,0:T(8,128)(2,1)}, bf16[2,512,256]{2,1,0:T(8,128)(2,1)}, u32[]{:S(2)}, u32[]{:S(2)}) collective-permute-start(bf16[2,512,256]{2,1,0:T(8,128)(2,1)} %get-tuple-element.52), channel_id=1, source_target_pairs={{0,1},{1,0},{2,10},{3,11},{4,5},{5,4},{6,14},{7,15},{8,9},{9,8},{1... | collective-permute-start | bytes 1572872 | tf_op jit(solution)/shard_map/ppermute | solution.py:303
  6.2 18.5 %collective-permute-start.1 = (bf16[2,512,256]{2,1,0:T(8,128)(2,1)}, bf16[2,512,256]{2,1,0:T(8,128)(2,1)S(1)}, u32[]{:S(2)}, u32[]{:S(2)}) collective-permute-start(bf16[2,512,256]{2,1,0:T(8,128)(2,1)} %get-tuple-element.51), channel_id=1, source_target_pairs={{0,16},{4,8},{8,18},{12,10},{16,20},{20,12},{24,22},{28,14},{1,9},... | collective-permute-start | bytes 1572872 | tf_op jit(solution)/shard_map/ppermute | solution.py:300
  6.5 23.0 %collective-permute-start.3 = (bf16[2,512,256]{2,1,0:T(8,128)(2,1)}, bf16[2,512,256]{2,1,0:T(8,128)(2,1)S(1)}, u32[]{:S(2)}, u32[]{:S(2)}) collective-permute-start(bf16[2,512,256]{2,1,0:T(8,128)(2,1)} %get-tuple-element.55), channel_id=1, source_target_pairs={{0,17},{4,9},{8,19},{12,11},{16,21},{20,13},{24,23},{28,15},{2,10}... | collective-permute-start | bytes 1572872 | tf_op jit(solution)/shard_map/ppermute | solution.py:300
  24.6 8.4 %collective-permute-start.6 = (bf16[2,512,256]{2,1,0:T(8,128)(2,1)S(1)}, bf16[2,512,256]{2,1,0:T(8,128)(2,1)S(1)}, u32[]{:S(2)}, u32[]{:S(2)}) collective-permute-start(bf16[2,512,256]{2,1,0:T(8,128)(2,1)S(1)} %broadcast_select_fusion), channel_id=1, source_target_pairs={{0,16},{1,17},{4,8},{5,9},{8,18},{9,19},{12,10},{13,11},{16,20},{1... | collective-permute-start | bytes 1572872 | tf_op jit(solution)/shard_map/ppermute | solution.py:308
  29.5 11.0 %collective-permute-start.4 = (bf16[2,512,256]{2,1,0:T(8,128)(2,1)S(1)}, bf16[2,512,256]{2,1,0:T(8,128)(2,1)S(1)}, u32[]{:S(2)}, u32[]{:S(2)}) collective-permute-start(bf16[2,512,256]{2,1,0:T(8,128)(2,1)S(1)} %shard_map.38.here_ref), channel_id=1, source_target_pairs={{0,8},{8,24},{16,0},{24,16},{1,9},{9,25},{17,1},{25,17},{2,10},{10... | collective-permute-start | bytes 1572872 | tf_op jit(solution)/shard_map/ppermute | solution.py:283
  33.0 17.7 %collective-permute-start.7 = (bf16[2,512,256]{2,1,0:T(8,128)(2,1)S(1)}, bf16[2,512,256]{2,1,0:T(8,128)(2,1)S(1)}, u32[]{:S(2)}, u32[]{:S(2)}) collective-permute-start(bf16[2,512,256]{2,1,0:T(8,128)(2,1)S(1)} %collective-permute-done.6.here_ref), channel_id=1, source_target_pairs={{0,8},{8,24},{16,0},{24,16},{1,9},{9,25},{17,1},{25,17},{2,10},{10... | collective-permute-start | bytes 1572872 | tf_op jit(solution)/shard_map/ppermute | solution.py:283
  43.4 14.0 %collective-permute-start.8 = (bf16[4,2,128,256]{3,2,1,0:T(8,128)(2,1)S(1)}, bf16[4,2,128,256]{3,2,1,0:T(8,128)(2,1)S(1)}, u32[]{:S(2)}, u32[]{:S(2)}) collective-permute-start(bf16[4,2,128,256]{3,2,1,0:T(8,128)(2,1)S(1)} %get-tuple-element.66), channel_id=1, source_target_pairs={{0,2},{1,3},{2,0},{3,1},{4,6},{5,7},{6,4},{7,5},{8,10},{9,11},{10,... | collective-permute-start | bytes 1572872 | tf_op jit(solution)/shard_map/ppermute | solution.py:237
  43.5 16.6 %collective-permute-start.5 = (bf16[4,2,128,256]{3,2,1,0:T(8,128)(2,1)S(1)}, bf16[4,2,128,256]{3,2,1,0:T(8,128)(2,1)S(1)}, u32[]{:S(2)}, u32[]{:S(2)}) collective-permute-start(bf16[4,2,128,256]{3,2,1,0:T(8,128)(2,1)S(1)} %get-tuple-element.57), channel_id=1, source_target_pairs={{0,1},{1,0},{2,3},{3,2},{4,5},{5,4},{6,7},{7,6},{8,9},{9,8},{10,11... | collective-permute-start | bytes 1572872 | tf_op jit(solution)/shard_map/ppermute | solution.py:237
  53.7 32.0 %collective-permute-start.13 = (bf16[4,2,128,256]{3,2,1,0:T(8,128)(2,1)S(1)}, bf16[4,2,128,256]{3,2,1,0:T(8,128)(2,1)S(1)}, u32[]{:S(2)}, u32[]{:S(2)}) collective-permute-start(bf16[4,2,128,256]{3,2,1,0:T(8,128)(2,1)S(1)} %get-tuple-element.81), channel_id=1, source_target_pairs={{0,4},{1,5},{2,6},{3,7},{4,0},{5,1},{6,2},{7,3},{8,12},{9,13},{10,... | collective-permute-start | bytes 1572872 | tf_op jit(solution)/shard_map/ppermute | solution.py:237
  57.4 28.2 %collective-permute-start.12 = (bf16[4,2,128,256]{3,2,1,0:T(8,128)(2,1)S(1)}, bf16[4,2,128,256]{3,2,1,0:T(8,128)(2,1)S(1)}, u32[]{:S(2)}, u32[]{:S(2)}) collective-permute-start(bf16[4,2,128,256]{3,2,1,0:T(8,128)(2,1)S(1)} %get-tuple-element.63), channel_id=1, source_target_pairs={{0,1},{1,0},{2,3},{3,2},{4,5},{5,4},{6,7},{7,6},{8,9},{9,8},{10,11... | collective-permute-start | bytes 1572872 | tf_op jit(solution)/shard_map/ppermute | solution.py:237
  60.3 15.7 %collective-permute-start.10 = (bf16[2,2,128,256]{3,2,1,0:T(8,128)(2,1)S(1)}, bf16[2,2,128,256]{3,2,1,0:T(8,128)(2,1)S(1)}, u32[]{:S(2)}, u32[]{:S(2)}) collective-permute-start(bf16[2,2,128,256]{3,2,1,0:T(8,128)(2,1)S(1)} %get-tuple-element.75), channel_id=1, source_target_pairs={{0,1},{1,0},{2,3},{3,2},{4,5},{5,4},{6,7},{7,6},{8,9},{9,8},{10,11... | collective-permute-start | bytes 786440 | tf_op jit(solution)/shard_map/ppermute | solution.py:237
  67.3 18.2 %collective-permute-start.9 = (bf16[2,2,128,256]{3,2,1,0:T(8,128)(2,1)S(1)}, bf16[2,2,128,256]{3,2,1,0:T(8,128)(2,1)S(1)}, u32[]{:S(2)}, u32[]{:S(2)}) collective-permute-start(bf16[2,2,128,256]{3,2,1,0:T(8,128)(2,1)S(1)} %get-tuple-element.69), channel_id=1, source_target_pairs={{0,2},{1,3},{2,0},{3,1},{4,6},{5,7},{6,4},{7,5},{8,10},{9,11},{10,... | collective-permute-start | bytes 786440 | tf_op jit(solution)/shard_map/ppermute | solution.py:237
  85.6 13.8 %collective-permute-start.11 = (bf16[2,2,128,256]{3,2,1,0:T(8,128)(2,1)S(1)}, bf16[2,2,128,256]{3,2,1,0:T(8,128)(2,1)S(1)}, u32[]{:S(2)}, u32[]{:S(2)}) collective-permute-start(bf16[2,2,128,256]{3,2,1,0:T(8,128)(2,1)S(1)} %get-tuple-element.78), channel_id=1, source_target_pairs={{0,4},{1,5},{2,6},{3,7},{4,0},{5,1},{6,2},{7,3},{8,12},{9,13},{10,... | collective-permute-start | bytes 786440 | tf_op jit(solution)/shard_map/ppermute | solution.py:237
  85.9 13.6 %collective-permute-start.14 = (bf16[2,2,128,256]{3,2,1,0:T(8,128)(2,1)S(1)}, bf16[2,2,128,256]{3,2,1,0:T(8,128)(2,1)S(1)}, u32[]{:S(2)}, u32[]{:S(2)}) collective-permute-start(bf16[2,2,128,256]{3,2,1,0:T(8,128)(2,1)S(1)} %get-tuple-element.83), channel_id=1, source_target_pairs={{0,2},{1,3},{2,0},{3,1},{4,6},{5,7},{6,4},{7,5},{8,10},{9,11},{10,... | collective-permute-start | bytes 786440 | tf_op jit(solution)/shard_map/ppermute | solution.py:237
  86.0 13.5 %collective-permute-start.15 = (bf16[2,2,128,256]{3,2,1,0:T(8,128)(2,1)S(1)}, bf16[2,2,128,256]{3,2,1,0:T(8,128)(2,1)S(1)}, u32[]{:S(2)}, u32[]{:S(2)}) collective-permute-start(bf16[2,2,128,256]{3,2,1,0:T(8,128)(2,1)S(1)} %get-tuple-element.86), channel_id=1, source_target_pairs={{0,1},{1,0},{2,3},{3,2},{4,5},{5,4},{6,7},{7,6},{8,9},{9,8},{10,11... | collective-permute-start | bytes 786440 | tf_op jit(solution)/shard_map/ppermute | solution.py:237
  99.6 7.0 %collective-permute-start.16 = (bf16[1,2,128,256]{3,2,1,0:T(8,128)(2,1)S(1)}, bf16[1,2,128,256]{3,2,1,0:T(8,128)(2,1)S(1)}, u32[]{:S(2)}, u32[]{:S(2)}) collective-permute-start(bf16[1,2,128,256]{3,2,1,0:T(8,128)(2,1)S(1)} %get-tuple-element.89), channel_id=1, source_target_pairs={{0,4},{1,5},{2,6},{3,7},{4,0},{5,1},{6,2},{7,3},{8,12},{9,13},{10,... | collective-permute-start | bytes 393224 | tf_op jit(solution)/shard_map/ppermute | solution.py:237
  99.7 6.9 %collective-permute-start.17 = (bf16[1,2,128,256]{3,2,1,0:T(8,128)(2,1)S(1)}, bf16[1,2,128,256]{3,2,1,0:T(8,128)(2,1)S(1)}, u32[]{:S(2)}, u32[]{:S(2)}) collective-permute-start(bf16[1,2,128,256]{3,2,1,0:T(8,128)(2,1)S(1)} %get-tuple-element.91), channel_id=1, source_target_pairs={{0,2},{1,3},{2,0},{3,1},{4,6},{5,7},{6,4},{7,5},{8,10},{9,11},{10,... | collective-permute-start | bytes 393224 | tf_op jit(solution)/shard_map/ppermute | solution.py:237
  99.8 8.8 %collective-permute-start.18 = (bf16[2,128,256]{2,1,0:T(8,128)(2,1)S(1)}, bf16[2,128,256]{2,1,0:T(8,128)(2,1)S(1)}, u32[]{:S(2)}, u32[]{:S(2)}) collective-permute-start(bf16[2,128,256]{2,1,0:T(8,128)(2,1)S(1)} %get-tuple-element.93), channel_id=1, source_target_pairs={{0,8},{8,0},{16,24},{24,16},{1,9},{9,1},{17,25},{25,17},{2,10},{10... | collective-permute-start | bytes 393224 | tf_op jit(solution)/shard_map/ppermute | solution.py:326
  106.7 2.9 %collective-permute-start.19 = (bf16[2,128,256]{2,1,0:T(8,128)(2,1)S(1)}, bf16[2,128,256]{2,1,0:T(8,128)(2,1)S(1)}, u32[]{:S(2)}, u32[]{:S(2)}) collective-permute-start(bf16[2,128,256]{2,1,0:T(8,128)(2,1)S(1)} %get-tuple-element.94), channel_id=1, source_target_pairs={{0,8},{8,0},{16,24},{24,16},{1,9},{9,1},{17,25},{25,17},{2,10},{10... | collective-permute-start | bytes 393224 | tf_op jit(solution)/shard_map/ppermute | solution.py:338

commit v7 on v4

--- a/solution.py
+++ b/solution.py
@@ -8,9 +8,8 @@
 from jax.sharding import PartitionSpec as P
 
 WAVES = 2
-VMEM_BYTES = 48 * 1024 * 1024
+VMEM_BYTES = 20 * 1024 * 1024
 VMEM = pl.BlockSpec(memory_space=pltpu.VMEM)
-SMEM = pl.BlockSpec(memory_space=pltpu.SMEM)
 PARAMS = pltpu.CompilerParams(vmem_limit_bytes=VMEM_BYTES)
 
 
@@ -22,20 +21,22 @@
     return list(range(count.bit_length() - 1))
 
 
-def layout_kernel(x_count, raw_ref, occupancy_ref, exponent_ref, *refs):
+def column_factors(occupancy, exponent):
+    power = jnp.left_shift(1, exponent + 2).astype(jnp.float32) * 0.25
+    return (occupancy.astype(jnp.float32) * power).astype(jnp.bfloat16)
+
+
+def layout_kernel(x_count, raw_ref, factors_ref, *refs):
     piece_refs, left_ref, factor_ref = refs[:-2], refs[-2], refs[-1]
-    tiles = []
+    _, share, width = piece_refs[0].shape
     for tile in range(x_count):
-        row = occupancy_ref[tile : tile + 1, :].astype(jnp.float32)
-        power = jnp.exp2(jnp.full(row.shape, exponent_ref[0, tile], jnp.int32).astype(jnp.float32))
-        tiles.append((row * power).astype(jnp.bfloat16))
-        factor_ref[tile] = tiles[tile].astype(jnp.float32)
-    _, share, width = piece_refs[0].shape
-    for index, out_ref in enumerate(piece_refs):
-        wave, tile = divmod(index, x_count)
-        columns = slice(wave * width, (wave + 1) * width)
-        for part in range(2):
-            out_ref[part] = raw_ref[part, tile * share : (tile + 1) * share, columns] * tiles[tile][:, columns]
+        factor = factors_ref[tile : tile + 1, :]
+        factor_ref[tile] = factor.astype(jnp.float32)
+        for wave in range(WAVES):
+            columns = slice(wave * width, (wave + 1) * width)
+            for part in range(2):
+                value = raw_ref[part, tile * share : (tile + 1) * share, columns]
+                piece_refs[wave * x_count + tile][part] = value * factor[:, columns]
     col, col_count = lax.axis_index("col"), lax.axis_size("col")
     depth = raw_ref.shape[2]
     rows = raw_ref.shape[1] // col_count
@@ -48,7 +49,7 @@
             left_ref[distance * rows : (distance + 1) * rows, part * depth : (part + 1) * depth] = value
 
 
-def lay_out(raw_blocks, occupancy, exponent, x_count):
+def lay_out(raw_blocks, factors, x_count):
     _, length, depth = raw_blocks.shape
     piece = jax.ShapeDtypeStruct((2, length // x_count, depth // WAVES), jnp.bfloat16)
     left = jax.ShapeDtypeStruct((length, 2 * depth), jnp.bfloat16)
@@ -56,12 +57,33 @@
     out = pl.pallas_call(
         functools.partial(layout_kernel, x_count),
         out_shape=[piece] * count + [left],
-        in_specs=[VMEM, VMEM, SMEM],
+        in_specs=[VMEM] * 2,
         out_specs=[VMEM] * (count + 1),
         scratch_shapes=[pltpu.VMEM((x_count, 1, depth), jnp.float32)],
         compiler_params=PARAMS,
-    )(raw_blocks, occupancy, exponent.T)
+    )(raw_blocks, factors)
     return out[:count], out[count]
+
+
+def pick_kernel(period, *refs):
+    options, out_ref = refs[:-1], refs[-1]
+    place = lax.axis_index("col") % period
+    place = jnp.where(place < len(options), place, 0)
+    for index, option_ref in enumerate(options):
+
+        @pl.when(place == index)
+        def _(option_ref=option_ref):
+            out_ref[...] = option_ref[...]
+
+
+def pick(options, period):
+    return pl.pallas_call(
+        functools.partial(pick_kernel, period),
+        out_shape=jax.ShapeDtypeStruct(options[0].shape, options[0].dtype),
+        in_specs=[VMEM] * len(options),
+        out_specs=VMEM,
+        compiler_params=PARAMS,
+    )(*options)
 
 
 def halves(blocks, bit):
@@ -254,19 +276,14 @@
         return [exchange(send, order[step]) for send, order in zip(sends, orders[wave])]
 
     def on_device(raw_blocks, occupancy, exponent):
-        my_col = lax.axis_index("col")
-        x = my_col % x_count
-        pieces, left = lay_out(raw_blocks, occupancy, exponent, x_count)
+        pieces, left = lay_out(raw_blocks, column_factors(occupancy, exponent), x_count)
 
         straight = [lax.ppermute(pieces[h], ("row", "col"), straight_pairs(h)) for h in range(x_count)]
-        second = pieces[x_count]
+        hopped = [pieces[x_count]]
         for h in range(1, x_count):
-            got = lax.ppermute(pieces[x_count + h], ("row", "col"), hop_pairs(h))
-            second = jnp.where(my_col % half_cols == h, got, second)
-        straight = [after(got, second) for got in straight]
-        first = straight[0]
-        for h in range(1, x_count):
-            first = jnp.where(x == h, straight[h], first)
+            hopped.append(lax.ppermute(pieces[x_count + h], ("row", "col"), hop_pairs(h)))
+        second = pick(hopped, half_cols)
+        first = pick([after(got, second) for got in straight], x_count)
         theirs = lax.ppermute(left, "row", swap_core)
 
         second = lax.ppermute(second, ("row", "col"), spread_pairs())

time: 109 us -> 106 us (0.972)
  Pallas kernels: 16.1 us -> 7.19 us
  waiting for transfers between devices: 58.3 us -> 62.6 us
  starting transfers between devices: 30.7 us -> 33.1 us
    ppermute x11, starting transfers between devices: 14.1 us -> 22.3 us  [exchange(): lax.ppermute(value, 'col', [(c, c ^ 1 << bit) for c in range(col_count)])]
    ppermute x2, starting transfers between devices: 10.2 us -> 3.84 us  [to_all_y(): across = lax.ppermute(here, 'row', across_pairs())]
    pallas_call x4, Pallas kernels: 11.6 us -> 5.29 us  [products(): pl.pallas_call(functools.partial(product_kernel, orders, index), out_shap...]
    ppermute x2, waiting for transfers between devices: 1.43 us -> 4.94 us  [to_all_y(): across = lax.ppermute(here, 'row', across_pairs())]
    ppermute x1, waiting for transfers between devices: 16.1 us -> 13.2 us  [on_device(): lax.ppermute(pieces[x_count + h], ('row', 'col'), hop_pairs(h))]
    pallas_call x1, Pallas kernels: 2.87 us -> 0.29 us  [lay_out(): pl.pallas_call(functools.partial(layout_kernel, x_count), out_shape=[piec...]
    ppermute x2, starting transfers between devices: 1.21 us -> 3.7 us  [on_device(): lax.ppermute(pieces[h], ('row', 'col'), straight_pairs(h))]
    ppermute x1, waiting for transfers between devices: 0.01 us -> 2.28 us  [on_device(): second = lax.ppermute(second, ('row', 'col'), spread_pairs())]
  transfers between devices with their start and end apart: 20 -> 20, of which waited for: 9 -> 11; matrix products, arithmetic and copies ran while one was open for 2% -> 0% of each run, Pallas kernels for 11% -> 6%
where the time goes in v7:
time: 106 us
  waiting for transfers between devices  62.6 us (59%)
  starting transfers between devices  33.1 us (31%)
  Pallas kernels  7.19 us (7%)
  local copies, waits for them, and re-layouts  1.59 us (2%)
  other arithmetic  1.42 us (1%)
    ppermute x11, waiting for transfers between devices, exchange(): lax.ppermute(value, 'col', [(c, c ^ 1 << bit) for c in range(col_count)])  35.2 us
    ppermute x11, starting transfers between devices, exchange(): lax.ppermute(value, 'col', [(c, c ^ 1 << bit) for c in range(col_count)])  22.3 us
    ppermute x1, waiting for transfers between devices, on_device(): lax.ppermute(pieces[x_count + h], ('row', 'col'), hop_pairs(h))  13.2 us
    ppermute x2, waiting for transfers between devices, on_device(): lax.ppermute(pieces[h], ('row', 'col'), straight_pairs(h))  5.95 us
    pallas_call x4, Pallas kernels, products(): pl.pallas_call(functools.partial(product_kernel, orders, index), out_shap...  5.29 us
    ppermute x2, waiting for transfers between devices, to_all_y(): across = lax.ppermute(here, 'row', across_pairs())  4.94 us
    ppermute x2, starting transfers between devices, to_all_y(): across = lax.ppermute(here, 'row', across_pairs())  3.84 us
    ppermute x2, starting transfers between devices, on_device(): lax.ppermute(pieces[h], ('row', 'col'), straight_pairs(h))  3.7 us
  transfers between devices with their start and end apart: 20, of which 11 were waited for; matrix products, arithmetic and copies ran while one was open for 0% of the time, Pallas kernels for 6%

profile of v7, /device:TPU:7, one launch (start us, length us, event | category | flops | bytes accessed | tf_op | source)
XLA Modules:
  0.0 106.1 jit_solution(16544359786725975561)
XLA Ops:
  1.4 1.6 %copy-done = bf16[2,1024,512]{2,1,0:T(8,128)(2,1)S(1)} copy-done((bf16[2,1024,512]{2,1,0:T(8,128)(2,1)S(1)}, bf16[2,1024,512]{2,1,0:T(8,128)(2,1)}, u32[]{:S(2)}) %copy-start) | copy-done | bytes 2097176
  4.7 3.4 %collective-permute-start.3 = (bf16[2,512,256]{2,1,0:T(8,128)(2,1)S(1)}, bf16[2,512,256]{2,1,0:T(8,128)(2,1)S(1)}, u32[]{:S(2)}, u32[]{:S(2)}) collective-permute-start(bf16[2,512,256]{2,1,0:T(8,128)(2,1)S(1)} %get-tuple-element.55), channel_id=1, source_target_pairs={{0,17},{4,9},{8,19},{12,11},{16,21},{20,13},{24,23},{28,15},{2,10}... | collective-permute-start | bytes 1572872 | tf_op jit(solution)/shard_map/ppermute | solution.py:281
  8.0 13.2 %collective-permute-done.2.refs_1_ = bf16[2,512,256]{2,1,0:T(8,128)(2,1)S(1)} collective-permute-done((bf16[2,512,256]{2,1,0:T(8,128)(2,1)S(1)}, bf16[2,512,256]{2,1,0:T(8,128)(2,1)S(1)}, u32[]{:S(2)}, u32[]{:S(2)}) %collective-permute-start.2) | collective-permute-done | bytes 524320 | tf_op jit(solution)/shard_map/ppermute | solution.py:284
  21.3 6.0 %collective-permute-done.3.refs_1_ = bf16[2,512,256]{2,1,0:T(8,128)(2,1)S(1)} collective-permute-done((bf16[2,512,256]{2,1,0:T(8,128)(2,1)S(1)}, bf16[2,512,256]{2,1,0:T(8,128)(2,1)S(1)}, u32[]{:S(2)}, u32[]{:S(2)}) %collective-permute-start.3) | collective-permute-done | bytes 524320 | tf_op jit(solution)/shard_map/ppermute | solution.py:281
  27.4 2.3 %collective-permute-done.6.here_ref = bf16[2,512,256]{2,1,0:T(8,128)(2,1)S(1)} collective-permute-done((bf16[2,512,256]{2,1,0:T(8,128)(2,1)S(1)}, bf16[2,512,256]{2,1,0:T(8,128)(2,1)S(1)}, u32[]{:S(2)}, u32[]{:S(2)}) %collective-permute-start.6) | collective-permute-done | bytes 524320 | tf_op jit(solution)/shard_map/ppermute | solution.py:289
  29.6 3.8 %collective-permute-start.7 = (bf16[2,512,256]{2,1,0:T(8,128)(2,1)S(1)}, bf16[2,512,256]{2,1,0:T(8,128)(2,1)S(1)}, u32[]{:S(2)}, u32[]{:S(2)}) collective-permute-start(bf16[2,512,256]{2,1,0:T(8,128)(2,1)S(1)} %collective-permute-done.6.here_ref), channel_id=1, source_target_pairs={{0,8},{8,24},{16,0},{24,16},{1,9},{9,25},{17,1},{25,17},{2,10},{10... | collective-permute-start | bytes 1572872 | tf_op jit(solution)/shard_map/ppermute | solution.py:265
  33.5 4.9 %collective-permute-done.4.across_ref = bf16[2,512,256]{2,1,0:T(8,128)(2,1)S(1)} collective-permute-done((bf16[2,512,256]{2,1,0:T(8,128)(2,1)S(1)}, bf16[2,512,256]{2,1,0:T(8,128)(2,1)S(1)}, u32[]{:S(2)}, u32[]{:S(2)}) %collective-permute-start.4) | collective-permute-done | bytes 524320 | tf_op jit(solution)/shard_map/ppermute | solution.py:265
  38.4 1.3 %shard_map.40 = (bf16[4,2,128,256]{3,2,1,0:T(8,128)(2,1)S(1)}, bf16[4,2,128,256]{3,2,1,0:T(8,128)(2,1)S(1)}) custom-call(bf16[1024,1024]{1,0:T(8,128)(2,1)S(1)} %get-tuple-element.50.mine_ref, bf16[1024,1024]{1,0:T(8,128)(2,1)S(1)} %collective-permute-done.theirs_ref, bf16[2,512,256]{2,1,0:T(8,128)(2,1)S(1)} %shard_map.39.here_ref, ...), custom_call_target="tpu_custom_call" | custom-call | tf_op jit(solution)/shard_map/pallas_call | solution.py:121
  39.8 4.3 %collective-permute-start.5 = (bf16[4,2,128,256]{3,2,1,0:T(8,128)(2,1)S(1)}, bf16[4,2,128,256]{3,2,1,0:T(8,128)(2,1)S(1)}, u32[]{:S(2)}, u32[]{:S(2)}) collective-permute-start(bf16[4,2,128,256]{3,2,1,0:T(8,128)(2,1)S(1)} %get-tuple-element.57), channel_id=1, source_target_pairs={{0,1},{1,0},{2,3},{3,2},{4,5},{5,4},{6,7},{7,6},{8,9},{9,8},{10,11... | collective-permute-start | bytes 1572872 | tf_op jit(solution)/shard_map/ppermute | solution.py:219
  44.1 1.3 %shard_map.41 = (bf16[4,2,128,256]{3,2,1,0:T(8,128)(2,1)S(1)}, bf16[4,2,128,256]{3,2,1,0:T(8,128)(2,1)S(1)}) custom-call(bf16[1024,1024]{1,0:T(8,128)(2,1)S(1)} %get-tuple-element.50.mine_ref, bf16[1024,1024]{1,0:T(8,128)(2,1)S(1)} %collective-permute-done.theirs_ref, bf16[2,512,256]{2,1,0:T(8,128)(2,1)S(1)} %shard_map.39.here_ref, ...), custom_call_target="tpu_custom_call" | custom-call | tf_op jit(solution)/shard_map/pallas_call | solution.py:121
  45.4 1.3 %shard_map.42 = (bf16[4,2,128,256]{3,2,1,0:T(8,128)(2,1)S(1)}, bf16[4,2,128,256]{3,2,1,0:T(8,128)(2,1)S(1)}) custom-call(bf16[1024,1024]{1,0:T(8,128)(2,1)S(1)} %get-tuple-element.50.mine_ref, bf16[1024,1024]{1,0:T(8,128)(2,1)S(1)} %collective-permute-done.theirs_ref, bf16[2,512,256]{2,1,0:T(8,128)(2,1)S(1)} %collective-permute-done.6.here_ref, ...), custom_call_target="tpu_custom_call" | custom-call | tf_op jit(solution)/shard_map/pallas_call | solution.py:121
  46.8 3.7 %collective-permute-start.13 = (bf16[4,2,128,256]{3,2,1,0:T(8,128)(2,1)S(1)}, bf16[4,2,128,256]{3,2,1,0:T(8,128)(2,1)S(1)}, u32[]{:S(2)}, u32[]{:S(2)}) collective-permute-start(bf16[4,2,128,256]{3,2,1,0:T(8,128)(2,1)S(1)} %get-tuple-element.81), channel_id=1, source_target_pairs={{0,4},{1,5},{2,6},{3,7},{4,0},{5,1},{6,2},{7,3},{8,12},{9,13},{10,... | collective-permute-start | bytes 1572872 | tf_op jit(solution)/shard_map/ppermute | solution.py:219
  51.5 2.7 %collective-permute-done.8.refs_3_ = bf16[4,2,128,256]{3,2,1,0:T(8,128)(2,1)S(1)} collective-permute-done((bf16[4,2,128,256]{3,2,1,0:T(8,128)(2,1)S(1)}, bf16[4,2,128,256]{3,2,1,0:T(8,128)(2,1)S(1)}, u32[]{:S(2)}, u32[]{:S(2)}) %collective-permute-start.8) | collective-permute-done | bytes 524320 | tf_op jit(solution)/shard_map/ppermute | solution.py:219
  54.1 2.3 %collective-permute-done.5.refs_1_ = bf16[4,2,128,256]{3,2,1,0:T(8,128)(2,1)S(1)} collective-permute-done((bf16[4,2,128,256]{3,2,1,0:T(8,128)(2,1)S(1)}, bf16[4,2,128,256]{3,2,1,0:T(8,128)(2,1)S(1)}, u32[]{:S(2)}, u32[]{:S(2)}) %collective-permute-start.5) | collective-permute-done | bytes 524320 | tf_op jit(solution)/shard_map/ppermute | solution.py:219
  56.6 7.1 %collective-permute-start.10 = (bf16[2,2,128,256]{3,2,1,0:T(8,128)(2,1)S(1)}, bf16[2,2,128,256]{3,2,1,0:T(8,128)(2,1)S(1)}, u32[]{:S(2)}, u32[]{:S(2)}) collective-permute-start(bf16[2,2,128,256]{3,2,1,0:T(8,128)(2,1)S(1)} %get-tuple-element.75), channel_id=1, source_target_pairs={{0,1},{1,0},{2,3},{3,2},{4,5},{5,4},{6,7},{7,6},{8,9},{9,8},{10,11... | collective-permute-start | bytes 786440 | tf_op jit(solution)/shard_map/ppermute | solution.py:219
  63.7 1.3 %shard_map.44 = (bf16[4,2,128,256]{3,2,1,0:T(8,128)(2,1)S(1)}, bf16[4,2,128,256]{3,2,1,0:T(8,128)(2,1)S(1)}) custom-call(bf16[1024,1024]{1,0:T(8,128)(2,1)S(1)} %get-tuple-element.50.mine_ref, bf16[1024,1024]{1,0:T(8,128)(2,1)S(1)} %collective-permute-done.theirs_ref, bf16[2,512,256]{2,1,0:T(8,128)(2,1)S(1)} %collective-permute-done.6.here_ref, ...), custom_call_target="tpu_custom_call" | custom-call | tf_op jit(solution)/shard_map/pallas_call | solution.py:121
  65.0 8.2 %collective-permute-done.10.refs_3_ = bf16[2,2,128,256]{3,2,1,0:T(8,128)(2,1)S(1)} collective-permute-done((bf16[2,2,128,256]{3,2,1,0:T(8,128)(2,1)S(1)}, bf16[2,2,128,256]{3,2,1,0:T(8,128)(2,1)S(1)}, u32[]{:S(2)}, u32[]{:S(2)}) %collective-permute-start.10) | collective-permute-done | bytes 262176 | tf_op jit(solution)/shard_map/ppermute | solution.py:219
  73.2 6.5 %collective-permute-done.9.refs_1_ = bf16[2,2,128,256]{3,2,1,0:T(8,128)(2,1)S(1)} collective-permute-done((bf16[2,2,128,256]{3,2,1,0:T(8,128)(2,1)S(1)}, bf16[2,2,128,256]{3,2,1,0:T(8,128)(2,1)S(1)}, u32[]{:S(2)}, u32[]{:S(2)}) %collective-permute-start.9) | collective-permute-done | bytes 262176 | tf_op jit(solution)/shard_map/ppermute | solution.py:219
  79.8 1.1 %collective-permute-start.11 = (bf16[2,2,128,256]{3,2,1,0:T(8,128)(2,1)S(1)}, bf16[2,2,128,256]{3,2,1,0:T(8,128)(2,1)S(1)}, u32[]{:S(2)}, u32[]{:S(2)}) collective-permute-start(bf16[2,2,128,256]{3,2,1,0:T(8,128)(2,1)S(1)} %get-tuple-element.78), channel_id=1, source_target_pairs={{0,4},{1,5},{2,6},{3,7},{4,0},{5,1},{6,2},{7,3},{8,12},{9,13},{10,... | collective-permute-start | bytes 786440 | tf_op jit(solution)/shard_map/ppermute | solution.py:219
  81.1 2.3 %collective-permute-start.14 = (bf16[2,2,128,256]{3,2,1,0:T(8,128)(2,1)S(1)}, bf16[2,2,128,256]{3,2,1,0:T(8,128)(2,1)S(1)}, u32[]{:S(2)}, u32[]{:S(2)}) collective-permute-start(bf16[2,2,128,256]{3,2,1,0:T(8,128)(2,1)S(1)} %get-tuple-element.83), channel_id=1, source_target_pairs={{0,2},{1,3},{2,0},{3,1},{4,6},{5,7},{6,4},{7,5},{8,10},{9,11},{10,... | collective-permute-start | bytes 786440 | tf_op jit(solution)/shard_map/ppermute | solution.py:219
  83.4 10.7 %collective-permute-done.11.refs_1_ = bf16[2,2,128,256]{3,2,1,0:T(8,128)(2,1)S(1)} collective-permute-done((bf16[2,2,128,256]{3,2,1,0:T(8,128)(2,1)S(1)}, bf16[2,2,128,256]{3,2,1,0:T(8,128)(2,1)S(1)}, u32[]{:S(2)}, u32[]{:S(2)}) %collective-permute-start.11) | collective-permute-done | bytes 262176 | tf_op jit(solution)/shard_map/ppermute | solution.py:219
  95.1 1.9 %collective-permute-start.17 = (bf16[1,2,128,256]{3,2,1,0:T(8,128)(2,1)S(1)}, bf16[1,2,128,256]{3,2,1,0:T(8,128)(2,1)S(1)}, u32[]{:S(2)}, u32[]{:S(2)}) collective-permute-start(bf16[1,2,128,256]{3,2,1,0:T(8,128)(2,1)S(1)} %get-tuple-element.91), channel_id=1, source_target_pairs={{0,2},{1,3},{2,0},{3,1},{4,6},{5,7},{6,4},{7,5},{8,10},{9,11},{10,... | collective-permute-start | bytes 393224 | tf_op jit(solution)/shard_map/ppermute | solution.py:219
  97.1 1.4 %collective-permute-start.18 = (bf16[2,128,256]{2,1,0:T(8,128)(2,1)S(1)}, bf16[2,128,256]{2,1,0:T(8,128)(2,1)S(1)}, u32[]{:S(2)}, u32[]{:S(2)}) collective-permute-start(bf16[2,128,256]{2,1,0:T(8,128)(2,1)S(1)} %get-tuple-element.93), channel_id=1, source_target_pairs={{0,8},{8,0},{16,24},{24,16},{1,9},{9,1},{17,25},{25,17},{2,10},{10... | collective-permute-start | bytes 393224 | tf_op jit(solution)/shard_map/ppermute | solution.py:307
  98.5 4.9 %collective-permute-done.16.refs_1_ = bf16[1,2,128,256]{3,2,1,0:T(8,128)(2,1)S(1)} collective-permute-done((bf16[1,2,128,256]{3,2,1,0:T(8,128)(2,1)S(1)}, bf16[1,2,128,256]{3,2,1,0:T(8,128)(2,1)S(1)}, u32[]{:S(2)}, u32[]{:S(2)}) %collective-permute-start.16) | collective-permute-done | bytes 131104 | tf_op jit(solution)/shard_map/ppermute | solution.py:219
  (34 shorter events, 8.5 us)
Async XLA Ops:
  1.4 1.6 %copy-start = (bf16[2,1024,512]{2,1,0:T(8,128)(2,1)S(1)}, bf16[2,1024,512]{2,1,0:T(8,128)(2,1)}, u32[]{:S(2)}) copy-start(bf16[2,1024,512]{2,1,0:T(8,128)(2,1)} %raw_ref.1) | copy-start | bytes 6291460
  3.3 35.1 %collective-permute-start = (bf16[1024,1024]{1,0:T(8,128)(2,1)S(1)}, bf16[1024,1024]{1,0:T(8,128)(2,1)S(1)}, u32[]{:S(2)}, u32[]{:S(2)}) collective-permute-start(bf16[1024,1024]{1,0:T(8,128)(2,1)S(1)} %get-tuple-element.50.mine_ref), channel_id=1, source_target_pairs={{0,8},{8,0},{16,24},{24,16},{1,9},{9,1},{17,25},{25,17},{2,10},{10... | collective-permute-start | bytes 6291464 | tf_op jit(solution)/shard_map/ppermute | solution.py:287
  4.0 17.2 %collective-permute-start.2 = (bf16[2,512,256]{2,1,0:T(8,128)(2,1)S(1)}, bf16[2,512,256]{2,1,0:T(8,128)(2,1)S(1)}, u32[]{:S(2)}, u32[]{:S(2)}) collective-permute-start(bf16[2,512,256]{2,1,0:T(8,128)(2,1)S(1)} %get-tuple-element.53), channel_id=1, source_target_pairs={{0,1},{1,0},{2,10},{3,11},{4,5},{5,4},{6,14},{7,15},{8,9},{9,8},{1... | collective-permute-start | bytes 1572872 | tf_op jit(solution)/shard_map/ppermute | solution.py:284
  4.3 17.0 %collective-permute-start.1 = (bf16[2,512,256]{2,1,0:T(8,128)(2,1)S(1)}, bf16[2,512,256]{2,1,0:T(8,128)(2,1)S(1)}, u32[]{:S(2)}, u32[]{:S(2)}) collective-permute-start(bf16[2,512,256]{2,1,0:T(8,128)(2,1)S(1)} %get-tuple-element.51), channel_id=1, source_target_pairs={{0,16},{4,8},{8,18},{12,10},{16,20},{20,12},{24,22},{28,14},{1,9},... | collective-permute-start | bytes 1572872 | tf_op jit(solution)/shard_map/ppermute | solution.py:281
  4.7 22.6 %collective-permute-start.3 = (bf16[2,512,256]{2,1,0:T(8,128)(2,1)S(1)}, bf16[2,512,256]{2,1,0:T(8,128)(2,1)S(1)}, u32[]{:S(2)}, u32[]{:S(2)}) collective-permute-start(bf16[2,512,256]{2,1,0:T(8,128)(2,1)S(1)} %get-tuple-element.55), channel_id=1, source_target_pairs={{0,17},{4,9},{8,19},{12,11},{16,21},{20,13},{24,23},{28,15},{2,10}... | collective-permute-start | bytes 1572872 | tf_op jit(solution)/shard_map/ppermute | solution.py:281
  21.3 8.4 %collective-permute-start.6 = (bf16[2,512,256]{2,1,0:T(8,128)(2,1)S(1)}, bf16[2,512,256]{2,1,0:T(8,128)(2,1)S(1)}, u32[]{:S(2)}, u32[]{:S(2)}) collective-permute-start(bf16[2,512,256]{2,1,0:T(8,128)(2,1)S(1)} %shard_map.38), channel_id=1, source_target_pairs={{0,16},{1,17},{4,8},{5,9},{8,18},{9,19},{12,10},{13,11},{16,20},{1... | collective-permute-start | bytes 1572872 | tf_op jit(solution)/shard_map/ppermute | solution.py:289
  27.3 11.1 %collective-permute-start.4 = (bf16[2,512,256]{2,1,0:T(8,128)(2,1)S(1)}, bf16[2,512,256]{2,1,0:T(8,128)(2,1)S(1)}, u32[]{:S(2)}, u32[]{:S(2)}) collective-permute-start(bf16[2,512,256]{2,1,0:T(8,128)(2,1)S(1)} %shard_map.39.here_ref), channel_id=1, source_target_pairs={{0,8},{8,24},{16,0},{24,16},{1,9},{9,25},{17,1},{25,17},{2,10},{10... | collective-permute-start | bytes 1572872 | tf_op jit(solution)/shard_map/ppermute | solution.py:265
  29.6 15.8 %collective-permute-start.7 = (bf16[2,512,256]{2,1,0:T(8,128)(2,1)S(1)}, bf16[2,512,256]{2,1,0:T(8,128)(2,1)S(1)}, u32[]{:S(2)}, u32[]{:S(2)}) collective-permute-start(bf16[2,512,256]{2,1,0:T(8,128)(2,1)S(1)} %collective-permute-done.6.here_ref), channel_id=1, source_target_pairs={{0,8},{8,24},{16,0},{24,16},{1,9},{9,25},{17,1},{25,17},{2,10},{10... | collective-permute-start | bytes 1572872 | tf_op jit(solution)/shard_map/ppermute | solution.py:265
  39.7 14.4 %collective-permute-start.8 = (bf16[4,2,128,256]{3,2,1,0:T(8,128)(2,1)S(1)}, bf16[4,2,128,256]{3,2,1,0:T(8,128)(2,1)S(1)}, u32[]{:S(2)}, u32[]{:S(2)}) collective-permute-start(bf16[4,2,128,256]{3,2,1,0:T(8,128)(2,1)S(1)} %get-tuple-element.66), channel_id=1, source_target_pairs={{0,2},{1,3},{2,0},{3,1},{4,6},{5,7},{6,4},{7,5},{8,10},{9,11},{10,... | collective-permute-start | bytes 1572872 | tf_op jit(solution)/shard_map/ppermute | solution.py:219
  39.8 16.6 %collective-permute-start.5 = (bf16[4,2,128,256]{3,2,1,0:T(8,128)(2,1)S(1)}, bf16[4,2,128,256]{3,2,1,0:T(8,128)(2,1)S(1)}, u32[]{:S(2)}, u32[]{:S(2)}) collective-permute-start(bf16[4,2,128,256]{3,2,1,0:T(8,128)(2,1)S(1)} %get-tuple-element.57), channel_id=1, source_target_pairs={{0,1},{1,0},{2,3},{3,2},{4,5},{5,4},{6,7},{7,6},{8,9},{9,8},{10,11... | collective-permute-start | bytes 1572872 | tf_op jit(solution)/shard_map/ppermute | solution.py:219
  46.8 34.1 %collective-permute-start.13 = (bf16[4,2,128,256]{3,2,1,0:T(8,128)(2,1)S(1)}, bf16[4,2,128,256]{3,2,1,0:T(8,128)(2,1)S(1)}, u32[]{:S(2)}, u32[]{:S(2)}) collective-permute-start(bf16[4,2,128,256]{3,2,1,0:T(8,128)(2,1)S(1)} %get-tuple-element.81), channel_id=1, source_target_pairs={{0,4},{1,5},{2,6},{3,7},{4,0},{5,1},{6,2},{7,3},{8,12},{9,13},{10,... | collective-permute-start | bytes 1572872 | tf_op jit(solution)/shard_map/ppermute | solution.py:219
  50.5 30.4 %collective-permute-start.12 = (bf16[4,2,128,256]{3,2,1,0:T(8,128)(2,1)S(1)}, bf16[4,2,128,256]{3,2,1,0:T(8,128)(2,1)S(1)}, u32[]{:S(2)}, u32[]{:S(2)}) collective-permute-start(bf16[4,2,128,256]{3,2,1,0:T(8,128)(2,1)S(1)} %get-tuple-element.63), channel_id=1, source_target_pairs={{0,1},{1,0},{2,3},{3,2},{4,5},{5,4},{6,7},{7,6},{8,9},{9,8},{10,11... | collective-permute-start | bytes 1572872 | tf_op jit(solution)/shard_map/ppermute | solution.py:219
  56.6 16.6 %collective-permute-start.10 = (bf16[2,2,128,256]{3,2,1,0:T(8,128)(2,1)S(1)}, bf16[2,2,128,256]{3,2,1,0:T(8,128)(2,1)S(1)}, u32[]{:S(2)}, u32[]{:S(2)}) collective-permute-start(bf16[2,2,128,256]{3,2,1,0:T(8,128)(2,1)S(1)} %get-tuple-element.75), channel_id=1, source_target_pairs={{0,1},{1,0},{2,3},{3,2},{4,5},{5,4},{6,7},{7,6},{8,9},{9,8},{10,11... | collective-permute-start | bytes 786440 | tf_op jit(solution)/shard_map/ppermute | solution.py:219
  63.7 16.0 %collective-permute-start.9 = (bf16[2,2,128,256]{3,2,1,0:T(8,128)(2,1)S(1)}, bf16[2,2,128,256]{3,2,1,0:T(8,128)(2,1)S(1)}, u32[]{:S(2)}, u32[]{:S(2)}) collective-permute-start(bf16[2,2,128,256]{3,2,1,0:T(8,128)(2,1)S(1)} %get-tuple-element.69), channel_id=1, source_target_pairs={{0,2},{1,3},{2,0},{3,1},{4,6},{5,7},{6,4},{7,5},{8,10},{9,11},{10,... | collective-permute-start | bytes 786440 | tf_op jit(solution)/shard_map/ppermute | solution.py:219
  79.8 14.3 %collective-permute-start.11 = (bf16[2,2,128,256]{3,2,1,0:T(8,128)(2,1)S(1)}, bf16[2,2,128,256]{3,2,1,0:T(8,128)(2,1)S(1)}, u32[]{:S(2)}, u32[]{:S(2)}) collective-permute-start(bf16[2,2,128,256]{3,2,1,0:T(8,128)(2,1)S(1)} %get-tuple-element.78), channel_id=1, source_target_pairs={{0,4},{1,5},{2,6},{3,7},{4,0},{5,1},{6,2},{7,3},{8,12},{9,13},{10,... | collective-permute-start | bytes 786440 | tf_op jit(solution)/shard_map/ppermute | solution.py:219
  81.1 13.0 %collective-permute-start.14 = (bf16[2,2,128,256]{3,2,1,0:T(8,128)(2,1)S(1)}, bf16[2,2,128,256]{3,2,1,0:T(8,128)(2,1)S(1)}, u32[]{:S(2)}, u32[]{:S(2)}) collective-permute-start(bf16[2,2,128,256]{3,2,1,0:T(8,128)(2,1)S(1)} %get-tuple-element.83), channel_id=1, source_target_pairs={{0,2},{1,3},{2,0},{3,1},{4,6},{5,7},{6,4},{7,5},{8,10},{9,11},{10,... | collective-permute-start | bytes 786440 | tf_op jit(solution)/shard_map/ppermute | solution.py:219
  83.4 10.8 %collective-permute-start.15 = (bf16[2,2,128,256]{3,2,1,0:T(8,128)(2,1)S(1)}, bf16[2,2,128,256]{3,2,1,0:T(8,128)(2,1)S(1)}, u32[]{:S(2)}, u32[]{:S(2)}) collective-permute-start(bf16[2,2,128,256]{3,2,1,0:T(8,128)(2,1)S(1)} %get-tuple-element.86), channel_id=1, source_target_pairs={{0,1},{1,0},{2,3},{3,2},{4,5},{5,4},{6,7},{7,6},{8,9},{9,8},{10,11... | collective-permute-start | bytes 786440 | tf_op jit(solution)/shard_map/ppermute | solution.py:219
  94.3 9.1 %collective-permute-start.16 = (bf16[1,2,128,256]{3,2,1,0:T(8,128)(2,1)S(1)}, bf16[1,2,128,256]{3,2,1,0:T(8,128)(2,1)S(1)}, u32[]{:S(2)}, u32[]{:S(2)}) collective-permute-start(bf16[1,2,128,256]{3,2,1,0:T(8,128)(2,1)S(1)} %get-tuple-element.89), channel_id=1, source_target_pairs={{0,4},{1,5},{2,6},{3,7},{4,0},{5,1},{6,2},{7,3},{8,12},{9,13},{10,... | collective-permute-start | bytes 393224 | tf_op jit(solution)/shard_map/ppermute | solution.py:219
  95.1 8.2 %collective-permute-start.17 = (bf16[1,2,128,256]{3,2,1,0:T(8,128)(2,1)S(1)}, bf16[1,2,128,256]{3,2,1,0:T(8,128)(2,1)S(1)}, u32[]{:S(2)}, u32[]{:S(2)}) collective-permute-start(bf16[1,2,128,256]{3,2,1,0:T(8,128)(2,1)S(1)} %get-tuple-element.91), channel_id=1, source_target_pairs={{0,2},{1,3},{2,0},{3,1},{4,6},{5,7},{6,4},{7,5},{8,10},{9,11},{10,... | collective-permute-start | bytes 393224 | tf_op jit(solution)/shard_map/ppermute | solution.py:219
  97.1 7.2 %collective-permute-start.18 = (bf16[2,128,256]{2,1,0:T(8,128)(2,1)S(1)}, bf16[2,128,256]{2,1,0:T(8,128)(2,1)S(1)}, u32[]{:S(2)}, u32[]{:S(2)}) collective-permute-start(bf16[2,128,256]{2,1,0:T(8,128)(2,1)S(1)} %get-tuple-element.93), channel_id=1, source_target_pairs={{0,8},{8,0},{16,24},{24,16},{1,9},{9,1},{17,25},{25,17},{2,10},{10... | collective-permute-start | bytes 393224 | tf_op jit(solution)/shard_map/ppermute | solution.py:307
  103.4 1.8 %collective-permute-start.19 = (bf16[2,128,256]{2,1,0:T(8,128)(2,1)S(1)}, bf16[2,128,256]{2,1,0:T(8,128)(2,1)S(1)}, u32[]{:S(2)}, u32[]{:S(2)}) collective-permute-start(bf16[2,128,256]{2,1,0:T(8,128)(2,1)S(1)} %get-tuple-element.94), channel_id=1, source_target_pairs={{0,8},{8,0},{16,24},{24,16},{1,9},{9,1},{17,25},{25,17},{2,10},{10... | collective-permute-start | bytes 393224 | tf_op jit(solution)/shard_map/ppermute | solution.py:319

commit v8 on v7

--- a/solution.py
+++ b/solution.py
@@ -148,12 +148,13 @@
 
 def halve(orders, step, keeps, others):
     blocks, *rest = keeps[0].shape
-    joined = step == len(orders[0]) - 1 and orders[0][step] == orders[1][step]
+    last = step == len(orders[0]) - 1
+    joined = last and orders[0][step] == orders[1][step]
     send = jax.ShapeDtypeStruct((2 if joined else blocks // 2, *rest), jnp.bfloat16)
     keep = jax.ShapeDtypeStruct(send.shape, jnp.float32)
     outs = pl.pallas_call(
         functools.partial(halve_kernel, orders, step, joined),
-        out_shape=[send, keep] if joined else [send, keep] * 2,
+        out_shape=[send, keep] if joined else [send, keep, send, send if last else keep],
         in_specs=[VMEM] * 4,
         out_specs=[VMEM] * (2 if joined else 4),
         compiler_params=PARAMS,
@@ -179,25 +180,25 @@
     )(*[value for pair in zip(keeps, others) for value in pair])
 
 
-def place_kernel(*refs):
-    out_ref = refs[-1]
+def finish_kernel(mine_ref, back_ref, *refs):
+    parts, out_ref = refs[:-1], refs[-1]
     core = lax.axis_index("row") % 2
-    for half, panel in enumerate((core, 1 - core)):
-        begin = 0
-        for ref in refs[half * WAVES : (half + 1) * WAVES]:
-            width = ref.shape[-1]
-            out_ref[panel, :, :, begin : begin + width] = ref[...]
-            begin += width
-
-
-def place(own, back, depth):
+    width = mine_ref.shape[-1]
+    for chain, (panel, ready_ref) in enumerate(((core, mine_ref), (1 - core, back_ref))):
+        out_ref[panel, :, :, :width] = ready_ref[...]
+        total = parts[2 * chain][0].astype(jnp.float32) + parts[2 * chain + 1][0].astype(jnp.float32)
+        out_ref[panel, :, :, width:] = total.astype(out_ref.dtype)
+
+
+def finish(mine, back, *parts):
+    width = mine.shape[-1] + parts[0].shape[-1]
     return pl.pallas_call(
-        place_kernel,
-        out_shape=jax.ShapeDtypeStruct((2, *own[0].shape[:-1], depth), jnp.bfloat16),
-        in_specs=[VMEM] * (2 * WAVES),
+        finish_kernel,
+        out_shape=jax.ShapeDtypeStruct((2, *mine.shape[:-1], width), jnp.bfloat16),
+        in_specs=[VMEM] * (2 + len(parts)),
         out_specs=VMEM,
         compiler_params=PARAMS,
-    )(*own, *back)
+    )(mine, back, *parts)
 
 
 def solution(mesh):
@@ -304,7 +305,7 @@
         for step in range(1, steps):
             if step + 1 == steps - 1:
                 mine, other_rows = add(keeps, others)
-                own, back = [mine], [lax.ppermute(other_rows, "row", swap_core)]
+                back = lax.ppermute(other_rows, "row", swap_core)
                 mark = mine
             elif step + 1 < steps - 1:
                 sends[0], keeps = halve(orders[0], step + 2, keeps, others)
@@ -313,11 +314,13 @@
             if step > 1:
                 later = [after(other, mark) for other in later]
             sends[1], stay = halve(orders[1], step, stay, later)
-            later = exchange_step(1, sends[1], step)
-        mine, other_rows = add(stay, later)
-        own.append(mine)
-        back.append(lax.ppermute(other_rows, "row", swap_core))
-        return place(own, back, raw_blocks.shape[2])
+            if step < steps - 1:
+                later = exchange_step(1, sends[1], step)
+        near = exchange(sends[1][0], orders[1][0][-1])
+        across = [(d, d ^ col_count ^ (1 << orders[1][1][-1])) for d in every]
+        far = lax.ppermute(sends[1][1], ("row", "col"), across)
+        kept = lax.ppermute(stay[1], "row", swap_core)
+        return finish(mine, back, stay[0], near, kept, far)
 
     placed = (P(None, "row", "col"), P("row", "col"), P("row", "col"))
     return jax.shard_map(

time: 106 us -> 106 us (level)
  starting transfers between devices: 33.1 us -> 31.9 us
    ppermute x11 -> x10, starting transfers between devices: 22.3 us -> 19.6 us  [exchange(): lax.ppermute(value, 'col', [(c, c ^ 1 << bit) for c in range(col_count)])]
    ppermute x2 -> x3, starting transfers between devices: 2.19 us -> 3.76 us  [the longest x1 1.63 us: on_device(): far = lax.ppermute(sends[1][1], ('row', 'col'), across)]
    ppermute x11 -> x10, waiting for transfers between devices: 35.2 us -> 36.5 us  [exchange(): lax.ppermute(value, 'col', [(c, c ^ 1 << bit) for c in range(col_count)])]
where the time goes in v8:
time: 106 us
  waiting for transfers between devices  63.4 us (60%)
  starting transfers between devices  31.9 us (30%)
  Pallas kernels  7.16 us (7%)
  local copies, waits for them, and re-layouts  1.59 us (2%)
  other arithmetic  1.42 us (1%)
    ppermute x10, waiting for transfers between devices, exchange(): lax.ppermute(value, 'col', [(c, c ^ 1 << bit) for c in range(col_count)])  36.5 us
    ppermute x10, starting transfers between devices, exchange(): lax.ppermute(value, 'col', [(c, c ^ 1 << bit) for c in range(col_count)])  19.6 us
    ppermute x1, waiting for transfers between devices, on_device(): lax.ppermute(pieces[x_count + h], ('row', 'col'), hop_pairs(h))  13.2 us
    ppermute x2, waiting for transfers between devices, on_device(): lax.ppermute(pieces[h], ('row', 'col'), straight_pairs(h))  5.95 us
    pallas_call x4, Pallas kernels, products(): pl.pallas_call(functools.partial(product_kernel, orders, index), out_shap...  5.29 us
    ppermute x2, waiting for transfers between devices, to_all_y(): across = lax.ppermute(here, 'row', across_pairs())  4.94 us
    ppermute x2, starting transfers between devices, to_all_y(): across = lax.ppermute(here, 'row', across_pairs())  3.84 us
    ppermute x2, starting transfers between devices, on_device(): lax.ppermute(pieces[h], ('row', 'col'), straight_pairs(h))  3.7 us
  transfers between devices with their start and end apart: 20, of which 11 were waited for; matrix products, arithmetic and copies ran while one was open for 0% of the time, Pallas kernels for 6%

profile of v8, /device:TPU:7, one launch (start us, length us, event | category | flops | bytes accessed | tf_op | source)
XLA Modules:
  0.0 105.6 jit_solution(9905104436845709150)
XLA Ops:
  1.4 1.6 %copy-done = bf16[2,1024,512]{2,1,0:T(8,128)(2,1)S(1)} copy-done((bf16[2,1024,512]{2,1,0:T(8,128)(2,1)S(1)}, bf16[2,1024,512]{2,1,0:T(8,128)(2,1)}, u32[]{:S(2)}) %copy-start) | copy-done | bytes 2097176
  4.7 3.4 %collective-permute-start.3 = (bf16[2,512,256]{2,1,0:T(8,128)(2,1)S(1)}, bf16[2,512,256]{2,1,0:T(8,128)(2,1)S(1)}, u32[]{:S(2)}, u32[]{:S(2)}) collective-permute-start(bf16[2,512,256]{2,1,0:T(8,128)(2,1)S(1)} %get-tuple-element.53), channel_id=1, source_target_pairs={{0,17},{4,9},{8,19},{12,11},{16,21},{20,13},{24,23},{28,15},{2,10}... | collective-permute-start | bytes 1572872 | tf_op jit(solution)/shard_map/ppermute | solution.py:282
  8.0 13.2 %collective-permute-done.2.refs_1_ = bf16[2,512,256]{2,1,0:T(8,128)(2,1)S(1)} collective-permute-done((bf16[2,512,256]{2,1,0:T(8,128)(2,1)S(1)}, bf16[2,512,256]{2,1,0:T(8,128)(2,1)S(1)}, u32[]{:S(2)}, u32[]{:S(2)}) %collective-permute-start.2) | collective-permute-done | bytes 524320 | tf_op jit(solution)/shard_map/ppermute | solution.py:285
  21.3 6.0 %collective-permute-done.3.refs_1_ = bf16[2,512,256]{2,1,0:T(8,128)(2,1)S(1)} collective-permute-done((bf16[2,512,256]{2,1,0:T(8,128)(2,1)S(1)}, bf16[2,512,256]{2,1,0:T(8,128)(2,1)S(1)}, u32[]{:S(2)}, u32[]{:S(2)}) %collective-permute-start.3) | collective-permute-done | bytes 524320 | tf_op jit(solution)/shard_map/ppermute | solution.py:282
  27.4 2.3 %collective-permute-done.6.here_ref = bf16[2,512,256]{2,1,0:T(8,128)(2,1)S(1)} collective-permute-done((bf16[2,512,256]{2,1,0:T(8,128)(2,1)S(1)}, bf16[2,512,256]{2,1,0:T(8,128)(2,1)S(1)}, u32[]{:S(2)}, u32[]{:S(2)}) %collective-permute-start.6) | collective-permute-done | bytes 524320 | tf_op jit(solution)/shard_map/ppermute | solution.py:290
  29.6 3.8 %collective-permute-start.7 = (bf16[2,512,256]{2,1,0:T(8,128)(2,1)S(1)}, bf16[2,512,256]{2,1,0:T(8,128)(2,1)S(1)}, u32[]{:S(2)}, u32[]{:S(2)}) collective-permute-start(bf16[2,512,256]{2,1,0:T(8,128)(2,1)S(1)} %collective-permute-done.6.here_ref), channel_id=1, source_target_pairs={{0,8},{8,24},{16,0},{24,16},{1,9},{9,25},{17,1},{25,17},{2,10},{10... | collective-permute-start | bytes 1572872 | tf_op jit(solution)/shard_map/ppermute | solution.py:266
  33.5 4.9 %collective-permute-done.4.across_ref = bf16[2,512,256]{2,1,0:T(8,128)(2,1)S(1)} collective-permute-done((bf16[2,512,256]{2,1,0:T(8,128)(2,1)S(1)}, bf16[2,512,256]{2,1,0:T(8,128)(2,1)S(1)}, u32[]{:S(2)}, u32[]{:S(2)}) %collective-permute-start.4) | collective-permute-done | bytes 524320 | tf_op jit(solution)/shard_map/ppermute | solution.py:266
  38.4 1.3 %shard_map.40 = (bf16[4,2,128,256]{3,2,1,0:T(8,128)(2,1)S(1)}, bf16[4,2,128,256]{3,2,1,0:T(8,128)(2,1)S(1)}) custom-call(bf16[1024,1024]{1,0:T(8,128)(2,1)S(1)} %get-tuple-element.48.mine_ref, bf16[1024,1024]{1,0:T(8,128)(2,1)S(1)} %collective-permute-done.theirs_ref, bf16[2,512,256]{2,1,0:T(8,128)(2,1)S(1)} %shard_map.39.here_ref, ...), custom_call_target="tpu_custom_call" | custom-call | tf_op jit(solution)/shard_map/pallas_call | solution.py:121
  39.8 4.3 %collective-permute-start.5 = (bf16[4,2,128,256]{3,2,1,0:T(8,128)(2,1)S(1)}, bf16[4,2,128,256]{3,2,1,0:T(8,128)(2,1)S(1)}, u32[]{:S(2)}, u32[]{:S(2)}) collective-permute-start(bf16[4,2,128,256]{3,2,1,0:T(8,128)(2,1)S(1)} %get-tuple-element.55), channel_id=1, source_target_pairs={{0,1},{1,0},{2,3},{3,2},{4,5},{5,4},{6,7},{7,6},{8,9},{9,8},{10,11... | collective-permute-start | bytes 1572872 | tf_op jit(solution)/shard_map/ppermute | solution.py:220
  44.1 1.3 %shard_map.41 = (bf16[4,2,128,256]{3,2,1,0:T(8,128)(2,1)S(1)}, bf16[4,2,128,256]{3,2,1,0:T(8,128)(2,1)S(1)}) custom-call(bf16[1024,1024]{1,0:T(8,128)(2,1)S(1)} %get-tuple-element.48.mine_ref, bf16[1024,1024]{1,0:T(8,128)(2,1)S(1)} %collective-permute-done.theirs_ref, bf16[2,512,256]{2,1,0:T(8,128)(2,1)S(1)} %shard_map.39.here_ref, ...), custom_call_target="tpu_custom_call" | custom-call | tf_op jit(solution)/shard_map/pallas_call | solution.py:121
  45.4 1.3 %shard_map.42 = (bf16[4,2,128,256]{3,2,1,0:T(8,128)(2,1)S(1)}, bf16[4,2,128,256]{3,2,1,0:T(8,128)(2,1)S(1)}) custom-call(bf16[1024,1024]{1,0:T(8,128)(2,1)S(1)} %get-tuple-element.48.mine_ref, bf16[1024,1024]{1,0:T(8,128)(2,1)S(1)} %collective-permute-done.theirs_ref, bf16[2,512,256]{2,1,0:T(8,128)(2,1)S(1)} %collective-permute-done.6.here_ref, ...), custom_call_target="tpu_custom_call" | custom-call | tf_op jit(solution)/shard_map/pallas_call | solution.py:121
  46.8 3.7 %collective-permute-start.14 = (bf16[4,2,128,256]{3,2,1,0:T(8,128)(2,1)S(1)}, bf16[4,2,128,256]{3,2,1,0:T(8,128)(2,1)S(1)}, u32[]{:S(2)}, u32[]{:S(2)}) collective-permute-start(bf16[4,2,128,256]{3,2,1,0:T(8,128)(2,1)S(1)} %get-tuple-element.80), channel_id=1, source_target_pairs={{0,4},{1,5},{2,6},{3,7},{4,0},{5,1},{6,2},{7,3},{8,12},{9,13},{10,... | collective-permute-start | bytes 1572872 | tf_op jit(solution)/shard_map/ppermute | solution.py:220
  51.5 2.7 %collective-permute-done.8.refs_3_ = bf16[4,2,128,256]{3,2,1,0:T(8,128)(2,1)S(1)} collective-permute-done((bf16[4,2,128,256]{3,2,1,0:T(8,128)(2,1)S(1)}, bf16[4,2,128,256]{3,2,1,0:T(8,128)(2,1)S(1)}, u32[]{:S(2)}, u32[]{:S(2)}) %collective-permute-start.8) | collective-permute-done | bytes 524320 | tf_op jit(solution)/shard_map/ppermute | solution.py:220
  54.1 2.3 %collective-permute-done.5.refs_1_ = bf16[4,2,128,256]{3,2,1,0:T(8,128)(2,1)S(1)} collective-permute-done((bf16[4,2,128,256]{3,2,1,0:T(8,128)(2,1)S(1)}, bf16[4,2,128,256]{3,2,1,0:T(8,128)(2,1)S(1)}, u32[]{:S(2)}, u32[]{:S(2)}) %collective-permute-start.5) | collective-permute-done | bytes 524320 | tf_op jit(solution)/shard_map/ppermute | solution.py:220
  56.6 7.1 %collective-permute-start.10 = (bf16[2,2,128,256]{3,2,1,0:T(8,128)(2,1)S(1)}, bf16[2,2,128,256]{3,2,1,0:T(8,128)(2,1)S(1)}, u32[]{:S(2)}, u32[]{:S(2)}) collective-permute-start(bf16[2,2,128,256]{3,2,1,0:T(8,128)(2,1)S(1)} %get-tuple-element.73), channel_id=1, source_target_pairs={{0,1},{1,0},{2,3},{3,2},{4,5},{5,4},{6,7},{7,6},{8,9},{9,8},{10,11... | collective-permute-start | bytes 786440 | tf_op jit(solution)/shard_map/ppermute | solution.py:220
  63.7 1.3 %shard_map.44 = (bf16[4,2,128,256]{3,2,1,0:T(8,128)(2,1)S(1)}, bf16[4,2,128,256]{3,2,1,0:T(8,128)(2,1)S(1)}) custom-call(bf16[1024,1024]{1,0:T(8,128)(2,1)S(1)} %get-tuple-element.48.mine_ref, bf16[1024,1024]{1,0:T(8,128)(2,1)S(1)} %collective-permute-done.theirs_ref, bf16[2,512,256]{2,1,0:T(8,128)(2,1)S(1)} %collective-permute-done.6.here_ref, ...), custom_call_target="tpu_custom_call" | custom-call | tf_op jit(solution)/shard_map/pallas_call | solution.py:121
  65.0 8.2 %collective-permute-done.10.refs_3_ = bf16[2,2,128,256]{3,2,1,0:T(8,128)(2,1)S(1)} collective-permute-done((bf16[2,2,128,256]{3,2,1,0:T(8,128)(2,1)S(1)}, bf16[2,2,128,256]{3,2,1,0:T(8,128)(2,1)S(1)}, u32[]{:S(2)}, u32[]{:S(2)}) %collective-permute-start.10) | collective-permute-done | bytes 262176 | tf_op jit(solution)/shard_map/ppermute | solution.py:220
  73.2 6.5 %collective-permute-done.9.refs_1_ = bf16[2,2,128,256]{3,2,1,0:T(8,128)(2,1)S(1)} collective-permute-done((bf16[2,2,128,256]{3,2,1,0:T(8,128)(2,1)S(1)}, bf16[2,2,128,256]{3,2,1,0:T(8,128)(2,1)S(1)}, u32[]{:S(2)}, u32[]{:S(2)}) %collective-permute-start.9) | collective-permute-done | bytes 262176 | tf_op jit(solution)/shard_map/ppermute | solution.py:220
  79.8 1.1 %collective-permute-start.11 = (bf16[2,2,128,256]{3,2,1,0:T(8,128)(2,1)S(1)}, bf16[2,2,128,256]{3,2,1,0:T(8,128)(2,1)S(1)}, u32[]{:S(2)}, u32[]{:S(2)}) collective-permute-start(bf16[2,2,128,256]{3,2,1,0:T(8,128)(2,1)S(1)} %get-tuple-element.76), channel_id=1, source_target_pairs={{0,4},{1,5},{2,6},{3,7},{4,0},{5,1},{6,2},{7,3},{8,12},{9,13},{10,... | collective-permute-start | bytes 786440 | tf_op jit(solution)/shard_map/ppermute | solution.py:220
  81.1 2.3 %collective-permute-start.15 = (bf16[2,2,128,256]{3,2,1,0:T(8,128)(2,1)S(1)}, bf16[2,2,128,256]{3,2,1,0:T(8,128)(2,1)S(1)}, u32[]{:S(2)}, u32[]{:S(2)}) collective-permute-start(bf16[2,2,128,256]{3,2,1,0:T(8,128)(2,1)S(1)} %get-tuple-element.82), channel_id=1, source_target_pairs={{0,2},{1,3},{2,0},{3,1},{4,6},{5,7},{6,4},{7,5},{8,10},{9,11},{10,... | collective-permute-start | bytes 786440 | tf_op jit(solution)/shard_map/ppermute | solution.py:220
  83.4 10.7 %collective-permute-done.11.refs_1_ = bf16[2,2,128,256]{3,2,1,0:T(8,128)(2,1)S(1)} collective-permute-done((bf16[2,2,128,256]{3,2,1,0:T(8,128)(2,1)S(1)}, bf16[2,2,128,256]{3,2,1,0:T(8,128)(2,1)S(1)}, u32[]{:S(2)}, u32[]{:S(2)}) %collective-permute-start.11) | collective-permute-done | bytes 262176 | tf_op jit(solution)/shard_map/ppermute | solution.py:220
  94.1 1.2 %collective-permute-start.12 = (bf16[2,128,256]{2,1,0:T(8,128)(2,1)S(1)}, bf16[2,128,256]{2,1,0:T(8,128)(2,1)S(1)}, u32[]{:S(2)}, u32[]{:S(2)}) collective-permute-start(bf16[2,128,256]{2,1,0:T(8,128)(2,1)S(1)} %get-tuple-element.78), channel_id=1, source_target_pairs={{0,8},{8,0},{16,24},{24,16},{1,9},{9,1},{17,25},{25,17},{2,10},{10... | collective-permute-start | bytes 393224 | tf_op jit(solution)/shard_map/ppermute | solution.py:308
  96.5 1.6 %collective-permute-start.19 = (bf16[1,2,128,256]{3,2,1,0:T(8,128)(2,1)S(1)}, bf16[1,2,128,256]{3,2,1,0:T(8,128)(2,1)S(1)}, u32[]{:S(2)}, u32[]{:S(2)}) collective-permute-start(bf16[1,2,128,256]{3,2,1,0:T(8,128)(2,1)S(1)} %get-tuple-element.90), channel_id=1, source_target_pairs={{0,10},{1,11},{2,8},{3,9},{4,14},{5,15},{6,12},{7,13},{8,2},{9,3},... | collective-permute-start | bytes 393224 | tf_op jit(solution)/shard_map/ppermute | solution.py:321
  98.1 6.2 %collective-permute-done.17.refs_1_ = bf16[1,2,128,256]{3,2,1,0:T(8,128)(2,1)S(1)} collective-permute-done((bf16[1,2,128,256]{3,2,1,0:T(8,128)(2,1)S(1)}, bf16[1,2,128,256]{3,2,1,0:T(8,128)(2,1)S(1)}, u32[]{:S(2)}, u32[]{:S(2)}) %collective-permute-start.17) | collective-permute-done | bytes 131104 | tf_op jit(solution)/shard_map/ppermute | solution.py:220
  (33 shorter events, 7.3 us)
Async XLA Ops:
  1.4 1.6 %copy-start = (bf16[2,1024,512]{2,1,0:T(8,128)(2,1)S(1)}, bf16[2,1024,512]{2,1,0:T(8,128)(2,1)}, u32[]{:S(2)}) copy-start(bf16[2,1024,512]{2,1,0:T(8,128)(2,1)} %raw_ref.1) | copy-start | bytes 6291460
  3.3 35.1 %collective-permute-start = (bf16[1024,1024]{1,0:T(8,128)(2,1)S(1)}, bf16[1024,1024]{1,0:T(8,128)(2,1)S(1)}, u32[]{:S(2)}, u32[]{:S(2)}) collective-permute-start(bf16[1024,1024]{1,0:T(8,128)(2,1)S(1)} %get-tuple-element.48.mine_ref), channel_id=1, source_target_pairs={{0,8},{8,0},{16,24},{24,16},{1,9},{9,1},{17,25},{25,17},{2,10},{10... | collective-permute-start | bytes 6291464 | tf_op jit(solution)/shard_map/ppermute | solution.py:288
  4.0 17.2 %collective-permute-start.2 = (bf16[2,512,256]{2,1,0:T(8,128)(2,1)S(1)}, bf16[2,512,256]{2,1,0:T(8,128)(2,1)S(1)}, u32[]{:S(2)}, u32[]{:S(2)}) collective-permute-start(bf16[2,512,256]{2,1,0:T(8,128)(2,1)S(1)} %get-tuple-element.51), channel_id=1, source_target_pairs={{0,1},{1,0},{2,10},{3,11},{4,5},{5,4},{6,14},{7,15},{8,9},{9,8},{1... | collective-permute-start | bytes 1572872 | tf_op jit(solution)/shard_map/ppermute | solution.py:285
  4.3 17.0 %collective-permute-start.1 = (bf16[2,512,256]{2,1,0:T(8,128)(2,1)S(1)}, bf16[2,512,256]{2,1,0:T(8,128)(2,1)S(1)}, u32[]{:S(2)}, u32[]{:S(2)}) collective-permute-start(bf16[2,512,256]{2,1,0:T(8,128)(2,1)S(1)} %get-tuple-element.49), channel_id=1, source_target_pairs={{0,16},{4,8},{8,18},{12,10},{16,20},{20,12},{24,22},{28,14},{1,9},... | collective-permute-start | bytes 1572872 | tf_op jit(solution)/shard_map/ppermute | solution.py:282
  4.7 22.6 %collective-permute-start.3 = (bf16[2,512,256]{2,1,0:T(8,128)(2,1)S(1)}, bf16[2,512,256]{2,1,0:T(8,128)(2,1)S(1)}, u32[]{:S(2)}, u32[]{:S(2)}) collective-permute-start(bf16[2,512,256]{2,1,0:T(8,128)(2,1)S(1)} %get-tuple-element.53), channel_id=1, source_target_pairs={{0,17},{4,9},{8,19},{12,11},{16,21},{20,13},{24,23},{28,15},{2,10}... | collective-permute-start | bytes 1572872 | tf_op jit(solution)/shard_map/ppermute | solution.py:282
  21.3 8.4 %collective-permute-start.6 = (bf16[2,512,256]{2,1,0:T(8,128)(2,1)S(1)}, bf16[2,512,256]{2,1,0:T(8,128)(2,1)S(1)}, u32[]{:S(2)}, u32[]{:S(2)}) collective-permute-start(bf16[2,512,256]{2,1,0:T(8,128)(2,1)S(1)} %shard_map.38), channel_id=1, source_target_pairs={{0,16},{1,17},{4,8},{5,9},{8,18},{9,19},{12,10},{13,11},{16,20},{1... | collective-permute-start | bytes 1572872 | tf_op jit(solution)/shard_map/ppermute | solution.py:290
  27.3 11.1 %collective-permute-start.4 = (bf16[2,512,256]{2,1,0:T(8,128)(2,1)S(1)}, bf16[2,512,256]{2,1,0:T(8,128)(2,1)S(1)}, u32[]{:S(2)}, u32[]{:S(2)}) collective-permute-start(bf16[2,512,256]{2,1,0:T(8,128)(2,1)S(1)} %shard_map.39.here_ref), channel_id=1, source_target_pairs={{0,8},{8,24},{16,0},{24,16},{1,9},{9,25},{17,1},{25,17},{2,10},{10... | collective-permute-start | bytes 1572872 | tf_op jit(solution)/shard_map/ppermute | solution.py:266
  29.6 15.8 %collective-permute-start.7 = (bf16[2,512,256]{2,1,0:T(8,128)(2,1)S(1)}, bf16[2,512,256]{2,1,0:T(8,128)(2,1)S(1)}, u32[]{:S(2)}, u32[]{:S(2)}) collective-permute-start(bf16[2,512,256]{2,1,0:T(8,128)(2,1)S(1)} %collective-permute-done.6.here_ref), channel_id=1, source_target_pairs={{0,8},{8,24},{16,0},{24,16},{1,9},{9,25},{17,1},{25,17},{2,10},{10... | collective-permute-start | bytes 1572872 | tf_op jit(solution)/shard_map/ppermute | solution.py:266
  39.7 14.4 %collective-permute-start.8 = (bf16[4,2,128,256]{3,2,1,0:T(8,128)(2,1)S(1)}, bf16[4,2,128,256]{3,2,1,0:T(8,128)(2,1)S(1)}, u32[]{:S(2)}, u32[]{:S(2)}) collective-permute-start(bf16[4,2,128,256]{3,2,1,0:T(8,128)(2,1)S(1)} %get-tuple-element.64), channel_id=1, source_target_pairs={{0,2},{1,3},{2,0},{3,1},{4,6},{5,7},{6,4},{7,5},{8,10},{9,11},{10,... | collective-permute-start | bytes 1572872 | tf_op jit(solution)/shard_map/ppermute | solution.py:220
  39.8 16.6 %collective-permute-start.5 = (bf16[4,2,128,256]{3,2,1,0:T(8,128)(2,1)S(1)}, bf16[4,2,128,256]{3,2,1,0:T(8,128)(2,1)S(1)}, u32[]{:S(2)}, u32[]{:S(2)}) collective-permute-start(bf16[4,2,128,256]{3,2,1,0:T(8,128)(2,1)S(1)} %get-tuple-element.55), channel_id=1, source_target_pairs={{0,1},{1,0},{2,3},{3,2},{4,5},{5,4},{6,7},{7,6},{8,9},{9,8},{10,11... | collective-permute-start | bytes 1572872 | tf_op jit(solution)/shard_map/ppermute | solution.py:220
  46.8 34.1 %collective-permute-start.14 = (bf16[4,2,128,256]{3,2,1,0:T(8,128)(2,1)S(1)}, bf16[4,2,128,256]{3,2,1,0:T(8,128)(2,1)S(1)}, u32[]{:S(2)}, u32[]{:S(2)}) collective-permute-start(bf16[4,2,128,256]{3,2,1,0:T(8,128)(2,1)S(1)} %get-tuple-element.80), channel_id=1, source_target_pairs={{0,4},{1,5},{2,6},{3,7},{4,0},{5,1},{6,2},{7,3},{8,12},{9,13},{10,... | collective-permute-start | bytes 1572872 | tf_op jit(solution)/shard_map/ppermute | solution.py:220
  50.5 30.4 %collective-permute-start.13 = (bf16[4,2,128,256]{3,2,1,0:T(8,128)(2,1)S(1)}, bf16[4,2,128,256]{3,2,1,0:T(8,128)(2,1)S(1)}, u32[]{:S(2)}, u32[]{:S(2)}) collective-permute-start(bf16[4,2,128,256]{3,2,1,0:T(8,128)(2,1)S(1)} %get-tuple-element.61), channel_id=1, source_target_pairs={{0,1},{1,0},{2,3},{3,2},{4,5},{5,4},{6,7},{7,6},{8,9},{9,8},{10,11... | collective-permute-start | bytes 1572872 | tf_op jit(solution)/shard_map/ppermute | solution.py:220
  56.6 16.6 %collective-permute-start.10 = (bf16[2,2,128,256]{3,2,1,0:T(8,128)(2,1)S(1)}, bf16[2,2,128,256]{3,2,1,0:T(8,128)(2,1)S(1)}, u32[]{:S(2)}, u32[]{:S(2)}) collective-permute-start(bf16[2,2,128,256]{3,2,1,0:T(8,128)(2,1)S(1)} %get-tuple-element.73), channel_id=1, source_target_pairs={{0,1},{1,0},{2,3},{3,2},{4,5},{5,4},{6,7},{7,6},{8,9},{9,8},{10,11... | collective-permute-start | bytes 786440 | tf_op jit(solution)/shard_map/ppermute | solution.py:220
  63.7 16.0 %collective-permute-start.9 = (bf16[2,2,128,256]{3,2,1,0:T(8,128)(2,1)S(1)}, bf16[2,2,128,256]{3,2,1,0:T(8,128)(2,1)S(1)}, u32[]{:S(2)}, u32[]{:S(2)}) collective-permute-start(bf16[2,2,128,256]{3,2,1,0:T(8,128)(2,1)S(1)} %get-tuple-element.67), channel_id=1, source_target_pairs={{0,2},{1,3},{2,0},{3,1},{4,6},{5,7},{6,4},{7,5},{8,10},{9,11},{10,... | collective-permute-start | bytes 786440 | tf_op jit(solution)/shard_map/ppermute | solution.py:220
  79.8 14.3 %collective-permute-start.11 = (bf16[2,2,128,256]{3,2,1,0:T(8,128)(2,1)S(1)}, bf16[2,2,128,256]{3,2,1,0:T(8,128)(2,1)S(1)}, u32[]{:S(2)}, u32[]{:S(2)}) collective-permute-start(bf16[2,2,128,256]{3,2,1,0:T(8,128)(2,1)S(1)} %get-tuple-element.76), channel_id=1, source_target_pairs={{0,4},{1,5},{2,6},{3,7},{4,0},{5,1},{6,2},{7,3},{8,12},{9,13},{10,... | collective-permute-start | bytes 786440 | tf_op jit(solution)/shard_map/ppermute | solution.py:220
  81.1 14.2 %collective-permute-start.15 = (bf16[2,2,128,256]{3,2,1,0:T(8,128)(2,1)S(1)}, bf16[2,2,128,256]{3,2,1,0:T(8,128)(2,1)S(1)}, u32[]{:S(2)}, u32[]{:S(2)}) collective-permute-start(bf16[2,2,128,256]{3,2,1,0:T(8,128)(2,1)S(1)} %get-tuple-element.82), channel_id=1, source_target_pairs={{0,2},{1,3},{2,0},{3,1},{4,6},{5,7},{6,4},{7,5},{8,10},{9,11},{10,... | collective-permute-start | bytes 786440 | tf_op jit(solution)/shard_map/ppermute | solution.py:220
  83.4 12.0 %collective-permute-start.16 = (bf16[2,2,128,256]{3,2,1,0:T(8,128)(2,1)S(1)}, bf16[2,2,128,256]{3,2,1,0:T(8,128)(2,1)S(1)}, u32[]{:S(2)}, u32[]{:S(2)}) collective-permute-start(bf16[2,2,128,256]{3,2,1,0:T(8,128)(2,1)S(1)} %get-tuple-element.85), channel_id=1, source_target_pairs={{0,1},{1,0},{2,3},{3,2},{4,5},{5,4},{6,7},{7,6},{8,9},{9,8},{10,11... | collective-permute-start | bytes 786440 | tf_op jit(solution)/shard_map/ppermute | solution.py:220
  94.1 3.9 %collective-permute-start.12 = (bf16[2,128,256]{2,1,0:T(8,128)(2,1)S(1)}, bf16[2,128,256]{2,1,0:T(8,128)(2,1)S(1)}, u32[]{:S(2)}, u32[]{:S(2)}) collective-permute-start(bf16[2,128,256]{2,1,0:T(8,128)(2,1)S(1)} %get-tuple-element.78), channel_id=1, source_target_pairs={{0,8},{8,0},{16,24},{24,16},{1,9},{9,1},{17,25},{25,17},{2,10},{10... | collective-permute-start | bytes 393224 | tf_op jit(solution)/shard_map/ppermute | solution.py:308
  95.4 8.8 %collective-permute-start.17 = (bf16[1,2,128,256]{3,2,1,0:T(8,128)(2,1)S(1)}, bf16[1,2,128,256]{3,2,1,0:T(8,128)(2,1)S(1)}, u32[]{:S(2)}, u32[]{:S(2)}) collective-permute-start(bf16[1,2,128,256]{3,2,1,0:T(8,128)(2,1)S(1)} %get-tuple-element.88), channel_id=1, source_target_pairs={{0,4},{1,5},{2,6},{3,7},{4,0},{5,1},{6,2},{7,3},{8,12},{9,13},{10,... | collective-permute-start | bytes 393224 | tf_op jit(solution)/shard_map/ppermute | solution.py:220
  95.5 8.7 %collective-permute-start.18 = (bf16[1,2,128,256]{3,2,1,0:T(8,128)(2,1)S(1)}, bf16[1,2,128,256]{3,2,1,0:T(8,128)(2,1)S(1)}, u32[]{:S(2)}, u32[]{:S(2)}) collective-permute-start(bf16[1,2,128,256]{3,2,1,0:T(8,128)(2,1)S(1)} %get-tuple-element.89), channel_id=1, source_target_pairs={{0,8},{8,0},{16,24},{24,16},{1,9},{9,1},{17,25},{25,17},{2,10},{10... | collective-permute-start | bytes 393224 | tf_op jit(solution)/shard_map/ppermute | solution.py:322
  96.5 8.3 %collective-permute-start.19 = (bf16[1,2,128,256]{3,2,1,0:T(8,128)(2,1)S(1)}, bf16[1,2,128,256]{3,2,1,0:T(8,128)(2,1)S(1)}, u32[]{:S(2)}, u32[]{:S(2)}) collective-permute-start(bf16[1,2,128,256]{3,2,1,0:T(8,128)(2,1)S(1)} %get-tuple-element.90), channel_id=1, source_target_pairs={{0,10},{1,11},{2,8},{3,9},{4,14},{5,15},{6,12},{7,13},{8,2},{9,3},... | collective-permute-start | bytes 393224 | tf_op jit(solution)/shard_map/ppermute | solution.py:321

commit v9 on v8

--- a/solution.py
+++ b/solution.py
@@ -129,7 +129,8 @@
 
 
 def halve_kernel(orders, step, joined, *refs):
-    ins, outs = refs[:4], refs[4:]
+    ins, refs = refs[:4], refs[4:]
+    outs = refs[-2:] if joined else refs[-4:]
     for chain, order in enumerate(orders):
         keep_ref, other_ref = ins[2 * chain : 2 * chain + 2]
         blocks = range(1 << len(order))
@@ -143,22 +144,26 @@
                 if joined:
                     outs[index][chain] = total.astype(outs[index].dtype)
                 else:
-                    outs[2 * chain + index][place] = total.astype(outs[2 * chain + index].dtype)
-
-
-def halve(orders, step, keeps, others):
+                    out_ref = outs[2 * chain + index]
+                    out_ref[out_ref.shape[0] - len(kept) + place] = total.astype(out_ref.dtype)
+    if len(refs) > len(outs):
+        outs[3][0] = refs[0][...]
+
+
+def halve(orders, step, keeps, others, ready=None):
     blocks, *rest = keeps[0].shape
     last = step == len(orders[0]) - 1
     joined = last and orders[0][step] == orders[1][step]
     send = jax.ShapeDtypeStruct((2 if joined else blocks // 2, *rest), jnp.bfloat16)
     keep = jax.ShapeDtypeStruct(send.shape, jnp.float32)
+    moving = jax.ShapeDtypeStruct((2, *rest), jnp.bfloat16)
     outs = pl.pallas_call(
         functools.partial(halve_kernel, orders, step, joined),
-        out_shape=[send, keep] if joined else [send, keep, send, send if last else keep],
-        in_specs=[VMEM] * 4,
+        out_shape=[send, keep] if joined else [send, keep, send, keep if ready is None else moving],
+        in_specs=[VMEM] * (4 if ready is None else 5),
         out_specs=[VMEM] * (2 if joined else 4),
         compiler_params=PARAMS,
-    )(keeps[0], others[0], keeps[1], others[1])
+    )(keeps[0], others[0], keeps[1], others[1], *(() if ready is None else (ready,)))
     return outs[0::2], outs[1::2]
 
 
@@ -180,25 +185,25 @@
     )(*[value for pair in zip(keeps, others) for value in pair])
 
 
-def finish_kernel(mine_ref, back_ref, *refs):
-    parts, out_ref = refs[:-1], refs[-1]
+def finish_kernel(mine_ref, keep_ref, near_ref, moved_ref, far_ref, out_ref):
     core = lax.axis_index("row") % 2
     width = mine_ref.shape[-1]
-    for chain, (panel, ready_ref) in enumerate(((core, mine_ref), (1 - core, back_ref))):
-        out_ref[panel, :, :, :width] = ready_ref[...]
-        total = parts[2 * chain][0].astype(jnp.float32) + parts[2 * chain + 1][0].astype(jnp.float32)
-        out_ref[panel, :, :, width:] = total.astype(out_ref.dtype)
-
-
-def finish(mine, back, *parts):
+    out_ref[core, :, :, :width] = mine_ref[...]
+    out_ref[core, :, :, width:] = (keep_ref[0] + near_ref[0].astype(jnp.float32)).astype(out_ref.dtype)
+    out_ref[1 - core, :, :, :width] = moved_ref[0]
+    total = moved_ref[1].astype(jnp.float32) + far_ref[0].astype(jnp.float32)
+    out_ref[1 - core, :, :, width:] = total.astype(out_ref.dtype)
+
+
+def finish(mine, *parts):
     width = mine.shape[-1] + parts[0].shape[-1]
     return pl.pallas_call(
         finish_kernel,
         out_shape=jax.ShapeDtypeStruct((2, *mine.shape[:-1], width), jnp.bfloat16),
-        in_specs=[VMEM] * (2 + len(parts)),
+        in_specs=[VMEM] * (1 + len(parts)),
         out_specs=VMEM,
         compiler_params=PARAMS,
-    )(mine, back, *parts)
+    )(mine, *parts)
 
 
 def solution(mesh):
@@ -305,7 +310,6 @@
         for step in range(1, steps):
             if step + 1 == steps - 1:
                 mine, other_rows = add(keeps, others)
-                back = lax.ppermute(other_rows, "row", swap_core)
                 mark = mine
             elif step + 1 < steps - 1:
                 sends[0], keeps = halve(orders[0], step + 2, keeps, others)
@@ -313,14 +317,14 @@
                 mark = sends[0][0]
             if step > 1:
                 later = [after(other, mark) for other in later]
-            sends[1], stay = halve(orders[1], step, stay, later)
+            sends[1], stay = halve(orders[1], step, stay, later, other_rows if step == steps - 1 else None)
             if step < steps - 1:
                 later = exchange_step(1, sends[1], step)
         near = exchange(sends[1][0], orders[1][0][-1])
         across = [(d, d ^ col_count ^ (1 << orders[1][1][-1])) for d in every]
         far = lax.ppermute(sends[1][1], ("row", "col"), across)
-        kept = lax.ppermute(stay[1], "row", swap_core)
-        return finish(mine, back, stay[0], near, kept, far)
+        moved = lax.ppermute(stay[1], "row", swap_core)
+        return finish(mine, stay[0], near, moved, far)
 
     placed = (P(None, "row", "col"), P("row", "col"), P("row", "col"))
     return jax.shard_map(

time: 106 us -> 106 us (level)
    ppermute x2 -> x1, starting transfers between devices: 2.13 us -> 1.48 us  [on_device(): moved = lax.ppermute(stay[1], 'row', swap_core)]
  transfers between devices with their start and end apart: 20 -> 19, of which waited for: 11 -> 10; matrix products, arithmetic and copies ran while one was open for 0% -> 0% of each run, Pallas kernels for 6% -> 6%
where the time goes in v9:
time: 106 us; the launch traced here: 105 us
  waiting for transfers between devices  63.1 us (60%)
  starting transfers between devices  32 us (30%)
  Pallas kernels  7.17 us (7%)
  local copies, waits for them, and re-layouts  1.59 us (2%)
  other arithmetic  1.42 us (1%)
    ppermute x10, waiting for transfers between devices, exchange(): lax.ppermute(value, 'col', [(c, c ^ 1 << bit) for c in range(col_count)])  36.7 us
    ppermute x10, starting transfers between devices, exchange(): lax.ppermute(value, 'col', [(c, c ^ 1 << bit) for c in range(col_count)])  19.9 us
    ppermute x1, waiting for transfers between devices, on_device(): lax.ppermute(pieces[x_count + h], ('row', 'col'), hop_pairs(h))  13.2 us
    ppermute x2, waiting for transfers between devices, on_device(): lax.ppermute(pieces[h], ('row', 'col'), straight_pairs(h))  5.95 us
    pallas_call x4, Pallas kernels, products(): pl.pallas_call(functools.partial(product_kernel, orders, index), out_shap...  5.29 us
    ppermute x2, waiting for transfers between devices, to_all_y(): across = lax.ppermute(here, 'row', across_pairs())  4.94 us
    ppermute x2, starting transfers between devices, to_all_y(): across = lax.ppermute(here, 'row', across_pairs())  3.84 us
    ppermute x2, starting transfers between devices, on_device(): lax.ppermute(pieces[h], ('row', 'col'), straight_pairs(h))  3.7 us
  transfers between devices with their start and end apart: 19, of which 10 were waited for; matrix products, arithmetic and copies ran while one was open for 0% of the time, Pallas kernels for 6%

profile of v9, /device:TPU:7, one launch (start us, length us, event | category | flops | bytes accessed | tf_op | source)
XLA Modules:
  0.0 105.4 jit_solution(13530393815867693001)
XLA Ops:
  1.4 1.6 %copy-done = bf16[2,1024,512]{2,1,0:T(8,128)(2,1)S(1)} copy-done((bf16[2,1024,512]{2,1,0:T(8,128)(2,1)S(1)}, bf16[2,1024,512]{2,1,0:T(8,128)(2,1)}, u32[]{:S(2)}) %copy-start) | copy-done | bytes 2097176
  4.7 3.4 %collective-permute-start.3 = (bf16[2,512,256]{2,1,0:T(8,128)(2,1)S(1)}, bf16[2,512,256]{2,1,0:T(8,128)(2,1)S(1)}, u32[]{:S(2)}, u32[]{:S(2)}) collective-permute-start(bf16[2,512,256]{2,1,0:T(8,128)(2,1)S(1)} %get-tuple-element.53), channel_id=1, source_target_pairs={{0,17},{4,9},{8,19},{12,11},{16,21},{20,13},{24,23},{28,15},{2,10}... | collective-permute-start | bytes 1572872 | tf_op jit(solution)/shard_map/ppermute | solution.py:287
  8.0 13.2 %collective-permute-done.2.refs_1_ = bf16[2,512,256]{2,1,0:T(8,128)(2,1)S(1)} collective-permute-done((bf16[2,512,256]{2,1,0:T(8,128)(2,1)S(1)}, bf16[2,512,256]{2,1,0:T(8,128)(2,1)S(1)}, u32[]{:S(2)}, u32[]{:S(2)}) %collective-permute-start.2) | collective-permute-done | bytes 524320 | tf_op jit(solution)/shard_map/ppermute | solution.py:290
  21.3 6.0 %collective-permute-done.3.refs_1_ = bf16[2,512,256]{2,1,0:T(8,128)(2,1)S(1)} collective-permute-done((bf16[2,512,256]{2,1,0:T(8,128)(2,1)S(1)}, bf16[2,512,256]{2,1,0:T(8,128)(2,1)S(1)}, u32[]{:S(2)}, u32[]{:S(2)}) %collective-permute-start.3) | collective-permute-done | bytes 524320 | tf_op jit(solution)/shard_map/ppermute | solution.py:287
  27.4 2.3 %collective-permute-done.6.here_ref = bf16[2,512,256]{2,1,0:T(8,128)(2,1)S(1)} collective-permute-done((bf16[2,512,256]{2,1,0:T(8,128)(2,1)S(1)}, bf16[2,512,256]{2,1,0:T(8,128)(2,1)S(1)}, u32[]{:S(2)}, u32[]{:S(2)}) %collective-permute-start.6) | collective-permute-done | bytes 524320 | tf_op jit(solution)/shard_map/ppermute | solution.py:295
  29.6 3.8 %collective-permute-start.7 = (bf16[2,512,256]{2,1,0:T(8,128)(2,1)S(1)}, bf16[2,512,256]{2,1,0:T(8,128)(2,1)S(1)}, u32[]{:S(2)}, u32[]{:S(2)}) collective-permute-start(bf16[2,512,256]{2,1,0:T(8,128)(2,1)S(1)} %collective-permute-done.6.here_ref), channel_id=1, source_target_pairs={{0,8},{8,24},{16,0},{24,16},{1,9},{9,25},{17,1},{25,17},{2,10},{10... | collective-permute-start | bytes 1572872 | tf_op jit(solution)/shard_map/ppermute | solution.py:271
  33.5 4.9 %collective-permute-done.4.across_ref = bf16[2,512,256]{2,1,0:T(8,128)(2,1)S(1)} collective-permute-done((bf16[2,512,256]{2,1,0:T(8,128)(2,1)S(1)}, bf16[2,512,256]{2,1,0:T(8,128)(2,1)S(1)}, u32[]{:S(2)}, u32[]{:S(2)}) %collective-permute-start.4) | collective-permute-done | bytes 524320 | tf_op jit(solution)/shard_map/ppermute | solution.py:271
  38.4 1.3 %shard_map.40 = (bf16[4,2,128,256]{3,2,1,0:T(8,128)(2,1)S(1)}, bf16[4,2,128,256]{3,2,1,0:T(8,128)(2,1)S(1)}) custom-call(bf16[1024,1024]{1,0:T(8,128)(2,1)S(1)} %get-tuple-element.48.mine_ref, bf16[1024,1024]{1,0:T(8,128)(2,1)S(1)} %collective-permute-done.theirs_ref, bf16[2,512,256]{2,1,0:T(8,128)(2,1)S(1)} %shard_map.39.here_ref, ...), custom_call_target="tpu_custom_call" | custom-call | tf_op jit(solution)/shard_map/pallas_call | solution.py:121
  39.8 4.3 %collective-permute-start.5 = (bf16[4,2,128,256]{3,2,1,0:T(8,128)(2,1)S(1)}, bf16[4,2,128,256]{3,2,1,0:T(8,128)(2,1)S(1)}, u32[]{:S(2)}, u32[]{:S(2)}) collective-permute-start(bf16[4,2,128,256]{3,2,1,0:T(8,128)(2,1)S(1)} %get-tuple-element.55), channel_id=1, source_target_pairs={{0,1},{1,0},{2,3},{3,2},{4,5},{5,4},{6,7},{7,6},{8,9},{9,8},{10,11... | collective-permute-start | bytes 1572872 | tf_op jit(solution)/shard_map/ppermute | solution.py:225
  44.1 1.3 %shard_map.41 = (bf16[4,2,128,256]{3,2,1,0:T(8,128)(2,1)S(1)}, bf16[4,2,128,256]{3,2,1,0:T(8,128)(2,1)S(1)}) custom-call(bf16[1024,1024]{1,0:T(8,128)(2,1)S(1)} %get-tuple-element.48.mine_ref, bf16[1024,1024]{1,0:T(8,128)(2,1)S(1)} %collective-permute-done.theirs_ref, bf16[2,512,256]{2,1,0:T(8,128)(2,1)S(1)} %shard_map.39.here_ref, ...), custom_call_target="tpu_custom_call" | custom-call | tf_op jit(solution)/shard_map/pallas_call | solution.py:121
  45.4 1.3 %shard_map.42 = (bf16[4,2,128,256]{3,2,1,0:T(8,128)(2,1)S(1)}, bf16[4,2,128,256]{3,2,1,0:T(8,128)(2,1)S(1)}) custom-call(bf16[1024,1024]{1,0:T(8,128)(2,1)S(1)} %get-tuple-element.48.mine_ref, bf16[1024,1024]{1,0:T(8,128)(2,1)S(1)} %collective-permute-done.theirs_ref, bf16[2,512,256]{2,1,0:T(8,128)(2,1)S(1)} %collective-permute-done.6.here_ref, ...), custom_call_target="tpu_custom_call" | custom-call | tf_op jit(solution)/shard_map/pallas_call | solution.py:121
  46.8 3.7 %collective-permute-start.13 = (bf16[4,2,128,256]{3,2,1,0:T(8,128)(2,1)S(1)}, bf16[4,2,128,256]{3,2,1,0:T(8,128)(2,1)S(1)}, u32[]{:S(2)}, u32[]{:S(2)}) collective-permute-start(bf16[4,2,128,256]{3,2,1,0:T(8,128)(2,1)S(1)} %get-tuple-element.79), channel_id=1, source_target_pairs={{0,4},{1,5},{2,6},{3,7},{4,0},{5,1},{6,2},{7,3},{8,12},{9,13},{10,... | collective-permute-start | bytes 1572872 | tf_op jit(solution)/shard_map/ppermute | solution.py:225
  51.5 2.7 %collective-permute-done.8.refs_3_ = bf16[4,2,128,256]{3,2,1,0:T(8,128)(2,1)S(1)} collective-permute-done((bf16[4,2,128,256]{3,2,1,0:T(8,128)(2,1)S(1)}, bf16[4,2,128,256]{3,2,1,0:T(8,128)(2,1)S(1)}, u32[]{:S(2)}, u32[]{:S(2)}) %collective-permute-start.8) | collective-permute-done | bytes 524320 | tf_op jit(solution)/shard_map/ppermute | solution.py:225
  54.1 2.3 %collective-permute-done.5.refs_1_ = bf16[4,2,128,256]{3,2,1,0:T(8,128)(2,1)S(1)} collective-permute-done((bf16[4,2,128,256]{3,2,1,0:T(8,128)(2,1)S(1)}, bf16[4,2,128,256]{3,2,1,0:T(8,128)(2,1)S(1)}, u32[]{:S(2)}, u32[]{:S(2)}) %collective-permute-start.5) | collective-permute-done | bytes 524320 | tf_op jit(solution)/shard_map/ppermute | solution.py:225
  56.6 7.1 %collective-permute-start.10 = (bf16[2,2,128,256]{3,2,1,0:T(8,128)(2,1)S(1)}, bf16[2,2,128,256]{3,2,1,0:T(8,128)(2,1)S(1)}, u32[]{:S(2)}, u32[]{:S(2)}) collective-permute-start(bf16[2,2,128,256]{3,2,1,0:T(8,128)(2,1)S(1)} %get-tuple-element.73), channel_id=1, source_target_pairs={{0,1},{1,0},{2,3},{3,2},{4,5},{5,4},{6,7},{7,6},{8,9},{9,8},{10,11... | collective-permute-start | bytes 786440 | tf_op jit(solution)/shard_map/ppermute | solution.py:225
  63.7 1.3 %shard_map.44 = (bf16[4,2,128,256]{3,2,1,0:T(8,128)(2,1)S(1)}, bf16[4,2,128,256]{3,2,1,0:T(8,128)(2,1)S(1)}) custom-call(bf16[1024,1024]{1,0:T(8,128)(2,1)S(1)} %get-tuple-element.48.mine_ref, bf16[1024,1024]{1,0:T(8,128)(2,1)S(1)} %collective-permute-done.theirs_ref, bf16[2,512,256]{2,1,0:T(8,128)(2,1)S(1)} %collective-permute-done.6.here_ref, ...), custom_call_target="tpu_custom_call" | custom-call | tf_op jit(solution)/shard_map/pallas_call | solution.py:121
  65.0 8.2 %collective-permute-done.10.refs_3_ = bf16[2,2,128,256]{3,2,1,0:T(8,128)(2,1)S(1)} collective-permute-done((bf16[2,2,128,256]{3,2,1,0:T(8,128)(2,1)S(1)}, bf16[2,2,128,256]{3,2,1,0:T(8,128)(2,1)S(1)}, u32[]{:S(2)}, u32[]{:S(2)}) %collective-permute-start.10) | collective-permute-done | bytes 262176 | tf_op jit(solution)/shard_map/ppermute | solution.py:225
  73.2 6.5 %collective-permute-done.9.refs_1_ = bf16[2,2,128,256]{3,2,1,0:T(8,128)(2,1)S(1)} collective-permute-done((bf16[2,2,128,256]{3,2,1,0:T(8,128)(2,1)S(1)}, bf16[2,2,128,256]{3,2,1,0:T(8,128)(2,1)S(1)}, u32[]{:S(2)}, u32[]{:S(2)}) %collective-permute-start.9) | collective-permute-done | bytes 262176 | tf_op jit(solution)/shard_map/ppermute | solution.py:225
  79.8 1.1 %collective-permute-start.11 = (bf16[2,2,128,256]{3,2,1,0:T(8,128)(2,1)S(1)}, bf16[2,2,128,256]{3,2,1,0:T(8,128)(2,1)S(1)}, u32[]{:S(2)}, u32[]{:S(2)}) collective-permute-start(bf16[2,2,128,256]{3,2,1,0:T(8,128)(2,1)S(1)} %get-tuple-element.76), channel_id=1, source_target_pairs={{0,4},{1,5},{2,6},{3,7},{4,0},{5,1},{6,2},{7,3},{8,12},{9,13},{10,... | collective-permute-start | bytes 786440 | tf_op jit(solution)/shard_map/ppermute | solution.py:225
  81.1 2.3 %collective-permute-start.14 = (bf16[2,2,128,256]{3,2,1,0:T(8,128)(2,1)S(1)}, bf16[2,2,128,256]{3,2,1,0:T(8,128)(2,1)S(1)}, u32[]{:S(2)}, u32[]{:S(2)}) collective-permute-start(bf16[2,2,128,256]{3,2,1,0:T(8,128)(2,1)S(1)} %get-tuple-element.81), channel_id=1, source_target_pairs={{0,2},{1,3},{2,0},{3,1},{4,6},{5,7},{6,4},{7,5},{8,10},{9,11},{10,... | collective-permute-start | bytes 786440 | tf_op jit(solution)/shard_map/ppermute | solution.py:225
  83.4 10.7 %collective-permute-done.11.refs_1_ = bf16[2,2,128,256]{3,2,1,0:T(8,128)(2,1)S(1)} collective-permute-done((bf16[2,2,128,256]{3,2,1,0:T(8,128)(2,1)S(1)}, bf16[2,2,128,256]{3,2,1,0:T(8,128)(2,1)S(1)}, u32[]{:S(2)}, u32[]{:S(2)}) %collective-permute-start.11) | collective-permute-done | bytes 262176 | tf_op jit(solution)/shard_map/ppermute | solution.py:225
  94.3 1.5 %collective-permute-start.17 = (bf16[2,2,128,256]{3,2,1,0:T(8,128)(2,1)S(1)}, bf16[2,2,128,256]{3,2,1,0:T(8,128)(2,1)S(1)}, u32[]{:S(2)}, u32[]{:S(2)}) collective-permute-start(bf16[2,2,128,256]{3,2,1,0:T(8,128)(2,1)S(1)} %get-tuple-element.89), channel_id=1, source_target_pairs={{0,8},{8,0},{16,24},{24,16},{1,9},{9,1},{17,25},{25,17},{2,10},{10... | collective-permute-start | bytes 786440 | tf_op jit(solution)/shard_map/ppermute | solution.py:326
  96.2 2.0 %collective-permute-start.18 = (bf16[1,2,128,256]{3,2,1,0:T(8,128)(2,1)S(1)}, bf16[1,2,128,256]{3,2,1,0:T(8,128)(2,1)S(1)}, u32[]{:S(2)}, u32[]{:S(2)}) collective-permute-start(bf16[1,2,128,256]{3,2,1,0:T(8,128)(2,1)S(1)} %get-tuple-element.90), channel_id=1, source_target_pairs={{0,10},{1,11},{2,8},{3,9},{4,14},{5,15},{6,12},{7,13},{8,2},{9,3},... | collective-permute-start | bytes 393224 | tf_op jit(solution)/shard_map/ppermute | solution.py:325
  98.2 6.3 %collective-permute-done.16.near_ref = bf16[1,2,128,256]{3,2,1,0:T(8,128)(2,1)S(1)} collective-permute-done((bf16[1,2,128,256]{3,2,1,0:T(8,128)(2,1)S(1)}, bf16[1,2,128,256]{3,2,1,0:T(8,128)(2,1)S(1)}, u32[]{:S(2)}, u32[]{:S(2)}) %collective-permute-start.16) | collective-permute-done | bytes 131104 | tf_op jit(solution)/shard_map/ppermute | solution.py:225
  (31 shorter events, 6.3 us)
Async XLA Ops:
  1.4 1.6 %copy-start = (bf16[2,1024,512]{2,1,0:T(8,128)(2,1)S(1)}, bf16[2,1024,512]{2,1,0:T(8,128)(2,1)}, u32[]{:S(2)}) copy-start(bf16[2,1024,512]{2,1,0:T(8,128)(2,1)} %raw_ref.1) | copy-start | bytes 6291460
  3.3 35.1 %collective-permute-start = (bf16[1024,1024]{1,0:T(8,128)(2,1)S(1)}, bf16[1024,1024]{1,0:T(8,128)(2,1)S(1)}, u32[]{:S(2)}, u32[]{:S(2)}) collective-permute-start(bf16[1024,1024]{1,0:T(8,128)(2,1)S(1)} %get-tuple-element.48.mine_ref), channel_id=1, source_target_pairs={{0,8},{8,0},{16,24},{24,16},{1,9},{9,1},{17,25},{25,17},{2,10},{10... | collective-permute-start | bytes 6291464 | tf_op jit(solution)/shard_map/ppermute | solution.py:293
  4.0 17.2 %collective-permute-start.2 = (bf16[2,512,256]{2,1,0:T(8,128)(2,1)S(1)}, bf16[2,512,256]{2,1,0:T(8,128)(2,1)S(1)}, u32[]{:S(2)}, u32[]{:S(2)}) collective-permute-start(bf16[2,512,256]{2,1,0:T(8,128)(2,1)S(1)} %get-tuple-element.51), channel_id=1, source_target_pairs={{0,1},{1,0},{2,10},{3,11},{4,5},{5,4},{6,14},{7,15},{8,9},{9,8},{1... | collective-permute-start | bytes 1572872 | tf_op jit(solution)/shard_map/ppermute | solution.py:290
  4.3 17.0 %collective-permute-start.1 = (bf16[2,512,256]{2,1,0:T(8,128)(2,1)S(1)}, bf16[2,512,256]{2,1,0:T(8,128)(2,1)S(1)}, u32[]{:S(2)}, u32[]{:S(2)}) collective-permute-start(bf16[2,512,256]{2,1,0:T(8,128)(2,1)S(1)} %get-tuple-element.49), channel_id=1, source_target_pairs={{0,16},{4,8},{8,18},{12,10},{16,20},{20,12},{24,22},{28,14},{1,9},... | collective-permute-start | bytes 1572872 | tf_op jit(solution)/shard_map/ppermute | solution.py:287
  4.7 22.6 %collective-permute-start.3 = (bf16[2,512,256]{2,1,0:T(8,128)(2,1)S(1)}, bf16[2,512,256]{2,1,0:T(8,128)(2,1)S(1)}, u32[]{:S(2)}, u32[]{:S(2)}) collective-permute-start(bf16[2,512,256]{2,1,0:T(8,128)(2,1)S(1)} %get-tuple-element.53), channel_id=1, source_target_pairs={{0,17},{4,9},{8,19},{12,11},{16,21},{20,13},{24,23},{28,15},{2,10}... | collective-permute-start | bytes 1572872 | tf_op jit(solution)/shard_map/ppermute | solution.py:287
  21.3 8.4 %collective-permute-start.6 = (bf16[2,512,256]{2,1,0:T(8,128)(2,1)S(1)}, bf16[2,512,256]{2,1,0:T(8,128)(2,1)S(1)}, u32[]{:S(2)}, u32[]{:S(2)}) collective-permute-start(bf16[2,512,256]{2,1,0:T(8,128)(2,1)S(1)} %shard_map.38), channel_id=1, source_target_pairs={{0,16},{1,17},{4,8},{5,9},{8,18},{9,19},{12,10},{13,11},{16,20},{1... | collective-permute-start | bytes 1572872 | tf_op jit(solution)/shard_map/ppermute | solution.py:295
  27.3 11.1 %collective-permute-start.4 = (bf16[2,512,256]{2,1,0:T(8,128)(2,1)S(1)}, bf16[2,512,256]{2,1,0:T(8,128)(2,1)S(1)}, u32[]{:S(2)}, u32[]{:S(2)}) collective-permute-start(bf16[2,512,256]{2,1,0:T(8,128)(2,1)S(1)} %shard_map.39.here_ref), channel_id=1, source_target_pairs={{0,8},{8,24},{16,0},{24,16},{1,9},{9,25},{17,1},{25,17},{2,10},{10... | collective-permute-start | bytes 1572872 | tf_op jit(solution)/shard_map/ppermute | solution.py:271
  29.6 15.8 %collective-permute-start.7 = (bf16[2,512,256]{2,1,0:T(8,128)(2,1)S(1)}, bf16[2,512,256]{2,1,0:T(8,128)(2,1)S(1)}, u32[]{:S(2)}, u32[]{:S(2)}) collective-permute-start(bf16[2,512,256]{2,1,0:T(8,128)(2,1)S(1)} %collective-permute-done.6.here_ref), channel_id=1, source_target_pairs={{0,8},{8,24},{16,0},{24,16},{1,9},{9,25},{17,1},{25,17},{2,10},{10... | collective-permute-start | bytes 1572872 | tf_op jit(solution)/shard_map/ppermute | solution.py:271
  39.7 14.4 %collective-permute-start.8 = (bf16[4,2,128,256]{3,2,1,0:T(8,128)(2,1)S(1)}, bf16[4,2,128,256]{3,2,1,0:T(8,128)(2,1)S(1)}, u32[]{:S(2)}, u32[]{:S(2)}) collective-permute-start(bf16[4,2,128,256]{3,2,1,0:T(8,128)(2,1)S(1)} %get-tuple-element.64), channel_id=1, source_target_pairs={{0,2},{1,3},{2,0},{3,1},{4,6},{5,7},{6,4},{7,5},{8,10},{9,11},{10,... | collective-permute-start | bytes 1572872 | tf_op jit(solution)/shard_map/ppermute | solution.py:225
  39.8 16.6 %collective-permute-start.5 = (bf16[4,2,128,256]{3,2,1,0:T(8,128)(2,1)S(1)}, bf16[4,2,128,256]{3,2,1,0:T(8,128)(2,1)S(1)}, u32[]{:S(2)}, u32[]{:S(2)}) collective-permute-start(bf16[4,2,128,256]{3,2,1,0:T(8,128)(2,1)S(1)} %get-tuple-element.55), channel_id=1, source_target_pairs={{0,1},{1,0},{2,3},{3,2},{4,5},{5,4},{6,7},{7,6},{8,9},{9,8},{10,11... | collective-permute-start | bytes 1572872 | tf_op jit(solution)/shard_map/ppermute | solution.py:225
  46.8 34.1 %collective-permute-start.13 = (bf16[4,2,128,256]{3,2,1,0:T(8,128)(2,1)S(1)}, bf16[4,2,128,256]{3,2,1,0:T(8,128)(2,1)S(1)}, u32[]{:S(2)}, u32[]{:S(2)}) collective-permute-start(bf16[4,2,128,256]{3,2,1,0:T(8,128)(2,1)S(1)} %get-tuple-element.79), channel_id=1, source_target_pairs={{0,4},{1,5},{2,6},{3,7},{4,0},{5,1},{6,2},{7,3},{8,12},{9,13},{10,... | collective-permute-start | bytes 1572872 | tf_op jit(solution)/shard_map/ppermute | solution.py:225
  50.5 30.4 %collective-permute-start.12 = (bf16[4,2,128,256]{3,2,1,0:T(8,128)(2,1)S(1)}, bf16[4,2,128,256]{3,2,1,0:T(8,128)(2,1)S(1)}, u32[]{:S(2)}, u32[]{:S(2)}) collective-permute-start(bf16[4,2,128,256]{3,2,1,0:T(8,128)(2,1)S(1)} %get-tuple-element.61), channel_id=1, source_target_pairs={{0,1},{1,0},{2,3},{3,2},{4,5},{5,4},{6,7},{7,6},{8,9},{9,8},{10,11... | collective-permute-start | bytes 1572872 | tf_op jit(solution)/shard_map/ppermute | solution.py:225
  56.6 16.6 %collective-permute-start.10 = (bf16[2,2,128,256]{3,2,1,0:T(8,128)(2,1)S(1)}, bf16[2,2,128,256]{3,2,1,0:T(8,128)(2,1)S(1)}, u32[]{:S(2)}, u32[]{:S(2)}) collective-permute-start(bf16[2,2,128,256]{3,2,1,0:T(8,128)(2,1)S(1)} %get-tuple-element.73), channel_id=1, source_target_pairs={{0,1},{1,0},{2,3},{3,2},{4,5},{5,4},{6,7},{7,6},{8,9},{9,8},{10,11... | collective-permute-start | bytes 786440 | tf_op jit(solution)/shard_map/ppermute | solution.py:225
  63.7 16.0 %collective-permute-start.9 = (bf16[2,2,128,256]{3,2,1,0:T(8,128)(2,1)S(1)}, bf16[2,2,128,256]{3,2,1,0:T(8,128)(2,1)S(1)}, u32[]{:S(2)}, u32[]{:S(2)}) collective-permute-start(bf16[2,2,128,256]{3,2,1,0:T(8,128)(2,1)S(1)} %get-tuple-element.67), channel_id=1, source_target_pairs={{0,2},{1,3},{2,0},{3,1},{4,6},{5,7},{6,4},{7,5},{8,10},{9,11},{10,... | collective-permute-start | bytes 786440 | tf_op jit(solution)/shard_map/ppermute | solution.py:225
  79.8 14.3 %collective-permute-start.11 = (bf16[2,2,128,256]{3,2,1,0:T(8,128)(2,1)S(1)}, bf16[2,2,128,256]{3,2,1,0:T(8,128)(2,1)S(1)}, u32[]{:S(2)}, u32[]{:S(2)}) collective-permute-start(bf16[2,2,128,256]{3,2,1,0:T(8,128)(2,1)S(1)} %get-tuple-element.76), channel_id=1, source_target_pairs={{0,4},{1,5},{2,6},{3,7},{4,0},{5,1},{6,2},{7,3},{8,12},{9,13},{10,... | collective-permute-start | bytes 786440 | tf_op jit(solution)/shard_map/ppermute | solution.py:225
  81.1 13.0 %collective-permute-start.14 = (bf16[2,2,128,256]{3,2,1,0:T(8,128)(2,1)S(1)}, bf16[2,2,128,256]{3,2,1,0:T(8,128)(2,1)S(1)}, u32[]{:S(2)}, u32[]{:S(2)}) collective-permute-start(bf16[2,2,128,256]{3,2,1,0:T(8,128)(2,1)S(1)} %get-tuple-element.81), channel_id=1, source_target_pairs={{0,2},{1,3},{2,0},{3,1},{4,6},{5,7},{6,4},{7,5},{8,10},{9,11},{10,... | collective-permute-start | bytes 786440 | tf_op jit(solution)/shard_map/ppermute | solution.py:225
  83.4 10.8 %collective-permute-start.15 = (bf16[2,2,128,256]{3,2,1,0:T(8,128)(2,1)S(1)}, bf16[2,2,128,256]{3,2,1,0:T(8,128)(2,1)S(1)}, u32[]{:S(2)}, u32[]{:S(2)}) collective-permute-start(bf16[2,2,128,256]{3,2,1,0:T(8,128)(2,1)S(1)} %get-tuple-element.84), channel_id=1, source_target_pairs={{0,1},{1,0},{2,3},{3,2},{4,5},{5,4},{6,7},{7,6},{8,9},{9,8},{10,11... | collective-permute-start | bytes 786440 | tf_op jit(solution)/shard_map/ppermute | solution.py:225
  94.3 10.3 %collective-permute-start.17 = (bf16[2,2,128,256]{3,2,1,0:T(8,128)(2,1)S(1)}, bf16[2,2,128,256]{3,2,1,0:T(8,128)(2,1)S(1)}, u32[]{:S(2)}, u32[]{:S(2)}) collective-permute-start(bf16[2,2,128,256]{3,2,1,0:T(8,128)(2,1)S(1)} %get-tuple-element.89), channel_id=1, source_target_pairs={{0,8},{8,0},{16,24},{24,16},{1,9},{9,1},{17,25},{25,17},{2,10},{10... | collective-permute-start | bytes 786440 | tf_op jit(solution)/shard_map/ppermute | solution.py:326
  95.8 8.7 %collective-permute-start.16 = (bf16[1,2,128,256]{3,2,1,0:T(8,128)(2,1)S(1)}, bf16[1,2,128,256]{3,2,1,0:T(8,128)(2,1)S(1)}, u32[]{:S(2)}, u32[]{:S(2)}) collective-permute-start(bf16[1,2,128,256]{3,2,1,0:T(8,128)(2,1)S(1)} %get-tuple-element.88), channel_id=1, source_target_pairs={{0,4},{1,5},{2,6},{3,7},{4,0},{5,1},{6,2},{7,3},{8,12},{9,13},{10,... | collective-permute-start | bytes 393224 | tf_op jit(solution)/shard_map/ppermute | solution.py:225
  96.2 8.4 %collective-permute-start.18 = (bf16[1,2,128,256]{3,2,1,0:T(8,128)(2,1)S(1)}, bf16[1,2,128,256]{3,2,1,0:T(8,128)(2,1)S(1)}, u32[]{:S(2)}, u32[]{:S(2)}) collective-permute-start(bf16[1,2,128,256]{3,2,1,0:T(8,128)(2,1)S(1)} %get-tuple-element.90), channel_id=1, source_target_pairs={{0,10},{1,11},{2,8},{3,9},{4,14},{5,15},{6,12},{7,13},{8,2},{9,3},... | collective-permute-start | bytes 393224 | tf_op jit(solution)/shard_map/ppermute | solution.py:325

commit v10 on v9

--- a/solution.py
+++ b/solution.py
@@ -22,8 +22,8 @@
 
 
 def column_factors(occupancy, exponent):
-    power = jnp.left_shift(1, exponent + 2).astype(jnp.float32) * 0.25
-    return (occupancy.astype(jnp.float32) * power).astype(jnp.bfloat16)
+    places = jnp.maximum(jnp.broadcast_to(exponent, occupancy.shape) + 2 * occupancy, 0)
+    return (jnp.left_shift(occupancy, places).astype(jnp.float32) * 0.25).astype(jnp.bfloat16)
 
 
 def layout_kernel(x_count, raw_ref, factors_ref, *refs):

time: 106 us -> 105 us (level)
  no operation moved by 1% of the time
where the time goes in v10:
time: 105 us
  waiting for transfers between devices  63.1 us (60%)
  starting transfers between devices  32 us (30%)
  Pallas kernels  7.17 us (7%)
  local copies, waits for them, and re-layouts  1.59 us (2%)
    ppermute x10, waiting for transfers between devices, exchange(): lax.ppermute(value, 'col', [(c, c ^ 1 << bit) for c in range(col_count)])  36.7 us
    ppermute x10, starting transfers between devices, exchange(): lax.ppermute(value, 'col', [(c, c ^ 1 << bit) for c in range(col_count)])  19.9 us
    ppermute x1, waiting for transfers between devices, on_device(): lax.ppermute(pieces[x_count + h], ('row', 'col'), hop_pairs(h))  13.2 us
    ppermute x2, waiting for transfers between devices, on_device(): lax.ppermute(pieces[h], ('row', 'col'), straight_pairs(h))  5.95 us
    pallas_call x4, Pallas kernels, products(): pl.pallas_call(functools.partial(product_kernel, orders, index), out_shap...  5.29 us
    ppermute x2, waiting for transfers between devices, to_all_y(): across = lax.ppermute(here, 'row', across_pairs())  4.94 us
    ppermute x2, starting transfers between devices, to_all_y(): across = lax.ppermute(here, 'row', across_pairs())  3.84 us
    ppermute x2, starting transfers between devices, on_device(): lax.ppermute(pieces[h], ('row', 'col'), straight_pairs(h))  3.7 us
  transfers between devices with their start and end apart: 19, of which 10 were waited for; matrix products, arithmetic and copies ran while one was open for 0% of the time, Pallas kernels for 6%

profile of v10, /device:TPU:7, one launch (start us, length us, event | category | flops | bytes accessed | tf_op | source)
XLA Modules:
  0.0 104.8 jit_solution(5485167649995695727)
XLA Ops:
  0.8 1.6 %copy-done = bf16[2,1024,512]{2,1,0:T(8,128)(2,1)S(1)} copy-done((bf16[2,1024,512]{2,1,0:T(8,128)(2,1)S(1)}, bf16[2,1024,512]{2,1,0:T(8,128)(2,1)}, u32[]{:S(2)}) %copy-start) | copy-done | bytes 2097176
  4.0 3.4 %collective-permute-start.3 = (bf16[2,512,256]{2,1,0:T(8,128)(2,1)S(1)}, bf16[2,512,256]{2,1,0:T(8,128)(2,1)S(1)}, u32[]{:S(2)}, u32[]{:S(2)}) collective-permute-start(bf16[2,512,256]{2,1,0:T(8,128)(2,1)S(1)} %get-tuple-element.53), channel_id=1, source_target_pairs={{0,17},{4,9},{8,19},{12,11},{16,21},{20,13},{24,23},{28,15},{2,10}... | collective-permute-start | bytes 1572872 | tf_op jit(solution)/shard_map/ppermute | solution.py:287
  7.4 13.2 %collective-permute-done.2.refs_1_ = bf16[2,512,256]{2,1,0:T(8,128)(2,1)S(1)} collective-permute-done((bf16[2,512,256]{2,1,0:T(8,128)(2,1)S(1)}, bf16[2,512,256]{2,1,0:T(8,128)(2,1)S(1)}, u32[]{:S(2)}, u32[]{:S(2)}) %collective-permute-start.2) | collective-permute-done | bytes 524320 | tf_op jit(solution)/shard_map/ppermute | solution.py:290
  20.7 6.0 %collective-permute-done.3.refs_1_ = bf16[2,512,256]{2,1,0:T(8,128)(2,1)S(1)} collective-permute-done((bf16[2,512,256]{2,1,0:T(8,128)(2,1)S(1)}, bf16[2,512,256]{2,1,0:T(8,128)(2,1)S(1)}, u32[]{:S(2)}, u32[]{:S(2)}) %collective-permute-start.3) | collective-permute-done | bytes 524320 | tf_op jit(solution)/shard_map/ppermute | solution.py:287
  26.7 2.3 %collective-permute-done.6.here_ref = bf16[2,512,256]{2,1,0:T(8,128)(2,1)S(1)} collective-permute-done((bf16[2,512,256]{2,1,0:T(8,128)(2,1)S(1)}, bf16[2,512,256]{2,1,0:T(8,128)(2,1)S(1)}, u32[]{:S(2)}, u32[]{:S(2)}) %collective-permute-start.6) | collective-permute-done | bytes 524320 | tf_op jit(solution)/shard_map/ppermute | solution.py:295
  29.0 3.8 %collective-permute-start.7 = (bf16[2,512,256]{2,1,0:T(8,128)(2,1)S(1)}, bf16[2,512,256]{2,1,0:T(8,128)(2,1)S(1)}, u32[]{:S(2)}, u32[]{:S(2)}) collective-permute-start(bf16[2,512,256]{2,1,0:T(8,128)(2,1)S(1)} %collective-permute-done.6.here_ref), channel_id=1, source_target_pairs={{0,8},{8,24},{16,0},{24,16},{1,9},{9,25},{17,1},{25,17},{2,10},{10... | collective-permute-start | bytes 1572872 | tf_op jit(solution)/shard_map/ppermute | solution.py:271
  32.8 4.9 %collective-permute-done.4.across_ref = bf16[2,512,256]{2,1,0:T(8,128)(2,1)S(1)} collective-permute-done((bf16[2,512,256]{2,1,0:T(8,128)(2,1)S(1)}, bf16[2,512,256]{2,1,0:T(8,128)(2,1)S(1)}, u32[]{:S(2)}, u32[]{:S(2)}) %collective-permute-start.4) | collective-permute-done | bytes 524320 | tf_op jit(solution)/shard_map/ppermute | solution.py:271
  37.7 1.3 %shard_map.40 = (bf16[4,2,128,256]{3,2,1,0:T(8,128)(2,1)S(1)}, bf16[4,2,128,256]{3,2,1,0:T(8,128)(2,1)S(1)}) custom-call(bf16[1024,1024]{1,0:T(8,128)(2,1)S(1)} %get-tuple-element.48.mine_ref, bf16[1024,1024]{1,0:T(8,128)(2,1)S(1)} %collective-permute-done.theirs_ref, bf16[2,512,256]{2,1,0:T(8,128)(2,1)S(1)} %shard_map.39.here_ref, ...), custom_call_target="tpu_custom_call" | custom-call | tf_op jit(solution)/shard_map/pallas_call | solution.py:121
  39.2 4.3 %collective-permute-start.5 = (bf16[4,2,128,256]{3,2,1,0:T(8,128)(2,1)S(1)}, bf16[4,2,128,256]{3,2,1,0:T(8,128)(2,1)S(1)}, u32[]{:S(2)}, u32[]{:S(2)}) collective-permute-start(bf16[4,2,128,256]{3,2,1,0:T(8,128)(2,1)S(1)} %get-tuple-element.55), channel_id=1, source_target_pairs={{0,1},{1,0},{2,3},{3,2},{4,5},{5,4},{6,7},{7,6},{8,9},{9,8},{10,11... | collective-permute-start | bytes 1572872 | tf_op jit(solution)/shard_map/ppermute | solution.py:225
  43.4 1.3 %shard_map.41 = (bf16[4,2,128,256]{3,2,1,0:T(8,128)(2,1)S(1)}, bf16[4,2,128,256]{3,2,1,0:T(8,128)(2,1)S(1)}) custom-call(bf16[1024,1024]{1,0:T(8,128)(2,1)S(1)} %get-tuple-element.48.mine_ref, bf16[1024,1024]{1,0:T(8,128)(2,1)S(1)} %collective-permute-done.theirs_ref, bf16[2,512,256]{2,1,0:T(8,128)(2,1)S(1)} %shard_map.39.here_ref, ...), custom_call_target="tpu_custom_call" | custom-call | tf_op jit(solution)/shard_map/pallas_call | solution.py:121
  44.8 1.3 %shard_map.42 = (bf16[4,2,128,256]{3,2,1,0:T(8,128)(2,1)S(1)}, bf16[4,2,128,256]{3,2,1,0:T(8,128)(2,1)S(1)}) custom-call(bf16[1024,1024]{1,0:T(8,128)(2,1)S(1)} %get-tuple-element.48.mine_ref, bf16[1024,1024]{1,0:T(8,128)(2,1)S(1)} %collective-permute-done.theirs_ref, bf16[2,512,256]{2,1,0:T(8,128)(2,1)S(1)} %collective-permute-done.6.here_ref, ...), custom_call_target="tpu_custom_call" | custom-call | tf_op jit(solution)/shard_map/pallas_call | solution.py:121
  46.1 3.7 %collective-permute-start.13 = (bf16[4,2,128,256]{3,2,1,0:T(8,128)(2,1)S(1)}, bf16[4,2,128,256]{3,2,1,0:T(8,128)(2,1)S(1)}, u32[]{:S(2)}, u32[]{:S(2)}) collective-permute-start(bf16[4,2,128,256]{3,2,1,0:T(8,128)(2,1)S(1)} %get-tuple-element.79), channel_id=1, source_target_pairs={{0,4},{1,5},{2,6},{3,7},{4,0},{5,1},{6,2},{7,3},{8,12},{9,13},{10,... | collective-permute-start | bytes 1572872 | tf_op jit(solution)/shard_map/ppermute | solution.py:225
  50.8 2.7 %collective-permute-done.8.refs_3_ = bf16[4,2,128,256]{3,2,1,0:T(8,128)(2,1)S(1)} collective-permute-done((bf16[4,2,128,256]{3,2,1,0:T(8,128)(2,1)S(1)}, bf16[4,2,128,256]{3,2,1,0:T(8,128)(2,1)S(1)}, u32[]{:S(2)}, u32[]{:S(2)}) %collective-permute-start.8) | collective-permute-done | bytes 524320 | tf_op jit(solution)/shard_map/ppermute | solution.py:225
  53.5 2.3 %collective-permute-done.5.refs_1_ = bf16[4,2,128,256]{3,2,1,0:T(8,128)(2,1)S(1)} collective-permute-done((bf16[4,2,128,256]{3,2,1,0:T(8,128)(2,1)S(1)}, bf16[4,2,128,256]{3,2,1,0:T(8,128)(2,1)S(1)}, u32[]{:S(2)}, u32[]{:S(2)}) %collective-permute-start.5) | collective-permute-done | bytes 524320 | tf_op jit(solution)/shard_map/ppermute | solution.py:225
  55.9 7.1 %collective-permute-start.10 = (bf16[2,2,128,256]{3,2,1,0:T(8,128)(2,1)S(1)}, bf16[2,2,128,256]{3,2,1,0:T(8,128)(2,1)S(1)}, u32[]{:S(2)}, u32[]{:S(2)}) collective-permute-start(bf16[2,2,128,256]{3,2,1,0:T(8,128)(2,1)S(1)} %get-tuple-element.73), channel_id=1, source_target_pairs={{0,1},{1,0},{2,3},{3,2},{4,5},{5,4},{6,7},{7,6},{8,9},{9,8},{10,11... | collective-permute-start | bytes 786440 | tf_op jit(solution)/shard_map/ppermute | solution.py:225
  63.1 1.3 %shard_map.44 = (bf16[4,2,128,256]{3,2,1,0:T(8,128)(2,1)S(1)}, bf16[4,2,128,256]{3,2,1,0:T(8,128)(2,1)S(1)}) custom-call(bf16[1024,1024]{1,0:T(8,128)(2,1)S(1)} %get-tuple-element.48.mine_ref, bf16[1024,1024]{1,0:T(8,128)(2,1)S(1)} %collective-permute-done.theirs_ref, bf16[2,512,256]{2,1,0:T(8,128)(2,1)S(1)} %collective-permute-done.6.here_ref, ...), custom_call_target="tpu_custom_call" | custom-call | tf_op jit(solution)/shard_map/pallas_call | solution.py:121
  64.4 8.2 %collective-permute-done.10.refs_3_ = bf16[2,2,128,256]{3,2,1,0:T(8,128)(2,1)S(1)} collective-permute-done((bf16[2,2,128,256]{3,2,1,0:T(8,128)(2,1)S(1)}, bf16[2,2,128,256]{3,2,1,0:T(8,128)(2,1)S(1)}, u32[]{:S(2)}, u32[]{:S(2)}) %collective-permute-start.10) | collective-permute-done | bytes 262176 | tf_op jit(solution)/shard_map/ppermute | solution.py:225
  72.6 6.5 %collective-permute-done.9.refs_1_ = bf16[2,2,128,256]{3,2,1,0:T(8,128)(2,1)S(1)} collective-permute-done((bf16[2,2,128,256]{3,2,1,0:T(8,128)(2,1)S(1)}, bf16[2,2,128,256]{3,2,1,0:T(8,128)(2,1)S(1)}, u32[]{:S(2)}, u32[]{:S(2)}) %collective-permute-start.9) | collective-permute-done | bytes 262176 | tf_op jit(solution)/shard_map/ppermute | solution.py:225
  79.2 1.1 %collective-permute-start.11 = (bf16[2,2,128,256]{3,2,1,0:T(8,128)(2,1)S(1)}, bf16[2,2,128,256]{3,2,1,0:T(8,128)(2,1)S(1)}, u32[]{:S(2)}, u32[]{:S(2)}) collective-permute-start(bf16[2,2,128,256]{3,2,1,0:T(8,128)(2,1)S(1)} %get-tuple-element.76), channel_id=1, source_target_pairs={{0,4},{1,5},{2,6},{3,7},{4,0},{5,1},{6,2},{7,3},{8,12},{9,13},{10,... | collective-permute-start | bytes 786440 | tf_op jit(solution)/shard_map/ppermute | solution.py:225
  80.5 2.3 %collective-permute-start.14 = (bf16[2,2,128,256]{3,2,1,0:T(8,128)(2,1)S(1)}, bf16[2,2,128,256]{3,2,1,0:T(8,128)(2,1)S(1)}, u32[]{:S(2)}, u32[]{:S(2)}) collective-permute-start(bf16[2,2,128,256]{3,2,1,0:T(8,128)(2,1)S(1)} %get-tuple-element.81), channel_id=1, source_target_pairs={{0,2},{1,3},{2,0},{3,1},{4,6},{5,7},{6,4},{7,5},{8,10},{9,11},{10,... | collective-permute-start | bytes 786440 | tf_op jit(solution)/shard_map/ppermute | solution.py:225
  82.7 10.7 %collective-permute-done.11.refs_1_ = bf16[2,2,128,256]{3,2,1,0:T(8,128)(2,1)S(1)} collective-permute-done((bf16[2,2,128,256]{3,2,1,0:T(8,128)(2,1)S(1)}, bf16[2,2,128,256]{3,2,1,0:T(8,128)(2,1)S(1)}, u32[]{:S(2)}, u32[]{:S(2)}) %collective-permute-start.11) | collective-permute-done | bytes 262176 | tf_op jit(solution)/shard_map/ppermute | solution.py:225
  93.6 1.5 %collective-permute-start.17 = (bf16[2,2,128,256]{3,2,1,0:T(8,128)(2,1)S(1)}, bf16[2,2,128,256]{3,2,1,0:T(8,128)(2,1)S(1)}, u32[]{:S(2)}, u32[]{:S(2)}) collective-permute-start(bf16[2,2,128,256]{3,2,1,0:T(8,128)(2,1)S(1)} %get-tuple-element.89), channel_id=1, source_target_pairs={{0,8},{8,0},{16,24},{24,16},{1,9},{9,1},{17,25},{25,17},{2,10},{10... | collective-permute-start | bytes 786440 | tf_op jit(solution)/shard_map/ppermute | solution.py:326
  95.5 2.0 %collective-permute-start.18 = (bf16[1,2,128,256]{3,2,1,0:T(8,128)(2,1)S(1)}, bf16[1,2,128,256]{3,2,1,0:T(8,128)(2,1)S(1)}, u32[]{:S(2)}, u32[]{:S(2)}) collective-permute-start(bf16[1,2,128,256]{3,2,1,0:T(8,128)(2,1)S(1)} %get-tuple-element.90), channel_id=1, source_target_pairs={{0,10},{1,11},{2,8},{3,9},{4,14},{5,15},{6,12},{7,13},{8,2},{9,3},... | collective-permute-start | bytes 393224 | tf_op jit(solution)/shard_map/ppermute | solution.py:325
  97.5 6.3 %collective-permute-done.16.near_ref = bf16[1,2,128,256]{3,2,1,0:T(8,128)(2,1)S(1)} collective-permute-done((bf16[1,2,128,256]{3,2,1,0:T(8,128)(2,1)S(1)}, bf16[1,2,128,256]{3,2,1,0:T(8,128)(2,1)S(1)}, u32[]{:S(2)}, u32[]{:S(2)}) %collective-permute-start.16) | collective-permute-done | bytes 131104 | tf_op jit(solution)/shard_map/ppermute | solution.py:225
  (30 shorter events, 5.6 us)
Async XLA Ops:
  0.8 1.6 %copy-start = (bf16[2,1024,512]{2,1,0:T(8,128)(2,1)S(1)}, bf16[2,1024,512]{2,1,0:T(8,128)(2,1)}, u32[]{:S(2)}) copy-start(bf16[2,1024,512]{2,1,0:T(8,128)(2,1)} %raw_ref.1) | copy-start | bytes 6291460
  2.6 35.1 %collective-permute-start = (bf16[1024,1024]{1,0:T(8,128)(2,1)S(1)}, bf16[1024,1024]{1,0:T(8,128)(2,1)S(1)}, u32[]{:S(2)}, u32[]{:S(2)}) collective-permute-start(bf16[1024,1024]{1,0:T(8,128)(2,1)S(1)} %get-tuple-element.48.mine_ref), channel_id=1, source_target_pairs={{0,8},{8,0},{16,24},{24,16},{1,9},{9,1},{17,25},{25,17},{2,10},{10... | collective-permute-start | bytes 6291464 | tf_op jit(solution)/shard_map/ppermute | solution.py:293
  3.4 17.2 %collective-permute-start.2 = (bf16[2,512,256]{2,1,0:T(8,128)(2,1)S(1)}, bf16[2,512,256]{2,1,0:T(8,128)(2,1)S(1)}, u32[]{:S(2)}, u32[]{:S(2)}) collective-permute-start(bf16[2,512,256]{2,1,0:T(8,128)(2,1)S(1)} %get-tuple-element.51), channel_id=1, source_target_pairs={{0,1},{1,0},{2,10},{3,11},{4,5},{5,4},{6,14},{7,15},{8,9},{9,8},{1... | collective-permute-start | bytes 1572872 | tf_op jit(solution)/shard_map/ppermute | solution.py:290
  3.7 17.0 %collective-permute-start.1 = (bf16[2,512,256]{2,1,0:T(8,128)(2,1)S(1)}, bf16[2,512,256]{2,1,0:T(8,128)(2,1)S(1)}, u32[]{:S(2)}, u32[]{:S(2)}) collective-permute-start(bf16[2,512,256]{2,1,0:T(8,128)(2,1)S(1)} %get-tuple-element.49), channel_id=1, source_target_pairs={{0,16},{4,8},{8,18},{12,10},{16,20},{20,12},{24,22},{28,14},{1,9},... | collective-permute-start | bytes 1572872 | tf_op jit(solution)/shard_map/ppermute | solution.py:287
  4.0 22.6 %collective-permute-start.3 = (bf16[2,512,256]{2,1,0:T(8,128)(2,1)S(1)}, bf16[2,512,256]{2,1,0:T(8,128)(2,1)S(1)}, u32[]{:S(2)}, u32[]{:S(2)}) collective-permute-start(bf16[2,512,256]{2,1,0:T(8,128)(2,1)S(1)} %get-tuple-element.53), channel_id=1, source_target_pairs={{0,17},{4,9},{8,19},{12,11},{16,21},{20,13},{24,23},{28,15},{2,10}... | collective-permute-start | bytes 1572872 | tf_op jit(solution)/shard_map/ppermute | solution.py:287
  20.6 8.4 %collective-permute-start.6 = (bf16[2,512,256]{2,1,0:T(8,128)(2,1)S(1)}, bf16[2,512,256]{2,1,0:T(8,128)(2,1)S(1)}, u32[]{:S(2)}, u32[]{:S(2)}) collective-permute-start(bf16[2,512,256]{2,1,0:T(8,128)(2,1)S(1)} %shard_map.38), channel_id=1, source_target_pairs={{0,16},{1,17},{4,8},{5,9},{8,18},{9,19},{12,10},{13,11},{16,20},{1... | collective-permute-start | bytes 1572872 | tf_op jit(solution)/shard_map/ppermute | solution.py:295
  26.7 11.1 %collective-permute-start.4 = (bf16[2,512,256]{2,1,0:T(8,128)(2,1)S(1)}, bf16[2,512,256]{2,1,0:T(8,128)(2,1)S(1)}, u32[]{:S(2)}, u32[]{:S(2)}) collective-permute-start(bf16[2,512,256]{2,1,0:T(8,128)(2,1)S(1)} %shard_map.39.here_ref), channel_id=1, source_target_pairs={{0,8},{8,24},{16,0},{24,16},{1,9},{9,25},{17,1},{25,17},{2,10},{10... | collective-permute-start | bytes 1572872 | tf_op jit(solution)/shard_map/ppermute | solution.py:271
  29.0 15.8 %collective-permute-start.7 = (bf16[2,512,256]{2,1,0:T(8,128)(2,1)S(1)}, bf16[2,512,256]{2,1,0:T(8,128)(2,1)S(1)}, u32[]{:S(2)}, u32[]{:S(2)}) collective-permute-start(bf16[2,512,256]{2,1,0:T(8,128)(2,1)S(1)} %collective-permute-done.6.here_ref), channel_id=1, source_target_pairs={{0,8},{8,24},{16,0},{24,16},{1,9},{9,25},{17,1},{25,17},{2,10},{10... | collective-permute-start | bytes 1572872 | tf_op jit(solution)/shard_map/ppermute | solution.py:271
  39.1 14.4 %collective-permute-start.8 = (bf16[4,2,128,256]{3,2,1,0:T(8,128)(2,1)S(1)}, bf16[4,2,128,256]{3,2,1,0:T(8,128)(2,1)S(1)}, u32[]{:S(2)}, u32[]{:S(2)}) collective-permute-start(bf16[4,2,128,256]{3,2,1,0:T(8,128)(2,1)S(1)} %get-tuple-element.64), channel_id=1, source_target_pairs={{0,2},{1,3},{2,0},{3,1},{4,6},{5,7},{6,4},{7,5},{8,10},{9,11},{10,... | collective-permute-start | bytes 1572872 | tf_op jit(solution)/shard_map/ppermute | solution.py:225
  39.2 16.6 %collective-permute-start.5 = (bf16[4,2,128,256]{3,2,1,0:T(8,128)(2,1)S(1)}, bf16[4,2,128,256]{3,2,1,0:T(8,128)(2,1)S(1)}, u32[]{:S(2)}, u32[]{:S(2)}) collective-permute-start(bf16[4,2,128,256]{3,2,1,0:T(8,128)(2,1)S(1)} %get-tuple-element.55), channel_id=1, source_target_pairs={{0,1},{1,0},{2,3},{3,2},{4,5},{5,4},{6,7},{7,6},{8,9},{9,8},{10,11... | collective-permute-start | bytes 1572872 | tf_op jit(solution)/shard_map/ppermute | solution.py:225
  46.1 34.1 %collective-permute-start.13 = (bf16[4,2,128,256]{3,2,1,0:T(8,128)(2,1)S(1)}, bf16[4,2,128,256]{3,2,1,0:T(8,128)(2,1)S(1)}, u32[]{:S(2)}, u32[]{:S(2)}) collective-permute-start(bf16[4,2,128,256]{3,2,1,0:T(8,128)(2,1)S(1)} %get-tuple-element.79), channel_id=1, source_target_pairs={{0,4},{1,5},{2,6},{3,7},{4,0},{5,1},{6,2},{7,3},{8,12},{9,13},{10,... | collective-permute-start | bytes 1572872 | tf_op jit(solution)/shard_map/ppermute | solution.py:225
  49.8 30.4 %collective-permute-start.12 = (bf16[4,2,128,256]{3,2,1,0:T(8,128)(2,1)S(1)}, bf16[4,2,128,256]{3,2,1,0:T(8,128)(2,1)S(1)}, u32[]{:S(2)}, u32[]{:S(2)}) collective-permute-start(bf16[4,2,128,256]{3,2,1,0:T(8,128)(2,1)S(1)} %get-tuple-element.61), channel_id=1, source_target_pairs={{0,1},{1,0},{2,3},{3,2},{4,5},{5,4},{6,7},{7,6},{8,9},{9,8},{10,11... | collective-permute-start | bytes 1572872 | tf_op jit(solution)/shard_map/ppermute | solution.py:225
  55.9 16.6 %collective-permute-start.10 = (bf16[2,2,128,256]{3,2,1,0:T(8,128)(2,1)S(1)}, bf16[2,2,128,256]{3,2,1,0:T(8,128)(2,1)S(1)}, u32[]{:S(2)}, u32[]{:S(2)}) collective-permute-start(bf16[2,2,128,256]{3,2,1,0:T(8,128)(2,1)S(1)} %get-tuple-element.73), channel_id=1, source_target_pairs={{0,1},{1,0},{2,3},{3,2},{4,5},{5,4},{6,7},{7,6},{8,9},{9,8},{10,11... | collective-permute-start | bytes 786440 | tf_op jit(solution)/shard_map/ppermute | solution.py:225
  63.1 16.0 %collective-permute-start.9 = (bf16[2,2,128,256]{3,2,1,0:T(8,128)(2,1)S(1)}, bf16[2,2,128,256]{3,2,1,0:T(8,128)(2,1)S(1)}, u32[]{:S(2)}, u32[]{:S(2)}) collective-permute-start(bf16[2,2,128,256]{3,2,1,0:T(8,128)(2,1)S(1)} %get-tuple-element.67), channel_id=1, source_target_pairs={{0,2},{1,3},{2,0},{3,1},{4,6},{5,7},{6,4},{7,5},{8,10},{9,11},{10,... | collective-permute-start | bytes 786440 | tf_op jit(solution)/shard_map/ppermute | solution.py:225
  79.2 14.3 %collective-permute-start.11 = (bf16[2,2,128,256]{3,2,1,0:T(8,128)(2,1)S(1)}, bf16[2,2,128,256]{3,2,1,0:T(8,128)(2,1)S(1)}, u32[]{:S(2)}, u32[]{:S(2)}) collective-permute-start(bf16[2,2,128,256]{3,2,1,0:T(8,128)(2,1)S(1)} %get-tuple-element.76), channel_id=1, source_target_pairs={{0,4},{1,5},{2,6},{3,7},{4,0},{5,1},{6,2},{7,3},{8,12},{9,13},{10,... | collective-permute-start | bytes 786440 | tf_op jit(solution)/shard_map/ppermute | solution.py:225
  80.5 13.0 %collective-permute-start.14 = (bf16[2,2,128,256]{3,2,1,0:T(8,128)(2,1)S(1)}, bf16[2,2,128,256]{3,2,1,0:T(8,128)(2,1)S(1)}, u32[]{:S(2)}, u32[]{:S(2)}) collective-permute-start(bf16[2,2,128,256]{3,2,1,0:T(8,128)(2,1)S(1)} %get-tuple-element.81), channel_id=1, source_target_pairs={{0,2},{1,3},{2,0},{3,1},{4,6},{5,7},{6,4},{7,5},{8,10},{9,11},{10,... | collective-permute-start | bytes 786440 | tf_op jit(solution)/shard_map/ppermute | solution.py:225
  82.7 10.8 %collective-permute-start.15 = (bf16[2,2,128,256]{3,2,1,0:T(8,128)(2,1)S(1)}, bf16[2,2,128,256]{3,2,1,0:T(8,128)(2,1)S(1)}, u32[]{:S(2)}, u32[]{:S(2)}) collective-permute-start(bf16[2,2,128,256]{3,2,1,0:T(8,128)(2,1)S(1)} %get-tuple-element.84), channel_id=1, source_target_pairs={{0,1},{1,0},{2,3},{3,2},{4,5},{5,4},{6,7},{7,6},{8,9},{9,8},{10,11... | collective-permute-start | bytes 786440 | tf_op jit(solution)/shard_map/ppermute | solution.py:225
  93.6 10.3 %collective-permute-start.17 = (bf16[2,2,128,256]{3,2,1,0:T(8,128)(2,1)S(1)}, bf16[2,2,128,256]{3,2,1,0:T(8,128)(2,1)S(1)}, u32[]{:S(2)}, u32[]{:S(2)}) collective-permute-start(bf16[2,2,128,256]{3,2,1,0:T(8,128)(2,1)S(1)} %get-tuple-element.89), channel_id=1, source_target_pairs={{0,8},{8,0},{16,24},{24,16},{1,9},{9,1},{17,25},{25,17},{2,10},{10... | collective-permute-start | bytes 786440 | tf_op jit(solution)/shard_map/ppermute | solution.py:326
  95.1 8.7 %collective-permute-start.16 = (bf16[1,2,128,256]{3,2,1,0:T(8,128)(2,1)S(1)}, bf16[1,2,128,256]{3,2,1,0:T(8,128)(2,1)S(1)}, u32[]{:S(2)}, u32[]{:S(2)}) collective-permute-start(bf16[1,2,128,256]{3,2,1,0:T(8,128)(2,1)S(1)} %get-tuple-element.88), channel_id=1, source_target_pairs={{0,4},{1,5},{2,6},{3,7},{4,0},{5,1},{6,2},{7,3},{8,12},{9,13},{10,... | collective-permute-start | bytes 393224 | tf_op jit(solution)/shard_map/ppermute | solution.py:225
  95.5 8.4 %collective-permute-start.18 = (bf16[1,2,128,256]{3,2,1,0:T(8,128)(2,1)S(1)}, bf16[1,2,128,256]{3,2,1,0:T(8,128)(2,1)S(1)}, u32[]{:S(2)}, u32[]{:S(2)}) collective-permute-start(bf16[1,2,128,256]{3,2,1,0:T(8,128)(2,1)S(1)} %get-tuple-element.90), channel_id=1, source_target_pairs={{0,10},{1,11},{2,8},{3,9},{4,14},{5,15},{6,12},{7,13},{8,2},{9,3},... | collective-permute-start | bytes 393224 | tf_op jit(solution)/shard_map/ppermute | solution.py:325
